TPU v7x, 256 devices: a whole 4x4x8 slice. The times are simulated.
256 devices in a mesh: shard: 16 (over y_lo, z), layer: 16 (over x, y_hi, core).
Axes of the slice: x: 4, y: 4 (y_hi: 2, y_lo: 2; y = y_hi * 2 + y_lo), z: 8, core: 2. Of those that a mesh axis runs over, the one named last changes fastest.
Arguments:
- grad: bfloat16 [16, 4608, 1024], P('layer', None, 'shard'), may hold values from -6 to 6
- momentum: float32 [16, 4608, 1024], P('layer', None, 'shard'), may hold values from -18 to 18
- second: float32 [16, 4608, 1024], P('layer', 'shard'), may hold values from 0.1 to 4
- left_slots: bfloat16 [16, 16, 1152, 1152], P('layer', 'shard'), may hold values from -0.1875 to 0.1875
- right_slots: bfloat16 [16, 16, 1024, 1024], P('layer', 'shard'), may hold values from -0.1875 to 0.1875
- owners: int32 [16, 16], P('layer'), may hold values from 0 to 15, each once within a row
Outputs:
- momentum_out: float32 [16, 4608, 1024], P('layer', None, 'shard')
- second_out: float32 [16, 4608, 1024], P('layer', 'shard')
- direction: bfloat16 [16, 4608, 1024], P('layer', None, 'shard')
Inputs may be any that keep to these rules, and one draw needn't show every extreme that they name: Each row of owners names every slot 0 to 15 once; entries 0 to 4 name the slots of the basis blocks, the rest are unused.
All inputs are finite; a program needn't handle non-finite values.
Results may differ from a plain program's by a relative error of at most 0.0061.
Values may be sent and summed in bfloat16 or wider, within the bound.
No kernel may reach another device: no remote copies, remote signals or barrier semaphores. Data moves between devices by JAX's collectives and lax.ppermute only.
A program may use at most 128 MiB of HBM per device.

v0:
```python
import jax
import jax.numpy as jnp
from jax import lax
from jax.sharding import PartitionSpec as P

BLK = 1152


first_decay = 0.9
second_decay = 0.95
guard_eps = 1e-08
clip_limit = 0.2


def broadcast(block, axis, owner):
    block = jnp.where(lax.axis_index(axis) == owner, block, jnp.zeros_like(block))
    return lax.psum(block, axis)


def body(grad, momentum, second, left_slots, right_slots, owners):
    shards = lax.axis_size("shard")
    rows_all = grad.shape[1]
    col_part = grad.shape[2]
    row_part = rows_all // shards
    count = rows_all // BLK
    owner_row = owners[0]
    blocks = jnp.stack(
        [broadcast(left_slots[0, 0], "shard", owner_row[block]) for block in range(count)]
    )
    right = broadcast(right_slots[0, 0], "shard", owner_row[count])
    moment_new = first_decay * momentum[0] + (1.0 - first_decay) * grad[0].astype(jnp.float32)
    paired = jnp.stack([grad[0], moment_new.astype(jnp.bfloat16)])
    rotated = jnp.einsum(
        "bkr,gbkn->gbrn",
        blocks,
        paired.reshape(2, count, BLK, col_part),
        preferred_element_type=jnp.float32,
    )
    outgoing = rotated.astype(jnp.bfloat16).reshape(2, shards, row_part, col_part)
    values = lax.all_to_all(outgoing, "shard", split_axis=1, concat_axis=3, tiled=True)
    flat = values.reshape(-1, values.shape[-1])
    turned = jnp.dot(flat, right, preferred_element_type=jnp.float32).reshape(values.shape)
    grad_rot = turned[0, 0]
    moment_rot = turned[1, 0]
    second_new = second_decay * second[0] + (1.0 - second_decay) * grad_rot * grad_rot
    scaled = (moment_rot / (jnp.sqrt(second_new) + guard_eps)).astype(jnp.bfloat16)
    back = lax.dot_general(
        scaled, right, (((1,), (1,)), ((), ())), preferred_element_type=jnp.float32
    ).astype(jnp.bfloat16)
    returning = back.reshape(row_part, shards, col_part)
    values = lax.all_to_all(returning, "shard", split_axis=1, concat_axis=0, tiled=True)
    width = values.shape[2]
    result = jnp.einsum(
        "brk,bkn->brn",
        blocks,
        values.reshape(count, BLK, width),
        preferred_element_type=jnp.float32,
    )
    raw = result.reshape(values.shape)[:, 0, :]
    moment_list = [moment_new]
    second_list = [second_new]
    raw_list = [raw]
    raw_all = jnp.stack(raw_list)
    local_total = jnp.sum(raw_all * raw_all)
    total = lax.psum(local_total, ("shard", "layer"))
    cells = lax.axis_size("layer") * grad.shape[0] * rows_all * col_part * shards
    factor = jnp.minimum(1.0, clip_limit / jnp.sqrt(total / cells + 1e-06))
    return (jnp.stack(moment_list), jnp.stack(second_list), (factor * raw_all).astype(jnp.bfloat16))


def solution(mesh):
    placed = (
        P("layer", None, "shard"),
        P("layer", None, "shard"),
        P("layer", "shard", None),
        P("layer", "shard", None, None),
        P("layer", "shard", None, None),
        P("layer", None),
    )
    return jax.shard_map(
        body,
        mesh=mesh,
        in_specs=placed,
        out_specs=(P("layer", None, "shard"), P("layer", "shard", None), P("layer", None, "shard")),
        check_vma=False,
    )
```

profile of v0, /device:TPU:1, one launch (start us, length us, event | category | flops | bytes accessed | tf_op | source)
XLA Modules:
  0.0 497.2 jit_solution(694099129966863384)
XLA Ops:
  7.2 0.0 all-reduce.3.cloned.1.call-start
  7.2 1.4 fusion.25
  11.8 0.0 copy-start.4
  11.8 1.6 select_bitcast_fusion.4
  13.4 0.9 copy-done.4
  14.3 4.1 select_bitcast_fusion
  18.4 0.0 copy-start.5
  18.4 0.0 copy-start.7
  18.4 0.0 all-reduce.3.cloned.1.call-update
  18.4 1.0 copy-done.5
  19.5 0.4 copy-done.7
  19.9 1.2 fusion.24
  21.1 0.1 copy_bitcast_fusion
  21.2 291.8 %all-reduce.3.cloned.1.call-done = (bf16[1,1152,1152]{2,1,0:T(8,128)(2,1)}, bf16[1,1152,1152]{2,1,0:T(8,128)(2,1)}, bf16[1,1152,1152]{2,1,0:T(8,128)(2,1)}, bf16...) async-done(((bf16[1,1152,1152]{2,1,0:T(8,128)(2,1)}, bf16[1,1152,1152]{2,1,0:T(8,128)(2,1)}, bf16[1,1152,1152]{2,1,0:T(8,128)(2,1)}, bf16[1,1152,1152]{2,1,0:T(8,128)(2,1)}, ...) | async-done | bytes 12714000 | tf_op jit(solution)/shard_map/psum | solution.py:17
  313.0 0.0 copy-start.3
  313.0 2.1 constant_dynamic-update-slice_fusion.3
  315.1 0.4 copy-done.3
  315.5 0.0 copy-start.2
  315.5 0.4 constant_dynamic-update-slice_fusion.2
  315.9 1.3 copy-done.2
  317.3 0.0 copy-start.1
  317.3 0.4 constant_dynamic-update-slice_fusion.1
  317.7 1.3 copy-done.1
  319.0 0.4 constant_dynamic-update-slice_fusion
  319.4 0.0 copy-start
  319.4 1.9 fusion.5
  321.4 2.1 copy-done
  323.5 0.9 copy.19
  324.4 1.7 reshape.80
  326.1 0.4 copy.20
  326.5 40.2 %all_to_all.30 = bf16[2,16,288,64]{2,3,0,1:T(8,128)(2,1)S(1)} all-to-all(bf16[2,16,288,64]{2,3,0,1:T(8,128)(2,1)S(1)} %copy.20), channel_id=1, replica_groups=mesh['shard'=16,'layer'=16] {'shard'}, dimensions={1} | all-to-all | bytes 2359296 | tf_op jit(solution)/shard_map/all_to_all | solution.py:40
  366.7 1.6 copy.21
  368.4 2.0 reshape.81
  370.4 0.0 copy-start.6
  370.4 0.0 copy-start.8
  370.4 3.5 fusion.26
  373.9 0.0 copy-done.6
  374.0 0.0 copy-done.8
  374.0 1.1 convolution_convert_fusion
  375.1 1.2 copy.22
  376.3 6.2 %all-to-all-start.1 = ((bf16[288,16,64]{0,2,1:T(8,128)(2,1)}), bf16[288,16,64]{0,2,1:T(8,128)(2,1)S(1)}, u32[]{:S(2)}, u32[]{:S(2)}) async-start(bf16[288,16,64]{0,2,1:T(8,128)(2,1)} %bitcast.66), calls=%async_computation.1 | async-start | bytes 1572864 | tf_op jit(solution)/shard_map/all_to_all | solution.py:51
  382.5 2.5 bitcast_add_fusion.1
  385.0 16.2 %all-to-all-done.1 = bf16[288,16,64]{0,2,1:T(8,128)(2,1)S(1)} async-done(((bf16[288,16,64]{0,2,1:T(8,128)(2,1)}), bf16[288,16,64]{0,2,1:T(8,128)(2,1)S(1)}, u32[]{:S(2)}, u32[]{:S(2)}) %all-to-all-start.1) | async-done | bytes 589856 | tf_op jit(solution)/shard_map/all_to_all | solution.py:51
  401.2 0.5 copy.23
  401.7 1.2 reshape.83
  402.9 7.9 %multiply_reduce_fusion = (f32[]{:T(128)}, f32[4,1152,64]{1,2,0:T(8,128)S(1)}) fusion(bf16[4,1152,1152]{2,1,0:T(8,128)(2,1)} %copy-done, bf16[4,1152,64]{1,0,2:T(4,128)(2,1)S(1)} %reshape.83), kind=kOutput, calls=%fused_computation.21 | convolution fusion | flops 680067072 | bytes 12386308 | tf_op jit(solution)/shard_map/brk,bkn->brn/dot_general | solution.py:53
  410.8 77.2 %psum.47 = f32[]{:T(128)} all-reduce(f32[]{:T(128)} %get-tuple-element.19), channel_id=1, replica_groups=mesh['shard'=16,'layer'=16] {'shard','layer'}, use_global_device_ids=true, to_apply=%region_6.7 | all-reduce | flops 1 | bytes 8 | tf_op jit(solution)/shard_map/psum | solution.py:65
  488.7 0.1 multiply_convert_fusion
  488.8 0.5 copy.25
  489.3 1.1 convert_element_type.42
Async XLA Ops:
  7.2 305.8 %all-reduce.3.cloned.1.call-start = ((), (), s32[]{:S(2)}) async-start(), calls=%async_computation.2 | async-start | bytes 25427968 | tf_op jit(solution)/shard_map/psum | solution.py:17
  11.8 2.5 copy-start.4
  18.4 1.1 copy-start.5
  18.4 1.5 copy-start.7
  313.0 2.5 copy-start.3
  315.5 1.7 copy-start.2
  317.3 1.7 copy-start.1
  319.4 4.0 copy-start
  370.4 3.5 copy-start.6
  370.4 3.6 copy-start.8
  376.3 24.9 %all-to-all-start.1 = ((bf16[288,16,64]{0,2,1:T(8,128)(2,1)}), bf16[288,16,64]{0,2,1:T(8,128)(2,1)S(1)}, u32[]{:S(2)}, u32[]{:S(2)}) async-start(bf16[288,16,64]{0,2,1:T(8,128)(2,1)} %bitcast.66), calls=%async_computation.1 | async-start | bytes 1572864 | tf_op jit(solution)/shard_map/all_to_all | solution.py:51
Sparse Core Ops, SparseCore 0:
  18.5 294.3 all-reduce.2
where the time goes:
time: 498 us; the launch traced here: 497 us
  waiting for transfers between devices  308 us (62%)
  blocking collectives  117 us (23%)
  local copies, waits for them, and re-layouts  23.5 us (5%)
  between operations  18 us (4%)
  matrix products  14.5 us (3%)
  other arithmetic  9.44 us (2%)
  starting transfers between devices  6.2 us (1%)
    psum x1, waiting for transfers between devices, broadcast(): return lax.psum(block, axis)  292 us
    psum x1, blocking collectives, body(): total = lax.psum(local_total, ('shard', 'layer'))  77.2 us
    all_to_all x1, blocking collectives, body(): lax.all_to_all(outgoing, 'shard', split_axis=1, concat_axis=3, tiled=True)  40.2 us
    all_to_all x1, waiting for transfers between devices, body(): lax.all_to_all(returning, 'shard', split_axis=1, concat_axis=0, tiled=True)  16.2 us
    unnamed x21, local copies, waits for them, and re-layouts  10.5 us
  transfers between devices with their start and end apart: 2, of which 2 were waited for; matrix products, arithmetic and copies ran while one was open for 1% of the time, Pallas kernels for 0%

commit v1 on v0

v1 whole, which is shorter than its diff:
```python
import jax
import jax.numpy as jnp
from jax import lax
from jax.sharding import PartitionSpec as P

BLK = 1152
RING = 8
SIDES = 2

first_decay = 0.9
second_decay = 0.95
guard_eps = 1e-08
clip_limit = 0.2


def rings():
    return [[y * RING + z for z in range(RING)] for y in range(SIDES)]


def ring_shift(value, step):
    pairs = [(y * RING + z, y * RING + (z + step) % RING) for y in range(SIDES) for z in range(RING)]
    return lax.ppermute(value, "shard", pairs)


def cross(value):
    return lax.ppermute(value, "shard", [(s, (s + RING) % (RING * SIDES)) for s in range(RING * SIDES)])


def ring_all_to_all(value):
    return lax.all_to_all(value, "shard", 0, 0, axis_index_groups=rings())


def ring_gather(chunk, z, last_forward):
    rows = chunk.shape[0]
    whole = jnp.zeros((RING * rows,) + chunk.shape[1:], chunk.dtype)

    def put(whole, piece, place):
        return lax.dynamic_update_slice(whole, piece, (((place + RING) % RING) * rows, 0))

    whole = put(whole, chunk, z)
    forward = backward = chunk
    for step in range(1, RING // 2):
        forward = ring_shift(forward, 1)
        backward = ring_shift(backward, -1)
        whole = put(whole, forward, z - step)
        whole = put(whole, backward, z + step)
    if last_forward:
        far = ring_shift(forward, 1)
    else:
        far = ring_shift(backward, -1)
    return put(whole, far, z + RING // 2)


def total_over(value, axis):
    tile = jnp.full((lax.axis_size(axis), 8, 128), value)
    return jnp.sum(lax.all_to_all(tile, axis, 0, 0)[:, 0, 0])


def body(grad, momentum, second, left_slots, right_slots, owners):
    me = lax.axis_index("shard")
    y = me // RING
    z = me % RING
    rows_all = grad.shape[1]
    cols = grad.shape[2]
    half = rows_all // SIDES
    row_part = rows_all // (RING * SIDES)
    count = half // BLK
    width = right_slots.shape[-1]
    piece = BLK // RING
    own = owners[0]
    own_y = own // RING
    own_z = own % RING
    first = y == 0

    left = left_slots[0, 0].reshape(RING, piece, BLK)
    right = right_slots[0, 0].reshape(SIDES, RING, cols, width).transpose(1, 0, 2, 3)
    right = right.reshape(RING, SIDES * cols, width)
    right = jnp.pad(right, ((0, 0), (0, piece - SIDES * cols), (0, BLK - width)))
    item = jnp.where(own[SIDES * count] == me, right, left)
    eighths = ring_all_to_all(item)

    grad_t = grad[0].T
    moment_new = first_decay * momentum[0].T + (1.0 - first_decay) * grad_t.astype(jnp.float32)
    paired = jnp.stack([grad_t, moment_new.astype(jnp.bfloat16)])
    mine = lax.dynamic_slice_in_dim(paired, y * half, half, 2)
    other = cross(lax.dynamic_slice_in_dim(paired, (1 - y) * half, half, 2))
    both = jnp.where(
        first, jnp.concatenate([mine, other], 1), jnp.concatenate([other, mine], 1)
    ).reshape(2 * SIDES * cols, half)

    def pick(block):
        return lax.dynamic_index_in_dim(eighths, own_z[block], 0, keepdims=False)

    keep = jnp.stack([pick(y * count + i) for i in range(count)])
    give = jnp.stack([pick((1 - y) * count + i) for i in range(count)])
    took = cross(give)
    chunk = [
        jnp.where(own_y[y * count + i] == y, keep[i], took[i]) for i in range(count)
    ]
    right_piece = pick(SIDES * count)[: SIDES * cols, :width].reshape(SIDES, cols, width)
    keep_right = lax.dynamic_index_in_dim(right_piece, y, 0, keepdims=False)
    took_right = cross(lax.dynamic_index_in_dim(right_piece, 1 - y, 0, keepdims=False))
    right_chunk = jnp.where(own_y[SIDES * count] == y, keep_right, took_right)

    right_half = ring_gather(right_chunk, z, True).reshape(RING, cols, width)
    right_other = cross(right_half)
    right_all = jnp.where(
        first,
        jnp.stack([right_half, right_other], 1),
        jnp.stack([right_other, right_half], 1),
    ).reshape(RING * SIDES * cols, width)
    blocks = [ring_gather(chunk[i], z, i % 2 == 0) for i in range(count)]

    rotated = jnp.stack(
        [
            lax.dot_general(
                blocks[i],
                both[:, i * BLK : (i + 1) * BLK],
                (((0,), (1,)), ((), ())),
                preferred_element_type=jnp.float32,
            ).astype(jnp.bfloat16)
            for i in range(count)
        ]
    )
    values = ring_all_to_all(rotated.reshape(RING, row_part, 2 * SIDES * cols))
    values = values.reshape(RING, row_part, 2, SIDES * cols).transpose(2, 1, 0, 3)
    flat = values.reshape(2 * row_part, width)
    turned = jnp.dot(flat, right_all, preferred_element_type=jnp.float32)
    grad_rot = turned[:row_part]
    moment_rot = turned[row_part:]
    second_new = second_decay * second[0] + (1.0 - second_decay) * grad_rot * grad_rot
    scaled = (moment_rot / (jnp.sqrt(second_new) + guard_eps)).astype(jnp.bfloat16)
    back = lax.dot_general(
        scaled, right_all, (((1,), (1,)), ((), ())), preferred_element_type=jnp.float32
    ).astype(jnp.bfloat16)
    returning = back.reshape(row_part, RING, SIDES * cols).transpose(1, 0, 2)
    values = ring_all_to_all(returning).reshape(count, BLK, SIDES * cols)
    raw = jnp.concatenate(
        [
            lax.dot_general(
                values[i], blocks[i], (((0,), (1,)), ((), ())), preferred_element_type=jnp.float32
            )
            for i in range(count)
        ],
        1,
    )
    local_total = jnp.sum(raw * raw)
    raw_mine = lax.dynamic_slice_in_dim(raw, y * cols, cols, 0)
    raw_other = cross(lax.dynamic_slice_in_dim(raw, (1 - y) * cols, cols, 0).astype(jnp.bfloat16))
    raw_other = raw_other.astype(jnp.float32)
    total = total_over(total_over(local_total, "shard"), "layer")
    cells = lax.axis_size("layer") * grad.shape[0] * rows_all * cols * RING * SIDES
    factor = jnp.minimum(1.0, clip_limit / jnp.sqrt(total / cells + 1e-06))
    direction = jnp.where(
        first,
        jnp.concatenate([raw_mine, raw_other], 1),
        jnp.concatenate([raw_other, raw_mine], 1),
    )
    direction = (factor * direction).astype(jnp.bfloat16)
    return (moment_new.T[None], second_new[None], direction.T[None])


def solution(mesh):
    placed = (
        P("layer", None, "shard"),
        P("layer", None, "shard"),
        P("layer", "shard", None),
        P("layer", "shard", None, None),
        P("layer", "shard", None, None),
        P("layer", None),
    )
    return jax.shard_map(
        body,
        mesh=mesh,
        in_specs=placed,
        out_specs=(P("layer", None, "shard"), P("layer", "shard", None), P("layer", None, "shard")),
        check_vma=False,
    )
```

time: 498 us -> 298 us (0.60)
  waiting for transfers between devices: 308 us -> 161 us
  blocking collectives: 117 us -> 0 us
  starting transfers between devices: 6.2 us -> 65 us
  other arithmetic: 9.44 us -> 25.9 us
  matrix products: 14.5 us -> 6.35 us
    psum x1 -> x0, waiting for transfers between devices: 292 us -> none  [broadcast(): return lax.psum(block, axis)]
    ppermute x0 -> x26, waiting for transfers between devices: none -> 83.5 us  [the longest x21 64.1 us: ring_shift(): return lax.ppermute(value, 'shard', pairs)]
    psum x1 -> x0, blocking collectives: 77.2 us -> none  [body(): total = lax.psum(local_total, ('shard', 'layer'))]
    all_to_all x1 -> x5, waiting for transfers between devices: 16.2 us -> 77.8 us  [the longest x3 64.5 us: ring_all_to_all(): return lax.all_to_all(value, 'shard', 0, 0, axis_index_groups=rings())]
    all_to_all x1 -> x0, blocking collectives: 40.2 us -> none  [body(): lax.all_to_all(outgoing, 'shard', split_axis=1, concat_axis=3, tiled=True)]
    all_to_all x1 -> x5, starting transfers between devices: 6.16 us -> 38.1 us  [the longest x3 23.5 us: ring_all_to_all(): return lax.all_to_all(value, 'shard', 0, 0, axis_index_groups=rings())]
    ppermute x0 -> x26, starting transfers between devices: none -> 26.9 us  [the longest x21 19.7 us: ring_shift(): return lax.ppermute(value, 'shard', pairs)]
    unnamed x21 -> x18, local copies, waits for them, and re-layouts: 10.5 us -> 0.85 us
  transfers between devices with their start and end apart: 2 -> 31, of which waited for: 2 -> 18; matrix products, arithmetic and copies ran while one was open for 1% -> 11% of each run, Pallas kernels for 0% -> 0%
where the time goes in v1:
time: 298 us; the launch traced here: 297 us
  waiting for transfers between devices  161 us (54%)
  starting transfers between devices  65 us (22%)
  other arithmetic  25.9 us (9%)
  local copies, waits for them, and re-layouts  24.3 us (8%)
  between operations  14.1 us (5%)
  matrix products  6.35 us (2%)
    all_to_all x3, waiting for transfers between devices, ring_all_to_all(): return lax.all_to_all(value, 'shard', 0, 0, axis_index_groups=rings())  64.5 us
    ppermute x21, waiting for transfers between devices, ring_shift(): return lax.ppermute(value, 'shard', pairs)  64.1 us
    all_to_all x3, starting transfers between devices, ring_all_to_all(): return lax.all_to_all(value, 'shard', 0, 0, axis_index_groups=rings())  23.5 us
    ppermute x21, starting transfers between devices, ring_shift(): return lax.ppermute(value, 'shard', pairs)  19.7 us
    ppermute x5, waiting for transfers between devices, cross(): lax.ppermute(value, 'shard', [(s, (s + RING) % (RING * SIDES)) for s in r...  19.4 us
    all_to_all x2, starting transfers between devices, total_over(): return jnp.sum(lax.all_to_all(tile, axis, 0, 0)[:, 0, 0])  14.6 us
    all_to_all x2, waiting for transfers between devices, total_over(): return jnp.sum(lax.all_to_all(tile, axis, 0, 0)[:, 0, 0])  13.3 us
    ppermute x5, starting transfers between devices, cross(): lax.ppermute(value, 'shard', [(s, (s + RING) % (RING * SIDES)) for s in r...  7.18 us
  transfers between devices with their start and end apart: 31, of which 18 were waited for; matrix products, arithmetic and copies ran while one was open for 11% of the time, Pallas kernels for 0%

profile of v1, /device:TPU:1, one launch (start us, length us, event | category | flops | bytes accessed | tf_op | source)
XLA Modules:
  0.0 297.0 jit_solution(10122872114401522156)
XLA Ops:
  0.6 1.2 slice.45
  1.9 1.8 copy.16
  4.3 3.9 %pad_select_fusion = bf16[8,144,1152]{2,1,0:T(8,128)(2,1)} fusion(bf16[8,144,1152]{2,1,0:T(8,128)(2,1)} %bitcast.110, bf16[8,128,1024]{2,1,0:T(8,128)(2,1)S(1)} %bitcast.106, pred[]{:T(512)S(6)} %eq.44), kind=kLoop, calls=%fused_computation | loop fusion | flops 1327104 | bytes 7405569 | tf_op jit(solution)/shard_map/jit(_where)/select_n | solution.py:79
  8.3 9.1 %all-to-all-start = ((bf16[8,144,1152]{2,1,0:T(8,128)(2,1)}), bf16[8,144,1152]{2,1,0:T(8,128)(2,1)S(1)}, u32[]{:S(2)}, u32[]{:S(2)}) async-start(bf16[8,144,1152]{2,1,0:T(8,128)(2,1)} %pad_select_fusion), calls=%async_computation | async-start | bytes 5308416 | tf_op jit(solution)/shard_map/all_to_all | solution.py:30
  17.4 1.5 fusion.13
  18.9 1.1 fusion.17
  20.0 1.3 collective-permute-start.8
  27.8 53.3 %all-to-all-done = bf16[8,144,1152]{2,1,0:T(8,128)(2,1)S(1)} async-done(((bf16[8,144,1152]{2,1,0:T(8,128)(2,1)}), bf16[8,144,1152]{2,1,0:T(8,128)(2,1)S(1)}, u32[]{:S(2)}, u32[]{:S(2)}) %all-to-all-start) | async-done | bytes 2654240 | tf_op jit(solution)/shard_map/all_to_all | solution.py:30
  82.0 1.3 collective-permute-start.16
  90.4 1.1 broadcast_in_dim.16
  92.2 2.7 collective-permute-start.18
  94.9 1.9 maximum_select_fusion.1
  97.3 2.7 collective-permute-start.20
  100.0 1.4 collective-permute-done
  101.6 1.1 constant_dynamic-update-slice_fusion.23
  102.8 2.7 collective-permute-start.2
  105.7 1.2 constant_dynamic-update-slice_fusion.15
  107.0 4.1 %collective-permute-done.1 = bf16[144,1152]{1,0:T(8,128)(2,1)S(1)} collective-permute-done((bf16[144,1152]{1,0:T(8,128)(2,1)S(1)}, bf16[144,1152]{1,0:T(8,128)(2,1)S(1)}, u32[]{:S(2)}, u32[]{:S(2)}) %collective-permute-start.1) | collective-permute-done | bytes 331808 | tf_op jit(solution)/shard_map/ppermute | solution.py:22
  111.1 1.5 collective-permute-start.3
  112.7 5.5 %collective-permute-done.9 = bf16[144,1152]{1,0:T(8,128)(2,1)S(1)} collective-permute-done((bf16[144,1152]{1,0:T(8,128)(2,1)S(1)}, bf16[144,1152]{1,0:T(8,128)(2,1)S(1)}, u32[]{:S(2)}, u32[]{:S(2)}) %collective-permute-start.9) | collective-permute-done | bytes 331808 | tf_op jit(solution)/shard_map/ppermute | solution.py:22
  118.2 1.5 collective-permute-start.11
  119.8 5.5 %collective-permute-done.3 = bf16[144,1152]{1,0:T(8,128)(2,1)S(1)} collective-permute-done((bf16[144,1152]{1,0:T(8,128)(2,1)S(1)}, bf16[144,1152]{1,0:T(8,128)(2,1)S(1)}, u32[]{:S(2)}, u32[]{:S(2)}) %collective-permute-start.3) | collective-permute-done | bytes 331808 | tf_op jit(solution)/shard_map/ppermute | solution.py:22
  125.3 6.5 %collective-permute-done.11 = bf16[144,1152]{1,0:T(8,128)(2,1)S(1)} collective-permute-done((bf16[144,1152]{1,0:T(8,128)(2,1)S(1)}, bf16[144,1152]{1,0:T(8,128)(2,1)S(1)}, u32[]{:S(2)}, u32[]{:S(2)}) %collective-permute-start.11) | collective-permute-done | bytes 331808 | tf_op jit(solution)/shard_map/ppermute | solution.py:22
  131.8 2.6 collective-permute-done.12
  134.4 2.7 collective-permute-start.14
  137.2 1.7 collective-permute-done.5
  139.0 6.6 %collective-permute-done.13 = bf16[144,1152]{1,0:T(8,128)(2,1)S(1)} collective-permute-done((bf16[144,1152]{1,0:T(8,128)(2,1)S(1)}, bf16[144,1152]{1,0:T(8,128)(2,1)S(1)}, u32[]{:S(2)}, u32[]{:S(2)}) %collective-permute-start.13) | collective-permute-done | bytes 331808 | tf_op jit(solution)/shard_map/ppermute | solution.py:22
  145.6 2.7 collective-permute-start.15
  148.4 4.7 %collective-permute-done.7 = bf16[144,1152]{1,0:T(8,128)(2,1)S(1)} collective-permute-done((bf16[144,1152]{1,0:T(8,128)(2,1)S(1)}, bf16[144,1152]{1,0:T(8,128)(2,1)S(1)}, u32[]{:S(2)}, u32[]{:S(2)}) %collective-permute-start.7) | collective-permute-done | bytes 331808 | tf_op jit(solution)/shard_map/ppermute | solution.py:22
  153.2 1.0 fusion
  154.7 1.3 collective-permute-done.15
  156.0 1.0 fusion.1
  157.0 1.1 pad_maximum_fusion.1
  158.1 4.7 %all-to-all-start.1 = ((bf16[8,288,256]{2,1,0:T(8,128)(2,1)}), bf16[8,288,256]{2,1,0:T(8,128)(2,1)}, u32[]{:S(2)}, u32[]{:S(2)}) async-start(bf16[8,288,256]{2,1,0:T(8,128)(2,1)} %bitcast.108), calls=%async_computation.1 | async-start | bytes 2359296 | tf_op jit(solution)/shard_map/all_to_all | solution.py:30
  162.8 1.6 constant_dynamic-update-slice_fusion.6
  165.1 1.5 collective-permute-start.21
  166.5 1.6 collective-permute-start.22
  168.1 1.6 constant_dynamic-update-slice_fusion.4
  170.3 21.1 %collective-permute-done.21 = bf16[64,1024]{1,0:T(8,128)(2,1)S(1)} collective-permute-done((bf16[64,1024]{1,0:T(8,128)(2,1)}, bf16[64,1024]{1,0:T(8,128)(2,1)S(1)}, u32[]{:S(2)}, u32[]{:S(2)}) %collective-permute-start.21) | collective-permute-done | bytes 131104 | tf_op jit(solution)/shard_map/ppermute | solution.py:22
  192.7 4.0 %collective-permute-done.23 = bf16[64,1024]{1,0:T(8,128)(2,1)S(1)} collective-permute-done((bf16[64,1024]{1,0:T(8,128)(2,1)S(1)}, bf16[64,1024]{1,0:T(8,128)(2,1)S(1)}, u32[]{:S(2)}, u32[]{:S(2)}) %collective-permute-start.23) | collective-permute-done | bytes 131104 | tf_op jit(solution)/shard_map/ppermute | solution.py:22
  197.3 3.0 %collective-permute-start.24 = (bf16[8,64,1024]{2,1,0:T(8,128)(2,1)}, bf16[8,64,1024]{2,1,0:T(8,128)(2,1)}, u32[]{:S(2)}, u32[]{:S(2)}) collective-permute-start(bf16[8,64,1024]{2,1,0:T(8,128)(2,1)} %bitcast.34), channel_id=1, source_target_pairs={{0,128},{16,144},{32,160},{48,176},{64,192},{80,208},{96,224},{112... | collective-permute-start | bytes 3145736 | tf_op jit(solution)/shard_map/ppermute | solution.py:26
  200.4 18.0 %collective-permute-done.24 = bf16[8,64,1024]{2,1,0:T(8,128)(2,1)} collective-permute-done((bf16[8,64,1024]{2,1,0:T(8,128)(2,1)}, bf16[8,64,1024]{2,1,0:T(8,128)(2,1)}, u32[]{:S(2)}, u32[]{:S(2)}) %collective-permute-start.24) | collective-permute-done | bytes 1048608 | tf_op jit(solution)/shard_map/ppermute | solution.py:26
  218.4 4.2 %maximum_select_fusion = bf16[8,2,64,1024]{3,2,1,0:T(8,128)(2,1)} fusion(bf16[8,1,64,1024]{3,2,1,0:T(8,128)(2,1)} %bitcast.35, bf16[8,1,64,1024]{3,2,1,0:T(8,128)(2,1)} %bitcast.33, pred[]{:T(512)S(6)} %eq.45), kind=kLoop, calls=%fused_computation.5 | loop fusion | flops 3145728 | bytes 4194305 | tf_op jit(solution)/shard_map/jit(_where)/select_n | solution.py:107
  222.6 3.5 %reshape.64 = bf16[8,288,2,128]{3,2,1,0:T(2,128)(2,1)} reshape(bf16[8,288,256]{2,1,0:T(8,128)(2,1)} %all-to-all-done.1) | data formatting | bytes 2359296 | tf_op jit(solution)/shard_map/reshape | solution.py:126
  226.2 2.2 copy.17
  228.4 1.4 fusion.6
  229.8 1.1 fusion.2
  231.3 0.9 copy.30
  232.2 9.7 %all-to-all-start.2 = ((bf16[8,288,128]{2,1,0:T(8,128)(2,1)}), bf16[8,288,128]{2,1,0:T(8,128)(2,1)}, u32[]{:S(2)}, u32[]{:S(2)}) async-start(bf16[8,288,128]{2,1,0:T(8,128)(2,1)} %bitcast.111), calls=%async_computation.2 | async-start | bytes 1179648 | tf_op jit(solution)/shard_map/all_to_all | solution.py:30
  241.8 2.5 multiply_add_fusion
  244.4 2.5 fusion.27
  246.9 11.2 %all-to-all-done.2 = bf16[8,288,128]{2,1,0:T(8,128)(2,1)} async-done(((bf16[8,288,128]{2,1,0:T(8,128)(2,1)}), bf16[8,288,128]{2,1,0:T(8,128)(2,1)}, u32[]{:S(2)}, u32[]{:S(2)}) %all-to-all-start.2) | async-done | bytes 589856 | tf_op jit(solution)/shard_map/all_to_all | solution.py:30
  258.1 1.2 fusion.33
  259.4 0.9 fusion.37
  260.3 0.9 fusion.36
  261.3 0.9 fusion.4
  262.2 1.2 broadcast_in_dim.18
  263.4 3.5 %all-to-all-start.3 = ((f32[16,8,128]{2,1,0:T(8,128)}), f32[16,8,128]{2,1,0:T(8,128)S(1)}, u32[]{:S(2)}, u32[]{:S(2)}) async-start(f32[16,8,128]{2,1,0:T(8,128)} %broadcast_in_dim.18), calls=%async_computation.3 | async-start | bytes 131072 | tf_op jit(solution)/shard_map/all_to_all | solution.py:56
  267.0 1.4 collective-permute-start.25
  268.4 6.0 %all-to-all-done.3 = f32[16,8,128]{2,1,0:T(8,128)S(1)} async-done(((f32[16,8,128]{2,1,0:T(8,128)}), f32[16,8,128]{2,1,0:T(8,128)S(1)}, u32[]{:S(2)}, u32[]{:S(2)}) %all-to-all-start.3) | async-done | bytes 65568 | tf_op jit(solution)/shard_map/all_to_all | solution.py:56
  275.0 1.2 broadcast_in_dim.19
  276.2 11.1 %all-to-all-start.4 = ((f32[16,8,128]{2,1,0:T(8,128)}), f32[16,8,128]{2,1,0:T(8,128)S(1)}, u32[]{:S(2)}, u32[]{:S(2)}) async-start(f32[16,8,128]{2,1,0:T(8,128)} %broadcast_in_dim.19), calls=%async_computation.4 | async-start | bytes 131072 | tf_op jit(solution)/shard_map/all_to_all | solution.py:56
  287.4 7.3 %all-to-all-done.4 = f32[16,8,128]{2,1,0:T(8,128)S(1)} async-done(((f32[16,8,128]{2,1,0:T(8,128)}), f32[16,8,128]{2,1,0:T(8,128)S(1)}, u32[]{:S(2)}, u32[]{:S(2)}) %all-to-all-start.4) | async-done | bytes 65568 | tf_op jit(solution)/shard_map/all_to_all | solution.py:56
  296.1 0.9 fusion.14
  (78 shorter events, 10.6 us)
Async XLA Ops:
  8.3 9.2 %copy-start.3 = (bf16[1,4608,64]{1,2,0:T(8,128)(2,1)S(1)}, bf16[1,4608,64]{1,2,0:T(8,128)(2,1)}, u32[]{:S(2)}) copy-start(bf16[1,4608,64]{1,2,0:T(8,128)(2,1)} %param.6) | copy-start | bytes 1769476
  8.3 72.8 %all-to-all-start = ((bf16[8,144,1152]{2,1,0:T(8,128)(2,1)}), bf16[8,144,1152]{2,1,0:T(8,128)(2,1)S(1)}, u32[]{:S(2)}, u32[]{:S(2)}) async-start(bf16[8,144,1152]{2,1,0:T(8,128)(2,1)} %pad_select_fusion), calls=%async_computation | async-start | bytes 5308416 | tf_op jit(solution)/shard_map/all_to_all | solution.py:30
  17.4 3.9 %copy-start.8 = (s32[1,16]{1,0:T(1,128)S(1)}, s32[1,16]{1,0:T(1,128)}, u32[]{:S(2)}) copy-start(s32[1,16]{1,0:T(1,128)} %param.11) | copy-start | bytes 196
  20.0 74.9 %collective-permute-start.8 = (bf16[2,64,2304]{2,1,0:T(8,128)(2,1)}, bf16[2,64,2304]{2,1,0:T(8,128)(2,1)}, u32[]{:S(2)}, u32[]{:S(2)}) collective-permute-start(bf16[2,64,2304]{2,1,0:T(8,128)(2,1)} %get-tuple-element.13), channel_id=1, source_target_pairs={{0,128},{16,144},{32,160},{48,176},{64,192},{80,208},{96,224},{112... | collective-permute-start | bytes 1769480 | tf_op jit(solution)/shard_map/ppermute | solution.py:26
  81.1 20.5 %copy-start.2 = (bf16[8,144,1152]{2,1,0:T(8,128)(2,1)}, bf16[8,144,1152]{2,1,0:T(8,128)(2,1)S(1)}, u32[]{:S(2)}) copy-start(bf16[8,144,1152]{2,1,0:T(8,128)(2,1)S(1)} %all-to-all-done) | copy-start | bytes 7962628
  82.0 8.3 %collective-permute-start.16 = (bf16[64,1024]{1,0:T(8,128)(2,1)}, bf16[64,1024]{1,0:T(8,128)(2,1)}, u32[]{:S(2)}, u32[]{:S(2)}) collective-permute-start(bf16[64,1024]{1,0:T(8,128)(2,1)} %dynamic-slice_bitcast_fusion.1), channel_id=1, source_target_pairs={{0,128},{16,144},{32,160},{48,176},{64,192},{80,208},{96,224},{112... | collective-permute-start | bytes 393224 | tf_op jit(solution)/shard_map/ppermute | solution.py:26
  84.2 17.2 %collective-permute-start = (bf16[2,144,1152]{2,1,0:T(8,128)(2,1)}, bf16[2,144,1152]{2,1,0:T(8,128)(2,1)}, u32[]{:S(2)}, u32[]{:S(2)}) collective-permute-start(bf16[2,144,1152]{2,1,0:T(8,128)(2,1)} %pad_maximum_fusion.2), channel_id=1, source_target_pairs={{0,128},{16,144},{32,160},{48,176},{64,192},{80,208},{96,224},{112... | collective-permute-start | bytes 1990664 | tf_op jit(solution)/shard_map/ppermute | solution.py:26
  92.2 5.1 %collective-permute-start.17 = (bf16[64,1024]{1,0:T(8,128)(2,1)S(1)}, bf16[64,1024]{1,0:T(8,128)(2,1)}, u32[]{:S(2)}, u32[]{:S(2)}) collective-permute-start(bf16[64,1024]{1,0:T(8,128)(2,1)S(1)} %get-tuple-element.8), channel_id=1, source_target_pairs={{0,16},{16,32},{32,48},{48,64},{64,80},{80,96},{96,112},{112,0},{1... | collective-permute-start | bytes 393224 | tf_op jit(solution)/shard_map/ppermute | solution.py:22
  92.2 5.1 %collective-permute-start.18 = (bf16[64,1024]{1,0:T(8,128)(2,1)S(1)}, bf16[64,1024]{1,0:T(8,128)(2,1)S(1)}, u32[]{:S(2)}, u32[]{:S(2)}) collective-permute-start(bf16[64,1024]{1,0:T(8,128)(2,1)S(1)} %get-tuple-element.8), channel_id=1, source_target_pairs={{0,112},{16,0},{32,16},{48,32},{64,48},{80,64},{96,80},{112,96},{1... | collective-permute-start | bytes 393224 | tf_op jit(solution)/shard_map/ppermute | solution.py:22
  97.3 67.7 %collective-permute-start.19 = (bf16[64,1024]{1,0:T(8,128)(2,1)}, bf16[64,1024]{1,0:T(8,128)(2,1)}, u32[]{:S(2)}, u32[]{:S(2)}) collective-permute-start(bf16[64,1024]{1,0:T(8,128)(2,1)} %collective-permute-done.17), channel_id=1, source_target_pairs={{0,16},{16,32},{32,48},{48,64},{64,80},{80,96},{96,112},{112,0},{1... | collective-permute-start | bytes 393224 | tf_op jit(solution)/shard_map/ppermute | solution.py:22
  97.3 69.2 %collective-permute-start.20 = (bf16[64,1024]{1,0:T(8,128)(2,1)S(1)}, bf16[64,1024]{1,0:T(8,128)(2,1)S(1)}, u32[]{:S(2)}, u32[]{:S(2)}) collective-permute-start(bf16[64,1024]{1,0:T(8,128)(2,1)S(1)} %collective-permute-done.18), channel_id=1, source_target_pairs={{0,112},{16,0},{32,16},{48,32},{64,48},{80,64},{96,80},{112,96},{1... | collective-permute-start | bytes 393224 | tf_op jit(solution)/shard_map/ppermute | solution.py:22
  102.7 8.3 %collective-permute-start.1 = (bf16[144,1152]{1,0:T(8,128)(2,1)S(1)}, bf16[144,1152]{1,0:T(8,128)(2,1)S(1)}, u32[]{:S(2)}, u32[]{:S(2)}) collective-permute-start(bf16[144,1152]{1,0:T(8,128)(2,1)S(1)} %get-tuple-element.4), channel_id=1, source_target_pairs={{0,16},{16,32},{32,48},{48,64},{64,80},{80,96},{96,112},{112,0},{1... | collective-permute-start | bytes 995336 | tf_op jit(solution)/shard_map/ppermute | solution.py:22
  102.8 8.3 %collective-permute-start.2 = (bf16[144,1152]{1,0:T(8,128)(2,1)S(1)}, bf16[144,1152]{1,0:T(8,128)(2,1)S(1)}, u32[]{:S(2)}, u32[]{:S(2)}) collective-permute-start(bf16[144,1152]{1,0:T(8,128)(2,1)S(1)} %get-tuple-element.4), channel_id=1, source_target_pairs={{0,112},{16,0},{32,16},{48,32},{64,48},{80,64},{96,80},{112,96},{1... | collective-permute-start | bytes 995336 | tf_op jit(solution)/shard_map/ppermute | solution.py:22
  106.9 11.3 %collective-permute-start.9 = (bf16[144,1152]{1,0:T(8,128)(2,1)S(1)}, bf16[144,1152]{1,0:T(8,128)(2,1)S(1)}, u32[]{:S(2)}, u32[]{:S(2)}) collective-permute-start(bf16[144,1152]{1,0:T(8,128)(2,1)S(1)} %get-tuple-element.6), channel_id=1, source_target_pairs={{0,16},{16,32},{32,48},{48,64},{64,80},{80,96},{96,112},{112,0},{1... | collective-permute-start | bytes 995336 | tf_op jit(solution)/shard_map/ppermute | solution.py:22
  111.1 7.2 %collective-permute-start.10 = (bf16[144,1152]{1,0:T(8,128)(2,1)S(1)}, bf16[144,1152]{1,0:T(8,128)(2,1)S(1)}, u32[]{:S(2)}, u32[]{:S(2)}) collective-permute-start(bf16[144,1152]{1,0:T(8,128)(2,1)S(1)} %get-tuple-element.6), channel_id=1, source_target_pairs={{0,112},{16,0},{32,16},{48,32},{64,48},{80,64},{96,80},{112,96},{1... | collective-permute-start | bytes 995336 | tf_op jit(solution)/shard_map/ppermute | solution.py:22
  111.1 14.2 %collective-permute-start.3 = (bf16[144,1152]{1,0:T(8,128)(2,1)S(1)}, bf16[144,1152]{1,0:T(8,128)(2,1)S(1)}, u32[]{:S(2)}, u32[]{:S(2)}) collective-permute-start(bf16[144,1152]{1,0:T(8,128)(2,1)S(1)} %collective-permute-done.1), channel_id=1, source_target_pairs={{0,16},{16,32},{32,48},{48,64},{64,80},{80,96},{96,112},{112,0},{1... | collective-permute-start | bytes 995336 | tf_op jit(solution)/shard_map/ppermute | solution.py:22
  118.2 16.3 %collective-permute-start.4 = (bf16[144,1152]{1,0:T(8,128)(2,1)S(1)}, bf16[144,1152]{1,0:T(8,128)(2,1)S(1)}, u32[]{:S(2)}, u32[]{:S(2)}) collective-permute-start(bf16[144,1152]{1,0:T(8,128)(2,1)S(1)} %collective-permute-done.2), channel_id=1, source_target_pairs={{0,112},{16,0},{32,16},{48,32},{64,48},{80,64},{96,80},{112,96},{1... | collective-permute-start | bytes 995336 | tf_op jit(solution)/shard_map/ppermute | solution.py:22
  118.2 13.6 %collective-permute-start.11 = (bf16[144,1152]{1,0:T(8,128)(2,1)S(1)}, bf16[144,1152]{1,0:T(8,128)(2,1)S(1)}, u32[]{:S(2)}, u32[]{:S(2)}) collective-permute-start(bf16[144,1152]{1,0:T(8,128)(2,1)S(1)} %collective-permute-done.9), channel_id=1, source_target_pairs={{0,16},{16,32},{32,48},{48,64},{64,80},{80,96},{96,112},{112,0},{1... | collective-permute-start | bytes 995336 | tf_op jit(solution)/shard_map/ppermute | solution.py:22
  125.3 9.1 %collective-permute-start.12 = (bf16[144,1152]{1,0:T(8,128)(2,1)S(1)}, bf16[144,1152]{1,0:T(8,128)(2,1)S(1)}, u32[]{:S(2)}, u32[]{:S(2)}) collective-permute-start(bf16[144,1152]{1,0:T(8,128)(2,1)S(1)} %collective-permute-done.10), channel_id=1, source_target_pairs={{0,112},{16,0},{32,16},{48,32},{64,48},{80,64},{96,80},{112,96},{1... | collective-permute-start | bytes 995336 | tf_op jit(solution)/shard_map/ppermute | solution.py:22
  131.8 7.2 %collective-permute-start.5 = (bf16[144,1152]{1,0:T(8,128)(2,1)S(1)}, bf16[144,1152]{1,0:T(8,128)(2,1)S(1)}, u32[]{:S(2)}, u32[]{:S(2)}) collective-permute-start(bf16[144,1152]{1,0:T(8,128)(2,1)S(1)} %collective-permute-done.3), channel_id=1, source_target_pairs={{0,16},{16,32},{32,48},{48,64},{64,80},{80,96},{96,112},{112,0},{1... | collective-permute-start | bytes 995336 | tf_op jit(solution)/shard_map/ppermute | solution.py:22
  134.4 11.2 %collective-permute-start.13 = (bf16[144,1152]{1,0:T(8,128)(2,1)S(1)}, bf16[144,1152]{1,0:T(8,128)(2,1)S(1)}, u32[]{:S(2)}, u32[]{:S(2)}) collective-permute-start(bf16[144,1152]{1,0:T(8,128)(2,1)S(1)} %collective-permute-done.11), channel_id=1, source_target_pairs={{0,16},{16,32},{32,48},{48,64},{64,80},{80,96},{96,112},{112,0},{1... | collective-permute-start | bytes 995336 | tf_op jit(solution)/shard_map/ppermute | solution.py:22
  134.4 11.2 %collective-permute-start.14 = (bf16[144,1152]{1,0:T(8,128)(2,1)S(1)}, bf16[144,1152]{1,0:T(8,128)(2,1)S(1)}, u32[]{:S(2)}, u32[]{:S(2)}) collective-permute-start(bf16[144,1152]{1,0:T(8,128)(2,1)S(1)} %collective-permute-done.12), channel_id=1, source_target_pairs={{0,112},{16,0},{32,16},{48,32},{64,48},{80,64},{96,80},{112,96},{1... | collective-permute-start | bytes 995336 | tf_op jit(solution)/shard_map/ppermute | solution.py:22
  139.0 9.4 %collective-permute-start.6 = (bf16[144,1152]{1,0:T(8,128)(2,1)S(1)}, bf16[144,1152]{1,0:T(8,128)(2,1)S(1)}, u32[]{:S(2)}, u32[]{:S(2)}) collective-permute-start(bf16[144,1152]{1,0:T(8,128)(2,1)S(1)} %collective-permute-done.4), channel_id=1, source_target_pairs={{0,112},{16,0},{32,16},{48,32},{64,48},{80,64},{96,80},{112,96},{1... | collective-permute-start | bytes 995336 | tf_op jit(solution)/shard_map/ppermute | solution.py:22
  145.6 7.6 %collective-permute-start.7 = (bf16[144,1152]{1,0:T(8,128)(2,1)S(1)}, bf16[144,1152]{1,0:T(8,128)(2,1)S(1)}, u32[]{:S(2)}, u32[]{:S(2)}) collective-permute-start(bf16[144,1152]{1,0:T(8,128)(2,1)S(1)} %collective-permute-done.5), channel_id=1, source_target_pairs={{0,16},{16,32},{32,48},{48,64},{64,80},{80,96},{96,112},{112,0},{1... | collective-permute-start | bytes 995336 | tf_op jit(solution)/shard_map/ppermute | solution.py:22
  145.6 10.4 %collective-permute-start.15 = (bf16[144,1152]{1,0:T(8,128)(2,1)S(1)}, bf16[144,1152]{1,0:T(8,128)(2,1)S(1)}, u32[]{:S(2)}, u32[]{:S(2)}) collective-permute-start(bf16[144,1152]{1,0:T(8,128)(2,1)S(1)} %collective-permute-done.14), channel_id=1, source_target_pairs={{0,112},{16,0},{32,16},{48,32},{64,48},{80,64},{96,80},{112,96},{1... | collective-permute-start | bytes 995336 | tf_op jit(solution)/shard_map/ppermute | solution.py:22
  153.2 1.5 copy-start
  158.1 64.5 %all-to-all-start.1 = ((bf16[8,288,256]{2,1,0:T(8,128)(2,1)}), bf16[8,288,256]{2,1,0:T(8,128)(2,1)}, u32[]{:S(2)}, u32[]{:S(2)}) async-start(bf16[8,288,256]{2,1,0:T(8,128)(2,1)} %bitcast.108), calls=%async_computation.1 | async-start | bytes 2359296 | tf_op jit(solution)/shard_map/all_to_all | solution.py:30
  165.1 26.3 %collective-permute-start.21 = (bf16[64,1024]{1,0:T(8,128)(2,1)}, bf16[64,1024]{1,0:T(8,128)(2,1)S(1)}, u32[]{:S(2)}, u32[]{:S(2)}) collective-permute-start(bf16[64,1024]{1,0:T(8,128)(2,1)} %collective-permute-done.19), channel_id=1, source_target_pairs={{0,16},{16,32},{32,48},{48,64},{64,80},{80,96},{96,112},{112,0},{1... | collective-permute-start | bytes 393224 | tf_op jit(solution)/shard_map/ppermute | solution.py:22
  166.5 25.5 %collective-permute-start.22 = (bf16[64,1024]{1,0:T(8,128)(2,1)S(1)}, bf16[64,1024]{1,0:T(8,128)(2,1)S(1)}, u32[]{:S(2)}, u32[]{:S(2)}) collective-permute-start(bf16[64,1024]{1,0:T(8,128)(2,1)S(1)} %collective-permute-done.20), channel_id=1, source_target_pairs={{0,112},{16,0},{32,16},{48,32},{64,48},{80,64},{96,80},{112,96},{1... | collective-permute-start | bytes 393224 | tf_op jit(solution)/shard_map/ppermute | solution.py:22
  191.4 5.3 %collective-permute-start.23 = (bf16[64,1024]{1,0:T(8,128)(2,1)S(1)}, bf16[64,1024]{1,0:T(8,128)(2,1)S(1)}, u32[]{:S(2)}, u32[]{:S(2)}) collective-permute-start(bf16[64,1024]{1,0:T(8,128)(2,1)S(1)} %collective-permute-done.21), channel_id=1, source_target_pairs={{0,16},{16,32},{32,48},{48,64},{64,80},{80,96},{96,112},{112,0},{1... | collective-permute-start | bytes 393224 | tf_op jit(solution)/shard_map/ppermute | solution.py:22
  197.3 21.1 %collective-permute-start.24 = (bf16[8,64,1024]{2,1,0:T(8,128)(2,1)}, bf16[8,64,1024]{2,1,0:T(8,128)(2,1)}, u32[]{:S(2)}, u32[]{:S(2)}) collective-permute-start(bf16[8,64,1024]{2,1,0:T(8,128)(2,1)} %bitcast.34), channel_id=1, source_target_pairs={{0,128},{16,144},{32,160},{48,176},{64,192},{80,208},{96,224},{112... | collective-permute-start | bytes 3145736 | tf_op jit(solution)/shard_map/ppermute | solution.py:26
  226.2 2.2 copy-start.4
  228.4 1.4 copy-start.5
  229.8 1.5 copy-start.7
  232.2 25.9 %all-to-all-start.2 = ((bf16[8,288,128]{2,1,0:T(8,128)(2,1)}), bf16[8,288,128]{2,1,0:T(8,128)(2,1)}, u32[]{:S(2)}, u32[]{:S(2)}) async-start(bf16[8,288,128]{2,1,0:T(8,128)(2,1)} %bitcast.111), calls=%async_computation.2 | async-start | bytes 1179648 | tf_op jit(solution)/shard_map/all_to_all | solution.py:30
  241.8 2.6 copy-start.6
  258.1 2.2 copy-start.1
  263.4 10.9 %all-to-all-start.3 = ((f32[16,8,128]{2,1,0:T(8,128)}), f32[16,8,128]{2,1,0:T(8,128)S(1)}, u32[]{:S(2)}, u32[]{:S(2)}) async-start(f32[16,8,128]{2,1,0:T(8,128)} %broadcast_in_dim.18), calls=%async_computation.3 | async-start | bytes 131072 | tf_op jit(solution)/shard_map/all_to_all | solution.py:56
  267.0 29.0 %collective-permute-start.25 = (bf16[64,2304]{1,0:T(8,128)(2,1)S(1)}, bf16[64,2304]{1,0:T(8,128)(2,1)S(1)}, u32[]{:S(2)}, u32[]{:S(2)}) collective-permute-start(bf16[64,2304]{1,0:T(8,128)(2,1)S(1)} %fusion.20), channel_id=1, source_target_pairs={{0,128},{16,144},{32,160},{48,176},{64,192},{80,208},{96,224},{112... | collective-permute-start | bytes 884744 | tf_op jit(solution)/shard_map/ppermute | solution.py:26
  276.2 18.5 %all-to-all-start.4 = ((f32[16,8,128]{2,1,0:T(8,128)}), f32[16,8,128]{2,1,0:T(8,128)S(1)}, u32[]{:S(2)}, u32[]{:S(2)}) async-start(f32[16,8,128]{2,1,0:T(8,128)} %broadcast_in_dim.19), calls=%async_computation.4 | async-start | bytes 131072 | tf_op jit(solution)/shard_map/all_to_all | solution.py:56

commit v2 on v1

v2 whole, which is shorter than its diff:
```python
import jax
import jax.numpy as jnp
from jax import lax
from jax.experimental import pallas as pl
from jax.experimental.pallas import tpu as pltpu
from jax.sharding import PartitionSpec as P

BLK = 1152
RING = 8
SIDES = 2
TILE = 256

first_decay = 0.9
second_decay = 0.95
guard_eps = 1e-08
clip_limit = 0.2


def rings():
    return [[y * RING + z for z in range(RING)] for y in range(SIDES)]


def ring_shift(value, step):
    pairs = [(y * RING + z, y * RING + (z + step) % RING) for y in range(SIDES) for z in range(RING)]
    return lax.ppermute(value, "shard", pairs)


def cross(value):
    return lax.ppermute(value, "shard", [(s, (s + RING) % (RING * SIDES)) for s in range(RING * SIDES)])


def ring_all_to_all(value):
    return lax.all_to_all(value, "shard", 0, 0, axis_index_groups=rings())


def ring_gather(chunks, z):
    rows = chunks[0].shape[0]
    whole = jnp.zeros((len(chunks), RING * rows) + chunks[0].shape[1:], chunks[0].dtype)

    def put(whole, piece, i, place):
        return lax.dynamic_update_slice(whole, piece[None], (i, ((place + RING) % RING) * rows, 0))

    forward = list(chunks)
    backward = list(chunks)
    for i, chunk in enumerate(chunks):
        whole = put(whole, chunk, i, z)
    for step in range(1, RING // 2):
        for i in range(len(chunks)):
            forward[i] = ring_shift(forward[i], 1)
            backward[i] = ring_shift(backward[i], -1)
            whole = put(whole, forward[i], i, z - step)
            whole = put(whole, backward[i], i, z + step)
    for i in range(len(chunks)):
        far = ring_shift(forward[i], 1) if i % 2 == 0 else ring_shift(backward[i], -1)
        whole = put(whole, far, i, z + RING // 2)
    return whole


def cut_kernel(owners, left, right, *pieces):
    me = lax.axis_index("shard")
    z = lax.rem(me, RING)
    holds_right = owners[0, owners.shape[1] // 4] == me
    rows, lanes = right.shape[1:]

    @pl.when(holds_right)
    def _():
        for step, piece in enumerate(pieces):
            piece[:rows, :lanes] = right[lax.rem(z + step, RING)]

    @pl.when(jnp.logical_not(holds_right))
    def _():
        for step, piece in enumerate(pieces):
            piece[...] = left[lax.rem(z + step, RING)]


def cut_slot(owners, left, right):
    return pl.pallas_call(
        cut_kernel,
        out_shape=[jax.ShapeDtypeStruct(left.shape[1:], left.dtype)] * RING,
        in_specs=[
            pl.BlockSpec(memory_space=pltpu.SMEM),
            pl.BlockSpec(memory_space=pltpu.VMEM),
            pl.BlockSpec(memory_space=pltpu.VMEM),
        ],
        compiler_params=pltpu.CompilerParams(vmem_limit_bytes=24 * 1024 * 1024),
    )(owners, left, right)


def raw_kernel(values, blocks, mine, other, sums):
    y = lax.div(lax.axis_index("shard"), RING)
    cols = mine.shape[0]
    order = blocks.shape[1]
    step = order // 3
    total = jnp.zeros((1, 128), jnp.float32)
    for i in range(blocks.shape[0]):
        back = values[i].T
        for j in range(order // step):
            raw = lax.dot_general(
                back,
                blocks[i, j * step : (j + 1) * step, :],
                (((1,), (1,)), ((), ())),
                preferred_element_type=jnp.float32,
            )
            low = raw[:cols]
            high = raw[cols:]
            lanes = slice(i * order + j * step, i * order + (j + 1) * step)
            mine[:, lanes] = jnp.where(y == 0, low, high)
            other[:, lanes] = jnp.where(y == 0, high, low).astype(jnp.bfloat16)
            square = jnp.sum(raw * raw, 0, keepdims=True)
            for k in range(step // 128):
                total += square[:, k * 128 : (k + 1) * 128]
    sums[...] = jnp.broadcast_to(total, sums.shape)


def raw_stage(values, blocks, devices):
    count, order, pairs = values.shape
    shape = (pairs // SIDES, count * order)
    return pl.pallas_call(
        raw_kernel,
        out_shape=(
            jax.ShapeDtypeStruct(shape, jnp.float32),
            jax.ShapeDtypeStruct(shape, jnp.bfloat16),
            jax.ShapeDtypeStruct((devices, 128), jnp.float32),
        ),
        compiler_params=pltpu.CompilerParams(vmem_limit_bytes=24 * 1024 * 1024),
    )(values, blocks)


def right_kernel(values, right, second, second_out, out, scaled):
    rows = second.shape[0]
    pair = out.shape[2]
    places = values.shape[0]
    grad_left = jnp.concatenate([values[i, :, :pair] for i in range(places)], 1)
    moment_left = jnp.concatenate([values[i, :, pair:] for i in range(places)], 1)

    def turn(j, carry):
        lanes = pl.ds(pl.multiple_of(j * TILE, TILE), TILE)
        basis = right[:, lanes]
        grad_rot = jnp.dot(grad_left, basis, preferred_element_type=jnp.float32)
        moment_rot = jnp.dot(moment_left, basis, preferred_element_type=jnp.float32)
        second_new = second_decay * second[:, lanes] + (1.0 - second_decay) * grad_rot * grad_rot
        second_out[:, lanes] = second_new
        scaled[:, lanes] = (moment_rot / (jnp.sqrt(second_new) + guard_eps)).astype(jnp.bfloat16)
        return carry

    lax.fori_loop(0, second.shape[1] // TILE, turn, 0)

    def turn_back(j, carry):
        basis = right[pl.ds(pl.multiple_of(j * TILE, TILE), TILE), :]
        back = lax.dot_general(
            scaled[...], basis, (((1,), (1,)), ((), ())), preferred_element_type=jnp.float32
        ).astype(jnp.bfloat16)
        for i in range(TILE // pair):
            out[j * (TILE // pair) + i] = back[:, i * pair : (i + 1) * pair]
        return carry

    lax.fori_loop(0, right.shape[0] // TILE, turn_back, 0)


def right_stage(values, right, second):
    places, rows, pairs = values.shape
    return pl.pallas_call(
        right_kernel,
        out_shape=(
            jax.ShapeDtypeStruct(second.shape, jnp.float32),
            jax.ShapeDtypeStruct((places, rows, pairs // 2), jnp.bfloat16),
        ),
        scratch_shapes=[pltpu.VMEM(second.shape, jnp.bfloat16)],
        compiler_params=pltpu.CompilerParams(vmem_limit_bytes=24 * 1024 * 1024),
    )(values, right, second)


def body(grad, momentum, second, left_slots, right_slots, owners):
    me = lax.axis_index("shard")
    y = me // RING
    z = me % RING
    rows_all = grad.shape[1]
    cols = grad.shape[2]
    half = rows_all // SIDES
    row_part = rows_all // (RING * SIDES)
    count = half // BLK
    width = right_slots.shape[-1]
    piece = BLK // RING
    own = owners[0]
    own_y = own // RING
    own_z = own % RING
    first = y == 0

    pieces = cut_slot(
        owners,
        left_slots[0, 0].reshape(RING, piece, BLK),
        right_slots[0, 0].reshape(RING, SIDES * cols, width),
    )
    eighths = jnp.zeros((RING, piece, BLK), jnp.bfloat16)
    for step in (0, 4, 3, 5, 2, 6, 1, 7):
        part = pieces[step]
        if step:
            part = ring_shift(part, step)
        eighths = lax.dynamic_update_slice(eighths, part[None], ((z - step + RING) % RING, 0, 0))

    grad_t = grad[0].T
    moment_new = first_decay * momentum[0].T + (1.0 - first_decay) * grad_t.astype(jnp.float32)
    paired = jnp.stack([grad_t, moment_new.astype(jnp.bfloat16)])
    mine = lax.dynamic_slice_in_dim(paired, y * half, half, 2)
    other = cross(lax.dynamic_slice_in_dim(paired, (1 - y) * half, half, 2))
    eighths, other = lax.optimization_barrier((eighths, other))
    both = jnp.where(
        first, jnp.concatenate([mine, other], 1), jnp.concatenate([other, mine], 1)
    ).reshape(2 * SIDES * cols, half)
    both = jnp.stack([both[:, i * BLK : (i + 1) * BLK] for i in range(count)])

    def pick(block):
        return lax.dynamic_index_in_dim(eighths, own_z[block], 0, keepdims=False)

    side = width // SIDES
    keep_right = pick(SIDES * count)[: SIDES * cols, :width]
    give_right = lax.dynamic_slice_in_dim(keep_right, (1 - y) * side, side, 1)
    keep_right = lax.dynamic_slice_in_dim(keep_right, y * side, side, 1)
    took_right = cross(give_right)
    right_chunk = jnp.where(own_y[SIDES * count] == y, keep_right, took_right)
    took = [cross(pick((1 - y) * count + i)) for i in range(count)]
    chunk = [
        jnp.where(own_y[y * count + i] == y, pick(y * count + i), took[i]) for i in range(count)
    ]

    right_half = ring_gather([right_chunk], z)[0]
    blocks = ring_gather(chunk, z)
    right_half, blocks = lax.optimization_barrier((right_half, blocks))
    right_other = cross(right_half)
    right_all = jnp.where(
        first,
        jnp.concatenate([right_half, right_other], 1),
        jnp.concatenate([right_other, right_half], 1),
    )
    right_all = right_all.reshape(SIDES, RING, cols, width).transpose(1, 0, 2, 3)
    right_all = right_all.reshape(RING * SIDES * cols, width)

    rotated = jnp.einsum(
        "bkr,bck->brc", blocks, both, preferred_element_type=jnp.float32
    ).astype(jnp.bfloat16)
    values = ring_all_to_all(rotated.reshape(RING, row_part, 2 * SIDES * cols))
    second_new, returning = right_stage(values, right_all, second[0])
    values = ring_all_to_all(returning).reshape(count, BLK, SIDES * cols)
    devices = lax.axis_size("shard") * lax.axis_size("layer")
    raw_mine, raw_give, sums = raw_stage(values, blocks, devices)
    raw_other = cross(raw_give).astype(jnp.float32)
    total = jnp.sum(lax.all_to_all(sums, ("shard", "layer"), 0, 0))
    cells = lax.axis_size("layer") * grad.shape[0] * rows_all * cols * RING * SIDES
    factor = jnp.minimum(1.0, clip_limit / jnp.sqrt(total / cells + 1e-06))
    direction = jnp.where(
        first,
        jnp.concatenate([raw_mine, raw_other], 1),
        jnp.concatenate([raw_other, raw_mine], 1),
    )
    direction = (factor * direction).astype(jnp.bfloat16)
    return (moment_new.T[None], second_new[None], direction.T[None])


def solution(mesh):
    placed = (
        P("layer", None, "shard"),
        P("layer", None, "shard"),
        P("layer", "shard", None),
        P("layer", "shard", None, None),
        P("layer", "shard", None, None),
        P("layer", None),
    )
    return jax.shard_map(
        body,
        mesh=mesh,
        in_specs=placed,
        out_specs=(P("layer", None, "shard"), P("layer", "shard", None), P("layer", None, "shard")),
        check_vma=False,
    )
```

time: 298 us -> 253 us (0.85)
  waiting for transfers between devices: 161 us -> 120 us
  other arithmetic: 25.9 us -> 8.52 us
  blocking collectives: 0 us -> 16.4 us
  local copies, waits for them, and re-layouts: 24.3 us -> 16.9 us
  Pallas kernels: 0 us -> 6.72 us
  matrix products: 6.35 us -> 3.34 us
    all_to_all x3 -> x1, waiting for transfers between devices: 64.5 us -> 7.33 us  [ring_all_to_all(): return lax.all_to_all(value, 'shard', 0, 0, axis_index_groups=rings())]
    ppermute x21 -> x28, starting transfers between devices: 19.7 us -> 43.5 us  [ring_shift(): return lax.ppermute(value, 'shard', pairs)]
    all_to_all x3 -> x1, starting transfers between devices: 23.5 us -> 4.61 us  [ring_all_to_all(): return lax.all_to_all(value, 'shard', 0, 0, axis_index_groups=rings())]
    all_to_all x0 -> x1, blocking collectives: none -> 16.4 us  [ring_all_to_all(): return lax.all_to_all(value, 'shard', 0, 0, axis_index_groups=rings())]
    ppermute x21 -> x28, waiting for transfers between devices: 64.1 us -> 74.4 us  [ring_shift(): return lax.ppermute(value, 'shard', pairs)]
    select_n x2 -> x0, other arithmetic: 8.15 us -> none  [the longest x1 4.23 us: body(): jnp.where(first, jnp.stack([right_half, right_other], 1), jnp.stack([righ...]
    ppermute x5 -> x6, waiting for transfers between devices: 19.4 us -> 27 us  [cross(): lax.ppermute(value, 'shard', [(s, (s + RING) % (RING * SIDES)) for s in r...]
    pallas_call x0 -> x2, Pallas kernels: none -> 6.72 us  [the longest x1 4.38 us: right_stage(): pl.pallas_call(right_kernel, out_shape=(jax.ShapeDtypeStruct(second.shape...]
  transfers between devices with their start and end apart: 31 -> 36, of which waited for: 18 -> 18; matrix products, arithmetic and copies ran while one was open for 11% -> 6% of each run, Pallas kernels for 0% -> 0%
where the time goes in v2:
time: 253 us; the launch traced here: 252 us
  waiting for transfers between devices  120 us (47%)
  starting transfers between devices  66.8 us (26%)
  local copies, waits for them, and re-layouts  16.9 us (7%)
  blocking collectives  16.4 us (6%)
  between operations  13.2 us (5%)
  other arithmetic  8.52 us (3%)
  Pallas kernels  6.72 us (3%)
  matrix products  3.34 us (1%)
    ppermute x28, waiting for transfers between devices, ring_shift(): return lax.ppermute(value, 'shard', pairs)  74.4 us
    ppermute x28, starting transfers between devices, ring_shift(): return lax.ppermute(value, 'shard', pairs)  43.5 us
    ppermute x6, waiting for transfers between devices, cross(): lax.ppermute(value, 'shard', [(s, (s + RING) % (RING * SIDES)) for s in r...  27 us
    all_to_all x1, blocking collectives, ring_all_to_all(): return lax.all_to_all(value, 'shard', 0, 0, axis_index_groups=rings())  16.4 us
    all_to_all x1, starting transfers between devices, body(): total = jnp.sum(lax.all_to_all(sums, ('shard', 'layer'), 0, 0))  13.1 us
    all_to_all x1, waiting for transfers between devices, body(): total = jnp.sum(lax.all_to_all(sums, ('shard', 'layer'), 0, 0))  11.8 us
    all_to_all x1, waiting for transfers between devices, ring_all_to_all(): return lax.all_to_all(value, 'shard', 0, 0, axis_index_groups=rings())  7.33 us
    ppermute x6, starting transfers between devices, cross(): lax.ppermute(value, 'shard', [(s, (s + RING) % (RING * SIDES)) for s in r...  5.63 us
  transfers between devices with their start and end apart: 36, of which 18 were waited for; matrix products, arithmetic and copies ran while one was open for 6% of the time, Pallas kernels for 0%

profile of v2, /device:TPU:1, one launch (start us, length us, event | category | flops | bytes accessed | tf_op | source)
XLA Modules:
  0.0 252.4 jit_solution(4765493137502320985)
XLA Ops:
  0.9 0.4 copy-done.9
  1.3 1.1 copy-done.6
  2.4 3.3 %shard_map.87 = (bf16[8,144,1152]{2,1,0:T(8,128)(2,1)S(1)}, bf16[144,1152]{1,0:T(8,128)(2,1)}, bf16[144,1152]{1,0:T(8,128)(2,1)}, bf16[144,1152]{1,0:T(8,128)(2,...) fusion(bf16[8,144,1152]{2,1,0:T(8,128)(2,1)S(1)} %broadcast_in_, ...), kind=kCustom, calls=%fused_computation.48 | custom fusion | bytes 7406084 | tf_op jit(solution)/shard_map/pallas_call | solution.py:77
  5.7 7.7 %collective-permute-start = (bf16[144,1152]{1,0:T(8,128)(2,1)}, bf16[144,1152]{1,0:T(8,128)(2,1)}, u32[]{:S(2)}, u32[]{:S(2)}) collective-permute-start(bf16[144,1152]{1,0:T(8,128)(2,1)} %get-tuple-element.40), channel_id=1, source_target_pairs={{0,64},{16,80},{32,96},{48,112},{64,0},{80,16},{96,32},{112,48},{1... | collective-permute-start | bytes 995336 | tf_op jit(solution)/shard_map/ppermute | solution.py:25
  13.4 1.6 collective-permute-start.1
  15.1 2.8 %collective-permute-start.2 = (bf16[144,1152]{1,0:T(8,128)(2,1)}, bf16[144,1152]{1,0:T(8,128)(2,1)}, u32[]{:S(2)}, u32[]{:S(2)}) collective-permute-start(bf16[144,1152]{1,0:T(8,128)(2,1)} %get-tuple-element.44), channel_id=1, source_target_pairs={{0,80},{16,96},{32,112},{48,0},{64,16},{80,32},{96,48},{112,64},{1... | collective-permute-start | bytes 995336 | tf_op jit(solution)/shard_map/ppermute | solution.py:25
  17.9 1.2 collective-permute-start.3
  19.1 2.4 collective-permute-start.4
  21.5 0.7 fusion.21
  24.8 2.3 fusion.7
  28.4 2.0 fusion.9
  30.4 0.7 collective-permute-start.5
  31.1 1.0 bitcast_dynamic-update-slice_fusion.22
  32.1 22.3 %collective-permute-done.1 = bf16[144,1152]{1,0:T(8,128)(2,1)} collective-permute-done((bf16[144,1152]{1,0:T(8,128)(2,1)}, bf16[144,1152]{1,0:T(8,128)(2,1)}, u32[]{:S(2)}, u32[]{:S(2)}) %collective-permute-start.1) | collective-permute-done | bytes 331808 | tf_op jit(solution)/shard_map/ppermute | solution.py:25
  54.4 1.0 bitcast_dynamic-update-slice_fusion.21
  55.4 1.2 collective-permute-start.7
  56.7 1.0 bitcast_dynamic-update-slice_fusion.20
  57.7 1.0 bitcast_dynamic-update-slice_fusion.19
  58.7 6.4 %collective-permute-done.4 = bf16[144,1152]{1,0:T(8,128)(2,1)} collective-permute-done((bf16[144,1152]{1,0:T(8,128)(2,1)}, bf16[144,1152]{1,0:T(8,128)(2,1)}, u32[]{:S(2)}, u32[]{:S(2)}) %collective-permute-start.4) | collective-permute-done | bytes 331808 | tf_op jit(solution)/shard_map/ppermute | solution.py:25
  65.1 1.0 bitcast_dynamic-update-slice_fusion.18
  66.1 4.9 %collective-permute-done.5 = bf16[144,1152]{1,0:T(8,128)(2,1)S(1)} collective-permute-done((bf16[144,1152]{1,0:T(8,128)(2,1)}, bf16[144,1152]{1,0:T(8,128)(2,1)S(1)}, u32[]{:S(2)}, u32[]{:S(2)}) %collective-permute-start.5) | collective-permute-done | bytes 331808 | tf_op jit(solution)/shard_map/ppermute | solution.py:25
  71.0 0.4 collective-permute-done.6
  71.4 0.9 dynamic-slice_bitcast_fusion
  72.3 1.3 collective-permute-start.16
  81.9 7.0 %collective-permute-done.17 = bf16[144,1152]{1,0:T(8,128)(2,1)S(1)} collective-permute-done((bf16[144,1152]{1,0:T(8,128)(2,1)}, bf16[144,1152]{1,0:T(8,128)(2,1)S(1)}, u32[]{:S(2)}, u32[]{:S(2)}) %collective-permute-start.17) | collective-permute-done | bytes 331808 | tf_op jit(solution)/shard_map/ppermute | solution.py:29
  89.6 2.2 collective-permute-start.18
  91.8 1.2 collective-permute-done.8
  93.1 2.2 collective-permute-start.9
  95.3 2.6 %collective-permute-start.10 = (bf16[128,512]{1,0:T(8,128)(2,1)S(1)}, bf16[128,512]{1,0:T(8,128)(2,1)S(1)}, u32[]{:S(2)}, u32[]{:S(2)}) collective-permute-start(bf16[128,512]{1,0:T(8,128)(2,1)S(1)} %get-tuple-element.58), channel_id=1, source_target_pairs={{0,112},{16,0},{32,16},{48,32},{64,48},{80,64},{96,80},{112,96},{1... | collective-permute-start | bytes 393224 | tf_op jit(solution)/shard_map/ppermute | solution.py:25
  98.0 1.3 collective-permute-start.19
  99.5 3.5 %collective-permute-done.9 = bf16[128,512]{1,0:T(8,128)(2,1)S(1)} collective-permute-done((bf16[128,512]{1,0:T(8,128)(2,1)S(1)}, bf16[128,512]{1,0:T(8,128)(2,1)S(1)}, u32[]{:S(2)}, u32[]{:S(2)}) %collective-permute-start.9) | collective-permute-done | bytes 131104 | tf_op jit(solution)/shard_map/ppermute | solution.py:25
  103.1 1.2 collective-permute-start.21
  104.7 2.5 collective-permute-start.12
  107.3 3.0 %collective-permute-done.20 = bf16[144,1152]{1,0:T(8,128)(2,1)S(1)} collective-permute-done((bf16[144,1152]{1,0:T(8,128)(2,1)S(1)}, bf16[144,1152]{1,0:T(8,128)(2,1)S(1)}, u32[]{:S(2)}, u32[]{:S(2)}) %collective-permute-start.20) | collective-permute-done | bytes 331808 | tf_op jit(solution)/shard_map/ppermute | solution.py:25
  110.3 1.1 collective-permute-start.23
  111.4 2.8 %collective-permute-done.21 = bf16[144,1152]{1,0:T(8,128)(2,1)S(1)} collective-permute-done((bf16[144,1152]{1,0:T(8,128)(2,1)S(1)}, bf16[144,1152]{1,0:T(8,128)(2,1)S(1)}, u32[]{:S(2)}, u32[]{:S(2)}) %collective-permute-start.21) | collective-permute-done | bytes 331808 | tf_op jit(solution)/shard_map/ppermute | solution.py:25
  114.4 2.7 %collective-permute-done.12 = bf16[128,512]{1,0:T(8,128)(2,1)S(1)} collective-permute-done((bf16[128,512]{1,0:T(8,128)(2,1)S(1)}, bf16[128,512]{1,0:T(8,128)(2,1)S(1)}, u32[]{:S(2)}, u32[]{:S(2)}) %collective-permute-start.12) | collective-permute-done | bytes 131104 | tf_op jit(solution)/shard_map/ppermute | solution.py:25
  117.0 1.3 collective-permute-start.14
  118.4 11.2 %collective-permute-done.13 = bf16[128,512]{1,0:T(8,128)(2,1)S(1)} collective-permute-done((bf16[128,512]{1,0:T(8,128)(2,1)S(1)}, bf16[128,512]{1,0:T(8,128)(2,1)S(1)}, u32[]{:S(2)}, u32[]{:S(2)}) %collective-permute-start.13) | collective-permute-done | bytes 131104 | tf_op jit(solution)/shard_map/ppermute | solution.py:25
  129.6 2.7 %collective-permute-start.25 = (bf16[144,1152]{1,0:T(8,128)(2,1)S(1)}, bf16[144,1152]{1,0:T(8,128)(2,1)S(1)}, u32[]{:S(2)}, u32[]{:S(2)}) collective-permute-start(bf16[144,1152]{1,0:T(8,128)(2,1)S(1)} %collective-permute-done.21), channel_id=1, source_target_pairs={{0,112},{16,0},{32,16},{48,32},{64,48},{80,64},{96,80},{112,96},{1... | collective-permute-start | bytes 995336 | tf_op jit(solution)/shard_map/ppermute | solution.py:25
  132.3 2.2 collective-permute-done.15
  134.7 2.7 %collective-permute-start.27 = (bf16[144,1152]{1,0:T(8,128)(2,1)S(1)}, bf16[144,1152]{1,0:T(8,128)(2,1)S(1)}, u32[]{:S(2)}, u32[]{:S(2)}) collective-permute-start(bf16[144,1152]{1,0:T(8,128)(2,1)S(1)} %collective-permute-done.23), channel_id=1, source_target_pairs={{0,112},{16,0},{32,16},{48,32},{64,48},{80,64},{96,80},{112,96},{1... | collective-permute-start | bytes 995336 | tf_op jit(solution)/shard_map/ppermute | solution.py:25
  137.5 3.0 %collective-permute-start.29 = (bf16[144,1152]{1,0:T(8,128)(2,1)S(1)}, bf16[144,1152]{1,0:T(8,128)(2,1)S(1)}, u32[]{:S(2)}, u32[]{:S(2)}) collective-permute-start(bf16[144,1152]{1,0:T(8,128)(2,1)S(1)} %collective-permute-done.25), channel_id=1, source_target_pairs={{0,112},{16,0},{32,16},{48,32},{64,48},{80,64},{96,80},{112,96},{1... | collective-permute-start | bytes 995336 | tf_op jit(solution)/shard_map/ppermute | solution.py:25
  140.5 1.3 collective-permute-done.26
  141.8 9.9 %collective-permute-done.29 = bf16[144,1152]{1,0:T(8,128)(2,1)S(1)} collective-permute-done((bf16[144,1152]{1,0:T(8,128)(2,1)S(1)}, bf16[144,1152]{1,0:T(8,128)(2,1)S(1)}, u32[]{:S(2)}, u32[]{:S(2)}) %collective-permute-start.29) | collective-permute-done | bytes 331808 | tf_op jit(solution)/shard_map/ppermute | solution.py:25
  151.7 3.4 %collective-permute-start.31 = (bf16[144,1152]{1,0:T(8,128)(2,1)S(1)}, bf16[144,1152]{1,0:T(8,128)(2,1)S(1)}, u32[]{:S(2)}, u32[]{:S(2)}) collective-permute-start(bf16[144,1152]{1,0:T(8,128)(2,1)S(1)} %collective-permute-done.29), channel_id=1, source_target_pairs={{0,112},{16,0},{32,16},{48,32},{64,48},{80,64},{96,80},{112,96},{1... | collective-permute-start | bytes 995336 | tf_op jit(solution)/shard_map/ppermute | solution.py:25
  155.4 3.8 %collective-permute-done.31 = bf16[144,1152]{1,0:T(8,128)(2,1)S(1)} collective-permute-done((bf16[144,1152]{1,0:T(8,128)(2,1)S(1)}, bf16[144,1152]{1,0:T(8,128)(2,1)S(1)}, u32[]{:S(2)}, u32[]{:S(2)}) %collective-permute-start.31) | collective-permute-done | bytes 331808 | tf_op jit(solution)/shard_map/ppermute | solution.py:25
  159.2 3.3 %convolution_convert_fusion = bf16[2,1152,256]{2,1,0:T(8,128)(2,1)} fusion(bf16[2,1152,1152]{2,1,0:T(8,128)(2,1)S(1)} %bitcast_dynamic-update-slice_fusion.blocks, bf16[1,256,1152]{2,1,0:T(8,128)(2,1)S(1)} %get-tuple-element.63, bf16[1,256,1152]{2,1,0:T(8,128)(2,1)S(1)} %get-tuple-element.62), kind=kOutput, calls=%fused_computation | convolution fusion | flops 1360134144 | bytes 7667712 | tf_op jit(solution)/shard_map/bkr,bck->brc/dot_general | solution.py:238
  162.6 4.6 %all-to-all-start = ((bf16[8,288,256]{2,1,0:T(8,128)(2,1)}), bf16[8,288,256]{2,1,0:T(8,128)(2,1)S(1)}, u32[]{:S(2)}, u32[]{:S(2)}) async-start(bf16[8,288,256]{2,1,0:T(8,128)(2,1)} %bitcast.131), calls=%async_computation | async-start | bytes 2359296 | tf_op jit(solution)/shard_map/all_to_all | solution.py:33
  167.2 1.3 collective-permute-start.32
  168.5 18.8 %collective-permute-done.32 = bf16[1024,512]{1,0:T(8,128)(2,1)S(1)} collective-permute-done((bf16[1024,512]{1,0:T(8,128)(2,1)S(1)}, bf16[1024,512]{1,0:T(8,128)(2,1)S(1)}, u32[]{:S(2)}, u32[]{:S(2)}) %collective-permute-start.32) | collective-permute-done | bytes 1048608 | tf_op jit(solution)/shard_map/ppermute | solution.py:29
  187.3 0.7 fusion
  188.2 7.3 %all-to-all-done.values = bf16[8,288,256]{2,1,0:T(8,128)(2,1)S(1)} async-done(((bf16[8,288,256]{2,1,0:T(8,128)(2,1)}), bf16[8,288,256]{2,1,0:T(8,128)(2,1)S(1)}, u32[]{:S(2)}, u32[]{:S(2)}) %all-to-all-start) | async-done | bytes 1179680 | tf_op jit(solution)/shard_map/all_to_all | solution.py:33
  195.5 1.3 copy-done.2
  196.8 4.4 %shard_map.85 = (f32[288,1024]{1,0:T(8,128)}, bf16[8,288,128]{2,1,0:T(8,128)(2,1)S(1)}) custom-call(bf16[8,288,256]{2,1,0:T(8,128)(2,1)S(1)} %all-to-all-done.values, bf16[1024,1024]{1,0:T(8,128)(2,1)S(1)} %bitcast.123, f32[288,1024]{1,0:T(8,128)S(1)} %bitcast.125), custom_call_target="tpu_custom_call" | custom-call | tf_op jit(solution)/shard_map/pallas_call | solution.py:162
  201.1 16.4 %all_to_all.19 = bf16[8,288,128]{2,1,0:T(8,128)(2,1)S(1)} all-to-all(bf16[8,288,128]{2,1,0:T(8,128)(2,1)S(1)} %get-tuple-element.33), channel_id=1, replica_groups={{0,16,32,48,64,80,96,112},{128,144,160,176,192,208,224,240},{1,17,33,49..., dimensions={0} | all-to-all | bytes 1179648 | tf_op jit(solution)/shard_map/all_to_all | solution.py:33
  217.6 2.5 copy-done.1
  220.1 2.3 shard_map.86
  222.4 1.3 collective-permute-start.33
  223.7 13.1 %all-to-all-start.2 = ((f32[256,1,128]{2,1,0:T(1,128)}), f32[256,1,128]{2,1,0:T(1,128)S(1)}, u32[]{:S(2)}, u32[]{:S(2)}) async-start(f32[256,1,128]{2,1,0:T(1,128)} %bitcast.59), calls=%async_computation.2 | async-start | bytes 262144 | tf_op jit(solution)/shard_map/all_to_all | solution.py:247
  236.8 1.2 multiply_add_fusion
  238.0 11.8 %all-to-all-done.2 = f32[256,1,128]{2,1,0:T(1,128)S(1)} async-done(((f32[256,1,128]{2,1,0:T(1,128)}), f32[256,1,128]{2,1,0:T(1,128)S(1)}, u32[]{:S(2)}, u32[]{:S(2)}) %all-to-all-start.2) | async-done | bytes 131104 | tf_op jit(solution)/shard_map/all_to_all | solution.py:247
  249.8 0.9 reduce_sum.9
  251.4 1.0 fusion.8
  (82 shorter events, 3.7 us)
Async XLA Ops:
  0.6 0.7 copy-start.9
  0.7 1.8 copy-start.6
  2.4 22.4 %copy-start.3 = (bf16[1,4608,64]{1,2,0:T(8,128)(2,1)S(1)}, bf16[1,4608,64]{1,2,0:T(8,128)(2,1)}, u32[]{:S(2)}) copy-start(bf16[1,4608,64]{1,2,0:T(8,128)(2,1)} %param.6) | copy-start | bytes 1769476
  5.7 24.7 %collective-permute-start = (bf16[144,1152]{1,0:T(8,128)(2,1)}, bf16[144,1152]{1,0:T(8,128)(2,1)}, u32[]{:S(2)}, u32[]{:S(2)}) collective-permute-start(bf16[144,1152]{1,0:T(8,128)(2,1)} %get-tuple-element.40), channel_id=1, source_target_pairs={{0,64},{16,80},{32,96},{48,112},{64,0},{80,16},{96,32},{112,48},{1... | collective-permute-start | bytes 995336 | tf_op jit(solution)/shard_map/ppermute | solution.py:25
  13.4 41.0 %collective-permute-start.1 = (bf16[144,1152]{1,0:T(8,128)(2,1)}, bf16[144,1152]{1,0:T(8,128)(2,1)}, u32[]{:S(2)}, u32[]{:S(2)}) collective-permute-start(bf16[144,1152]{1,0:T(8,128)(2,1)} %get-tuple-element.42), channel_id=1, source_target_pairs={{0,48},{16,64},{32,80},{48,96},{64,112},{80,0},{96,16},{112,32},{1... | collective-permute-start | bytes 995336 | tf_op jit(solution)/shard_map/ppermute | solution.py:25
  15.1 40.3 %collective-permute-start.2 = (bf16[144,1152]{1,0:T(8,128)(2,1)}, bf16[144,1152]{1,0:T(8,128)(2,1)}, u32[]{:S(2)}, u32[]{:S(2)}) collective-permute-start(bf16[144,1152]{1,0:T(8,128)(2,1)} %get-tuple-element.44), channel_id=1, source_target_pairs={{0,80},{16,96},{32,112},{48,0},{64,16},{80,32},{96,48},{112,64},{1... | collective-permute-start | bytes 995336 | tf_op jit(solution)/shard_map/ppermute | solution.py:25
  17.9 39.8 %collective-permute-start.3 = (bf16[144,1152]{1,0:T(8,128)(2,1)}, bf16[144,1152]{1,0:T(8,128)(2,1)}, u32[]{:S(2)}, u32[]{:S(2)}) collective-permute-start(bf16[144,1152]{1,0:T(8,128)(2,1)} %get-tuple-element.46), channel_id=1, source_target_pairs={{0,32},{16,48},{32,64},{48,80},{64,96},{80,112},{96,0},{112,16},{1... | collective-permute-start | bytes 995336 | tf_op jit(solution)/shard_map/ppermute | solution.py:25
  19.1 46.0 %collective-permute-start.4 = (bf16[144,1152]{1,0:T(8,128)(2,1)}, bf16[144,1152]{1,0:T(8,128)(2,1)}, u32[]{:S(2)}, u32[]{:S(2)}) collective-permute-start(bf16[144,1152]{1,0:T(8,128)(2,1)} %get-tuple-element.48), channel_id=1, source_target_pairs={{0,96},{16,112},{32,0},{48,16},{64,32},{80,48},{96,64},{112,80},{1... | collective-permute-start | bytes 995336 | tf_op jit(solution)/shard_map/ppermute | solution.py:25
  28.4 26.0 %copy-start.8 = (bf16[144,1152]{1,0:T(8,128)(2,1)S(1)}, bf16[144,1152]{1,0:T(8,128)(2,1)}, u32[]{:S(2)}) copy-start(bf16[144,1152]{1,0:T(8,128)(2,1)} %get-tuple-element.52) | copy-start | bytes 995332
  30.4 40.6 %collective-permute-start.5 = (bf16[144,1152]{1,0:T(8,128)(2,1)}, bf16[144,1152]{1,0:T(8,128)(2,1)S(1)}, u32[]{:S(2)}, u32[]{:S(2)}) collective-permute-start(bf16[144,1152]{1,0:T(8,128)(2,1)} %get-tuple-element.50), channel_id=1, source_target_pairs={{0,16},{16,32},{32,48},{48,64},{64,80},{80,96},{96,112},{112,0},{1... | collective-permute-start | bytes 995336 | tf_op jit(solution)/shard_map/ppermute | solution.py:25
  54.4 17.0 %collective-permute-start.6 = (bf16[144,1152]{1,0:T(8,128)(2,1)S(1)}, bf16[144,1152]{1,0:T(8,128)(2,1)S(1)}, u32[]{:S(2)}, u32[]{:S(2)}) collective-permute-start(bf16[144,1152]{1,0:T(8,128)(2,1)S(1)} %copy-done.8), channel_id=1, source_target_pairs={{0,112},{16,0},{32,16},{48,32},{64,48},{80,64},{96,80},{112,96},{1... | collective-permute-start | bytes 995336 | tf_op jit(solution)/shard_map/ppermute | solution.py:25
  55.4 16.0 %collective-permute-start.7 = (bf16[2,64,2304]{2,1,0:T(8,128)(2,1)S(1)}, bf16[2,64,2304]{2,1,0:T(8,128)(2,1)S(1)}, u32[]{:S(2)}, u32[]{:S(2)}) collective-permute-start(bf16[2,64,2304]{2,1,0:T(8,128)(2,1)S(1)} %get-tuple-element.65), channel_id=1, source_target_pairs={{0,128},{16,144},{32,160},{48,176},{64,192},{80,208},{96,224},{112... | collective-permute-start | bytes 1769480 | tf_op jit(solution)/shard_map/ppermute | solution.py:29
  72.3 9.0 %collective-permute-start.16 = (bf16[144,1152]{1,0:T(8,128)(2,1)}, bf16[144,1152]{1,0:T(8,128)(2,1)}, u32[]{:S(2)}, u32[]{:S(2)}) collective-permute-start(bf16[144,1152]{1,0:T(8,128)(2,1)} %get-tuple-element.61), channel_id=1, source_target_pairs={{0,128},{16,144},{32,160},{48,176},{64,192},{80,208},{96,224},{112... | collective-permute-start | bytes 995336 | tf_op jit(solution)/shard_map/ppermute | solution.py:29
  81.1 7.8 %collective-permute-start.17 = (bf16[144,1152]{1,0:T(8,128)(2,1)}, bf16[144,1152]{1,0:T(8,128)(2,1)S(1)}, u32[]{:S(2)}, u32[]{:S(2)}) collective-permute-start(bf16[144,1152]{1,0:T(8,128)(2,1)} %get-tuple-element.60), channel_id=1, source_target_pairs={{0,128},{16,144},{32,160},{48,176},{64,192},{80,208},{96,224},{112... | collective-permute-start | bytes 995336 | tf_op jit(solution)/shard_map/ppermute | solution.py:29
  81.8 7.6 %copy-start.7 = (bf16[2,64,2304]{2,1,0:T(8,128)(2,1)S(1)}, bf16[2,64,2304]{2,1,0:T(8,128)(2,1)}, u32[]{:S(2)}) copy-start(bf16[2,64,2304]{2,1,0:T(8,128)(2,1)} %get-tuple-element.64) | copy-start | bytes 1769476
  89.1 3.9 %collective-permute-start.8 = (bf16[128,512]{1,0:T(8,128)(2,1)S(1)}, bf16[128,512]{1,0:T(8,128)(2,1)S(1)}, u32[]{:S(2)}, u32[]{:S(2)}) collective-permute-start(bf16[128,512]{1,0:T(8,128)(2,1)S(1)} %constant_dynamic-slice_fusion), channel_id=1, source_target_pairs={{0,128},{16,144},{32,160},{48,176},{64,192},{80,208},{96,224},{112... | collective-permute-start | bytes 393224 | tf_op jit(solution)/shard_map/ppermute | solution.py:29
  89.6 15.1 %collective-permute-start.18 = (bf16[144,1152]{1,0:T(8,128)(2,1)S(1)}, bf16[144,1152]{1,0:T(8,128)(2,1)S(1)}, u32[]{:S(2)}, u32[]{:S(2)}) collective-permute-start(bf16[144,1152]{1,0:T(8,128)(2,1)S(1)} %get-tuple-element.56), channel_id=1, source_target_pairs={{0,16},{16,32},{32,48},{48,64},{64,80},{80,96},{96,112},{112,0},{1... | collective-permute-start | bytes 995336 | tf_op jit(solution)/shard_map/ppermute | solution.py:25
  93.1 10.0 %collective-permute-start.9 = (bf16[128,512]{1,0:T(8,128)(2,1)S(1)}, bf16[128,512]{1,0:T(8,128)(2,1)S(1)}, u32[]{:S(2)}, u32[]{:S(2)}) collective-permute-start(bf16[128,512]{1,0:T(8,128)(2,1)S(1)} %get-tuple-element.58), channel_id=1, source_target_pairs={{0,16},{16,32},{32,48},{48,64},{64,80},{80,96},{96,112},{112,0},{1... | collective-permute-start | bytes 393224 | tf_op jit(solution)/shard_map/ppermute | solution.py:25
  95.3 9.0 %collective-permute-start.10 = (bf16[128,512]{1,0:T(8,128)(2,1)S(1)}, bf16[128,512]{1,0:T(8,128)(2,1)S(1)}, u32[]{:S(2)}, u32[]{:S(2)}) collective-permute-start(bf16[128,512]{1,0:T(8,128)(2,1)S(1)} %get-tuple-element.58), channel_id=1, source_target_pairs={{0,112},{16,0},{32,16},{48,32},{64,48},{80,64},{96,80},{112,96},{1... | collective-permute-start | bytes 393224 | tf_op jit(solution)/shard_map/ppermute | solution.py:25
  98.0 9.2 %collective-permute-start.19 = (bf16[144,1152]{1,0:T(8,128)(2,1)S(1)}, bf16[144,1152]{1,0:T(8,128)(2,1)S(1)}, u32[]{:S(2)}, u32[]{:S(2)}) collective-permute-start(bf16[144,1152]{1,0:T(8,128)(2,1)S(1)} %get-tuple-element.56), channel_id=1, source_target_pairs={{0,112},{16,0},{32,16},{48,32},{64,48},{80,64},{96,80},{112,96},{1... | collective-permute-start | bytes 995336 | tf_op jit(solution)/shard_map/ppermute | solution.py:25
  99.3 11.0 %collective-permute-start.20 = (bf16[144,1152]{1,0:T(8,128)(2,1)S(1)}, bf16[144,1152]{1,0:T(8,128)(2,1)S(1)}, u32[]{:S(2)}, u32[]{:S(2)}) collective-permute-start(bf16[144,1152]{1,0:T(8,128)(2,1)S(1)} %get-tuple-element.54), channel_id=1, source_target_pairs={{0,16},{16,32},{32,48},{48,64},{64,80},{80,96},{96,112},{112,0},{1... | collective-permute-start | bytes 995336 | tf_op jit(solution)/shard_map/ppermute | solution.py:25
  103.1 11.2 %collective-permute-start.21 = (bf16[144,1152]{1,0:T(8,128)(2,1)S(1)}, bf16[144,1152]{1,0:T(8,128)(2,1)S(1)}, u32[]{:S(2)}, u32[]{:S(2)}) collective-permute-start(bf16[144,1152]{1,0:T(8,128)(2,1)S(1)} %get-tuple-element.54), channel_id=1, source_target_pairs={{0,112},{16,0},{32,16},{48,32},{64,48},{80,64},{96,80},{112,96},{1... | collective-permute-start | bytes 995336 | tf_op jit(solution)/shard_map/ppermute | solution.py:25
  104.3 10.0 %collective-permute-start.11 = (bf16[128,512]{1,0:T(8,128)(2,1)S(1)}, bf16[128,512]{1,0:T(8,128)(2,1)S(1)}, u32[]{:S(2)}, u32[]{:S(2)}) collective-permute-start(bf16[128,512]{1,0:T(8,128)(2,1)S(1)} %collective-permute-done.9), channel_id=1, source_target_pairs={{0,16},{16,32},{32,48},{48,64},{64,80},{80,96},{96,112},{112,0},{1... | collective-permute-start | bytes 393224 | tf_op jit(solution)/shard_map/ppermute | solution.py:25
  104.7 12.4 %collective-permute-start.12 = (bf16[128,512]{1,0:T(8,128)(2,1)S(1)}, bf16[128,512]{1,0:T(8,128)(2,1)S(1)}, u32[]{:S(2)}, u32[]{:S(2)}) collective-permute-start(bf16[128,512]{1,0:T(8,128)(2,1)S(1)} %collective-permute-done.10), channel_id=1, source_target_pairs={{0,112},{16,0},{32,16},{48,32},{64,48},{80,64},{96,80},{112,96},{1... | collective-permute-start | bytes 393224 | tf_op jit(solution)/shard_map/ppermute | solution.py:25
  107.2 27.4 %collective-permute-start.22 = (bf16[144,1152]{1,0:T(8,128)(2,1)S(1)}, bf16[144,1152]{1,0:T(8,128)(2,1)S(1)}, u32[]{:S(2)}, u32[]{:S(2)}) collective-permute-start(bf16[144,1152]{1,0:T(8,128)(2,1)S(1)} %collective-permute-done.18), channel_id=1, source_target_pairs={{0,16},{16,32},{32,48},{48,64},{64,80},{80,96},{96,112},{112,0},{1... | collective-permute-start | bytes 995336 | tf_op jit(solution)/shard_map/ppermute | solution.py:25
  110.3 24.4 %collective-permute-start.23 = (bf16[144,1152]{1,0:T(8,128)(2,1)S(1)}, bf16[144,1152]{1,0:T(8,128)(2,1)S(1)}, u32[]{:S(2)}, u32[]{:S(2)}) collective-permute-start(bf16[144,1152]{1,0:T(8,128)(2,1)S(1)} %collective-permute-done.19), channel_id=1, source_target_pairs={{0,112},{16,0},{32,16},{48,32},{64,48},{80,64},{96,80},{112,96},{1... | collective-permute-start | bytes 995336 | tf_op jit(solution)/shard_map/ppermute | solution.py:25
  114.2 23.1 %collective-permute-start.24 = (bf16[144,1152]{1,0:T(8,128)(2,1)S(1)}, bf16[144,1152]{1,0:T(8,128)(2,1)S(1)}, u32[]{:S(2)}, u32[]{:S(2)}) collective-permute-start(bf16[144,1152]{1,0:T(8,128)(2,1)S(1)} %collective-permute-done.20), channel_id=1, source_target_pairs={{0,16},{16,32},{32,48},{48,64},{64,80},{80,96},{96,112},{112,0},{1... | collective-permute-start | bytes 995336 | tf_op jit(solution)/shard_map/ppermute | solution.py:25
  114.3 15.2 %collective-permute-start.13 = (bf16[128,512]{1,0:T(8,128)(2,1)S(1)}, bf16[128,512]{1,0:T(8,128)(2,1)S(1)}, u32[]{:S(2)}, u32[]{:S(2)}) collective-permute-start(bf16[128,512]{1,0:T(8,128)(2,1)S(1)} %collective-permute-done.11), channel_id=1, source_target_pairs={{0,16},{16,32},{32,48},{48,64},{64,80},{80,96},{96,112},{112,0},{1... | collective-permute-start | bytes 393224 | tf_op jit(solution)/shard_map/ppermute | solution.py:25
  117.0 12.5 %collective-permute-start.14 = (bf16[128,512]{1,0:T(8,128)(2,1)S(1)}, bf16[128,512]{1,0:T(8,128)(2,1)S(1)}, u32[]{:S(2)}, u32[]{:S(2)}) collective-permute-start(bf16[128,512]{1,0:T(8,128)(2,1)S(1)} %collective-permute-done.12), channel_id=1, source_target_pairs={{0,112},{16,0},{32,16},{48,32},{64,48},{80,64},{96,80},{112,96},{1... | collective-permute-start | bytes 393224 | tf_op jit(solution)/shard_map/ppermute | solution.py:25
  129.5 5.0 %collective-permute-start.15 = (bf16[128,512]{1,0:T(8,128)(2,1)S(1)}, bf16[128,512]{1,0:T(8,128)(2,1)S(1)}, u32[]{:S(2)}, u32[]{:S(2)}) collective-permute-start(bf16[128,512]{1,0:T(8,128)(2,1)S(1)} %collective-permute-done.13), channel_id=1, source_target_pairs={{0,16},{16,32},{32,48},{48,64},{64,80},{80,96},{96,112},{112,0},{1... | collective-permute-start | bytes 393224 | tf_op jit(solution)/shard_map/ppermute | solution.py:25
  129.6 7.9 %collective-permute-start.25 = (bf16[144,1152]{1,0:T(8,128)(2,1)S(1)}, bf16[144,1152]{1,0:T(8,128)(2,1)S(1)}, u32[]{:S(2)}, u32[]{:S(2)}) collective-permute-start(bf16[144,1152]{1,0:T(8,128)(2,1)S(1)} %collective-permute-done.21), channel_id=1, source_target_pairs={{0,112},{16,0},{32,16},{48,32},{64,48},{80,64},{96,80},{112,96},{1... | collective-permute-start | bytes 995336 | tf_op jit(solution)/shard_map/ppermute | solution.py:25
  134.6 7.3 %collective-permute-start.26 = (bf16[144,1152]{1,0:T(8,128)(2,1)S(1)}, bf16[144,1152]{1,0:T(8,128)(2,1)S(1)}, u32[]{:S(2)}, u32[]{:S(2)}) collective-permute-start(bf16[144,1152]{1,0:T(8,128)(2,1)S(1)} %collective-permute-done.22), channel_id=1, source_target_pairs={{0,16},{16,32},{32,48},{48,64},{64,80},{80,96},{96,112},{112,0},{1... | collective-permute-start | bytes 995336 | tf_op jit(solution)/shard_map/ppermute | solution.py:25
  134.7 20.5 %collective-permute-start.27 = (bf16[144,1152]{1,0:T(8,128)(2,1)S(1)}, bf16[144,1152]{1,0:T(8,128)(2,1)S(1)}, u32[]{:S(2)}, u32[]{:S(2)}) collective-permute-start(bf16[144,1152]{1,0:T(8,128)(2,1)S(1)} %collective-permute-done.23), channel_id=1, source_target_pairs={{0,112},{16,0},{32,16},{48,32},{64,48},{80,64},{96,80},{112,96},{1... | collective-permute-start | bytes 995336 | tf_op jit(solution)/shard_map/ppermute | solution.py:25
  137.3 17.9 %collective-permute-start.28 = (bf16[144,1152]{1,0:T(8,128)(2,1)S(1)}, bf16[144,1152]{1,0:T(8,128)(2,1)S(1)}, u32[]{:S(2)}, u32[]{:S(2)}) collective-permute-start(bf16[144,1152]{1,0:T(8,128)(2,1)S(1)} %collective-permute-done.24), channel_id=1, source_target_pairs={{0,16},{16,32},{32,48},{48,64},{64,80},{80,96},{96,112},{112,0},{1... | collective-permute-start | bytes 995336 | tf_op jit(solution)/shard_map/ppermute | solution.py:25
  137.5 14.2 %collective-permute-start.29 = (bf16[144,1152]{1,0:T(8,128)(2,1)S(1)}, bf16[144,1152]{1,0:T(8,128)(2,1)S(1)}, u32[]{:S(2)}, u32[]{:S(2)}) collective-permute-start(bf16[144,1152]{1,0:T(8,128)(2,1)S(1)} %collective-permute-done.25), channel_id=1, source_target_pairs={{0,112},{16,0},{32,16},{48,32},{64,48},{80,64},{96,80},{112,96},{1... | collective-permute-start | bytes 995336 | tf_op jit(solution)/shard_map/ppermute | solution.py:25
  141.8 13.5 %collective-permute-start.30 = (bf16[144,1152]{1,0:T(8,128)(2,1)S(1)}, bf16[144,1152]{1,0:T(8,128)(2,1)S(1)}, u32[]{:S(2)}, u32[]{:S(2)}) collective-permute-start(bf16[144,1152]{1,0:T(8,128)(2,1)S(1)} %collective-permute-done.26), channel_id=1, source_target_pairs={{0,16},{16,32},{32,48},{48,64},{64,80},{80,96},{96,112},{112,0},{1... | collective-permute-start | bytes 995336 | tf_op jit(solution)/shard_map/ppermute | solution.py:25
  151.7 7.5 %collective-permute-start.31 = (bf16[144,1152]{1,0:T(8,128)(2,1)S(1)}, bf16[144,1152]{1,0:T(8,128)(2,1)S(1)}, u32[]{:S(2)}, u32[]{:S(2)}) collective-permute-start(bf16[144,1152]{1,0:T(8,128)(2,1)S(1)} %collective-permute-done.29), channel_id=1, source_target_pairs={{0,112},{16,0},{32,16},{48,32},{64,48},{80,64},{96,80},{112,96},{1... | collective-permute-start | bytes 995336 | tf_op jit(solution)/shard_map/ppermute | solution.py:25
  159.2 3.4 %copy-start = (bf16[2,1152,1152]{2,1,0:T(8,128)(2,1)}, bf16[2,1152,1152]{2,1,0:T(8,128)(2,1)S(1)}, u32[]{:S(2)}) copy-start(bf16[2,1152,1152]{2,1,0:T(8,128)(2,1)S(1)} %bitcast_dynamic-update-slice_fusion.blocks) | copy-start | bytes 15925252
  162.6 32.9 %all-to-all-start = ((bf16[8,288,256]{2,1,0:T(8,128)(2,1)}), bf16[8,288,256]{2,1,0:T(8,128)(2,1)S(1)}, u32[]{:S(2)}, u32[]{:S(2)}) async-start(bf16[8,288,256]{2,1,0:T(8,128)(2,1)} %bitcast.131), calls=%async_computation | async-start | bytes 2359296 | tf_op jit(solution)/shard_map/all_to_all | solution.py:33
  167.2 20.1 %collective-permute-start.32 = (bf16[1024,512]{1,0:T(8,128)(2,1)S(1)}, bf16[1024,512]{1,0:T(8,128)(2,1)S(1)}, u32[]{:S(2)}, u32[]{:S(2)}) collective-permute-start(bf16[1024,512]{1,0:T(8,128)(2,1)S(1)} %constant_dynamic-update-slice_fusion), channel_id=1, source_target_pairs={{0,128},{16,144},{32,160},{48,176},{64,192},{80,208},{96,224},{112... | collective-permute-start | bytes 3145736 | tf_op jit(solution)/shard_map/ppermute | solution.py:29
  195.5 1.3 copy-start.2
  217.6 2.5 copy-start.1
  220.1 16.7 %copy-start.4 = (bf16[1,4608,64]{1,2,0:T(8,128)(2,1)S(1)}, bf16[1,4608,64]{1,2,0:T(8,128)(2,1)}, u32[]{:S(2)}) copy-start(bf16[1,4608,64]{1,2,0:T(8,128)(2,1)} %param.6) | copy-start | bytes 1769476
  220.1 16.7 %copy-start.5 = (f32[1,4608,64]{1,2,0:T(8,128)S(1)}, f32[1,4608,64]{1,2,0:T(8,128)}, u32[]{:S(2)}) copy-start(f32[1,4608,64]{1,2,0:T(8,128)} %param.7) | copy-start | bytes 3538948
  222.4 29.0 %collective-permute-start.33 = (bf16[64,2304]{1,0:T(8,128)(2,1)S(1)}, bf16[64,2304]{1,0:T(8,128)(2,1)S(1)}, u32[]{:S(2)}, u32[]{:S(2)}) collective-permute-start(bf16[64,2304]{1,0:T(8,128)(2,1)S(1)} %get-tuple-element.36), channel_id=1, source_target_pairs={{0,128},{16,144},{32,160},{48,176},{64,192},{80,208},{96,224},{112... | collective-permute-start | bytes 884744 | tf_op jit(solution)/shard_map/ppermute | solution.py:29
  223.7 26.1 %all-to-all-start.2 = ((f32[256,1,128]{2,1,0:T(1,128)}), f32[256,1,128]{2,1,0:T(1,128)S(1)}, u32[]{:S(2)}, u32[]{:S(2)}) async-start(f32[256,1,128]{2,1,0:T(1,128)} %bitcast.59), calls=%async_computation.2 | async-start | bytes 262144 | tf_op jit(solution)/shard_map/all_to_all | solution.py:247

commit v3 on v2

--- a/solution.py
+++ b/solution.py
@@ -1,3 +1,5 @@
+import functools
+
 import jax
 import jax.numpy as jnp
 from jax import lax
@@ -8,6 +10,7 @@
 BLK = 1152
 RING = 8
 SIDES = 2
+COUNT = 2
 TILE = 256
 
 first_decay = 0.9
@@ -35,7 +38,7 @@
 
 def ring_gather(chunks, z):
     rows = chunks[0].shape[0]
-    whole = jnp.zeros((len(chunks), RING * rows) + chunks[0].shape[1:], chunks[0].dtype)
+    whole = unset((len(chunks), RING * rows) + chunks[0].shape[1:], chunks[0].dtype)
 
     def put(whole, piece, i, place):
         return lax.dynamic_update_slice(whole, piece[None], (i, ((place + RING) % RING) * rows, 0))
@@ -56,6 +59,25 @@
     return whole
 
 
+def unset(shape, dtype):
+    return pl.pallas_call(
+        lambda out: None,
+        out_shape=jax.ShapeDtypeStruct(shape, dtype),
+        out_specs=pl.BlockSpec(memory_space=pl.ANY),
+    )()
+
+
+def after(values, ready):
+    count = len(values)
+    return pl.pallas_call(
+        lambda *refs: None,
+        out_shape=[jax.ShapeDtypeStruct(value.shape, value.dtype) for value in values],
+        in_specs=[pl.BlockSpec(memory_space=pl.ANY)] * (count + len(ready)),
+        out_specs=[pl.BlockSpec(memory_space=pl.ANY)] * count,
+        input_output_aliases={i: i for i in range(count)},
+    )(*values, *ready)
+
+
 def cut_kernel(owners, left, right, *pieces):
     me = lax.axis_index("shard")
     z = lax.rem(me, RING)
@@ -88,42 +110,61 @@
 
 def raw_kernel(values, blocks, mine, other, sums):
     y = lax.div(lax.axis_index("shard"), RING)
-    cols = mine.shape[0]
-    order = blocks.shape[1]
+    cols, order = mine.shape[1:]
     step = order // 3
     total = jnp.zeros((1, 128), jnp.float32)
-    for i in range(blocks.shape[0]):
+    for i in range(COUNT):
         back = values[i].T
-        for j in range(order // step):
+        for j in range(3):
+            lanes = slice(j * step, (j + 1) * step)
             raw = lax.dot_general(
-                back,
-                blocks[i, j * step : (j + 1) * step, :],
-                (((1,), (1,)), ((), ())),
-                preferred_element_type=jnp.float32,
+                back, blocks[i, lanes, :], (((1,), (1,)), ((), ())), preferred_element_type=jnp.float32
             )
             low = raw[:cols]
             high = raw[cols:]
-            lanes = slice(i * order + j * step, i * order + (j + 1) * step)
-            mine[:, lanes] = jnp.where(y == 0, low, high)
-            other[:, lanes] = jnp.where(y == 0, high, low).astype(jnp.bfloat16)
-            square = jnp.sum(raw * raw, 0, keepdims=True)
+            mine[i, :, lanes] = jnp.where(y == 0, low, high)
+            other[i, :, lanes] = jnp.where(y == 0, high, low).astype(jnp.bfloat16)
+            squares = jnp.sum(raw * raw, 0, keepdims=True)
             for k in range(step // 128):
-                total += square[:, k * 128 : (k + 1) * 128]
+                total += squares[:, k * 128 : (k + 1) * 128]
     sums[...] = jnp.broadcast_to(total, sums.shape)
 
 
 def raw_stage(values, blocks, devices):
     count, order, pairs = values.shape
-    shape = (pairs // SIDES, count * order)
+    cols = pairs // SIDES
     return pl.pallas_call(
         raw_kernel,
         out_shape=(
-            jax.ShapeDtypeStruct(shape, jnp.float32),
-            jax.ShapeDtypeStruct(shape, jnp.bfloat16),
+            jax.ShapeDtypeStruct((count, cols, order), jnp.float32),
+            jax.ShapeDtypeStruct((count, cols, order), jnp.bfloat16),
             jax.ShapeDtypeStruct((devices, 128), jnp.float32),
         ),
         compiler_params=pltpu.CompilerParams(vmem_limit_bytes=24 * 1024 * 1024),
     )(values, blocks)
+
+
+def clip_kernel(cells, sums, mine, other, out):
+    y = lax.div(lax.axis_index("shard"), RING)
+    count, _, order = mine.shape
+    total = jnp.sum(jnp.sum(sums[...], 0, keepdims=True), 1, keepdims=True)
+    factor = jnp.minimum(1.0, clip_limit / jnp.sqrt(total / cells + 1e-06))
+    for i in range(count):
+        own = factor * mine[i]
+        far = factor * other[i].astype(jnp.float32)
+        low = slice(i * order, (i + 1) * order)
+        high = slice((count + i) * order, (count + i + 1) * order)
+        out[:, low] = jnp.where(y == 0, own, far).astype(jnp.bfloat16)
+        out[:, high] = jnp.where(y == 0, far, own).astype(jnp.bfloat16)
+
+
+def clip_stage(sums, mine, other, cells):
+    count, cols, order = mine.shape
+    return pl.pallas_call(
+        functools.partial(clip_kernel, cells),
+        out_shape=jax.ShapeDtypeStruct((cols, SIDES * count * order), jnp.bfloat16),
+        compiler_params=pltpu.CompilerParams(vmem_limit_bytes=24 * 1024 * 1024),
+    )(sums, mine, other)
 
 
 def right_kernel(values, right, second, second_out, out, scaled):
@@ -191,7 +232,7 @@
         left_slots[0, 0].reshape(RING, piece, BLK),
         right_slots[0, 0].reshape(RING, SIDES * cols, width),
     )
-    eighths = jnp.zeros((RING, piece, BLK), jnp.bfloat16)
+    eighths = unset((RING, piece, BLK), jnp.bfloat16)
     for step in (0, 4, 3, 5, 2, 6, 1, 7):
         part = pieces[step]
         if step:
@@ -218,15 +259,17 @@
     keep_right = lax.dynamic_slice_in_dim(keep_right, y * side, side, 1)
     took_right = cross(give_right)
     right_chunk = jnp.where(own_y[SIDES * count] == y, keep_right, took_right)
-    took = [cross(pick((1 - y) * count + i)) for i in range(count)]
+    give = [pick((1 - y) * count + i) for i in range(count)]
+    give = after(give, [took_right])
+    took = [cross(value) for value in give]
     chunk = [
         jnp.where(own_y[y * count + i] == y, pick(y * count + i), took[i]) for i in range(count)
     ]
 
     right_half = ring_gather([right_chunk], z)[0]
     blocks = ring_gather(chunk, z)
-    right_half, blocks = lax.optimization_barrier((right_half, blocks))
     right_other = cross(right_half)
+    (both,) = after([both], [right_other])
     right_all = jnp.where(
         first,
         jnp.concatenate([right_half, right_other], 1),
@@ -243,16 +286,10 @@
     values = ring_all_to_all(returning).reshape(count, BLK, SIDES * cols)
     devices = lax.axis_size("shard") * lax.axis_size("layer")
     raw_mine, raw_give, sums = raw_stage(values, blocks, devices)
-    raw_other = cross(raw_give).astype(jnp.float32)
-    total = jnp.sum(lax.all_to_all(sums, ("shard", "layer"), 0, 0))
+    raw_other = cross(raw_give)
+    sums = lax.all_to_all(sums, ("shard", "layer"), 0, 0)
     cells = lax.axis_size("layer") * grad.shape[0] * rows_all * cols * RING * SIDES
-    factor = jnp.minimum(1.0, clip_limit / jnp.sqrt(total / cells + 1e-06))
-    direction = jnp.where(
-        first,
-        jnp.concatenate([raw_mine, raw_other], 1),
-        jnp.concatenate([raw_other, raw_mine], 1),
-    )
-    direction = (factor * direction).astype(jnp.bfloat16)
+    direction = clip_stage(sums, raw_mine, raw_other, float(cells))
     return (moment_new.T[None], second_new[None], direction.T[None])
 
 

time: 253 us -> 245 us (0.968)
  waiting for transfers between devices: 120 us -> 88.5 us
  local copies, waits for them, and re-layouts: 16.9 us -> 31.9 us
  starting transfers between devices: 66.8 us -> 71.3 us
  matrix products: 3.34 us -> 6.1 us
    ppermute x28, waiting for transfers between devices: 74.4 us -> 50.2 us  [ring_shift(): return lax.ppermute(value, 'shard', pairs)]
    ppermute x6, waiting for transfers between devices: 27 us -> 3.02 us  [cross(): lax.ppermute(value, 'shard', [(s, (s + RING) % (RING * SIDES)) for s in r...]
    all_to_all x1, waiting for transfers between devices: 7.33 us -> 24.9 us  [ring_all_to_all(): return lax.all_to_all(value, 'shard', 0, 0, axis_index_groups=rings())]
    dynamic_update_slice x21, local copies, waits for them, and re-layouts: 0.61 us -> 15.2 us  [put(): lax.dynamic_update_slice(whole, piece[None], (i, (place + RING) % RING *...]
    dot_general x1, matrix products: 3.34 us -> 6.1 us  [body(): jnp.einsum('bkr,bck->brc', blocks, both, preferred_element_type=jnp.float32)]
    unnamed x20 -> x24, local copies, waits for them, and re-layouts: 5.35 us -> 6.51 us
  transfers between devices with their start and end apart: 36 -> 36, of which waited for: 18 -> 13; matrix products, arithmetic and copies ran while one was open for 6% -> 12% of each run, Pallas kernels for 0% -> 0%
where the time goes in v3:
time: 245 us; the launch traced here: 244 us
  waiting for transfers between devices  88.5 us (36%)
  starting transfers between devices  71.3 us (29%)
  local copies, waits for them, and re-layouts  31.9 us (13%)
  blocking collectives  15.4 us (6%)
  between operations  12.1 us (5%)
  other arithmetic  10.7 us (4%)
  Pallas kernels  7.85 us (3%)
  matrix products  6.1 us (2%)
    ppermute x28, waiting for transfers between devices, ring_shift(): return lax.ppermute(value, 'shard', pairs)  50.2 us
    ppermute x28, starting transfers between devices, ring_shift(): return lax.ppermute(value, 'shard', pairs)  46 us
    all_to_all x1, waiting for transfers between devices, ring_all_to_all(): return lax.all_to_all(value, 'shard', 0, 0, axis_index_groups=rings())  24.9 us
    all_to_all x1, blocking collectives, ring_all_to_all(): return lax.all_to_all(value, 'shard', 0, 0, axis_index_groups=rings())  15.4 us
    dynamic_update_slice x21, local copies, waits for them, and re-layouts, put(): lax.dynamic_update_slice(whole, piece[None], (i, (place + RING) % RING *...  15.2 us
    all_to_all x1, starting transfers between devices, body(): sums = lax.all_to_all(sums, ('shard', 'layer'), 0, 0)  14.1 us
    all_to_all x1, waiting for transfers between devices, body(): sums = lax.all_to_all(sums, ('shard', 'layer'), 0, 0)  10.3 us
    ppermute x6, starting transfers between devices, cross(): lax.ppermute(value, 'shard', [(s, (s + RING) % (RING * SIDES)) for s in r...  6.79 us
  transfers between devices with their start and end apart: 36, of which 13 were waited for; matrix products, arithmetic and copies ran while one was open for 12% of the time, Pallas kernels for 0%

profile of v3, /device:TPU:1, one launch (start us, length us, event | category | flops | bytes accessed | tf_op | source)
XLA Modules:
  0.0 243.9 jit_solution(167474894720195744)
XLA Ops:
  1.3 1.1 copy-done.8
  2.4 3.3 %shard_map.93 = (bf16[8,144,1152]{2,1,0:T(8,128)(2,1)}, bf16[144,1152]{1,0:T(8,128)(2,1)}, bf16[144,1152]{1,0:T(8,128)(2,1)}, bf16[144,1152]{1,0:T(8,128)(2,1)},...) fusion(bf16[8,144,1152]{2,1,0:T(8,128)(2,1)} %shard_map.86, ...), kind=kCustom, calls=%fused_computation.43 | custom fusion | bytes 7405636 | tf_op jit(solution)/shard_map/pallas_call | solution.py:99
  5.7 7.7 %collective-permute-start = (bf16[144,1152]{1,0:T(8,128)(2,1)}, bf16[144,1152]{1,0:T(8,128)(2,1)}, u32[]{:S(2)}, u32[]{:S(2)}) collective-permute-start(bf16[144,1152]{1,0:T(8,128)(2,1)} %get-tuple-element.40), channel_id=1, source_target_pairs={{0,64},{16,80},{32,96},{48,112},{64,0},{80,16},{96,32},{112,48},{1... | collective-permute-start | bytes 995336 | tf_op jit(solution)/shard_map/ppermute | solution.py:28
  13.4 1.6 collective-permute-start.1
  15.1 2.8 %collective-permute-start.2 = (bf16[144,1152]{1,0:T(8,128)(2,1)}, bf16[144,1152]{1,0:T(8,128)(2,1)}, u32[]{:S(2)}, u32[]{:S(2)}) collective-permute-start(bf16[144,1152]{1,0:T(8,128)(2,1)} %get-tuple-element.44), channel_id=1, source_target_pairs={{0,80},{16,96},{32,112},{48,0},{64,16},{80,32},{96,48},{112,64},{1... | collective-permute-start | bytes 995336 | tf_op jit(solution)/shard_map/ppermute | solution.py:28
  17.9 1.2 collective-permute-start.3
  19.1 2.4 collective-permute-start.4
  30.4 2.3 fusion.1
  35.7 1.2 fusion.2
  36.9 0.8 collective-permute-start.5
  37.7 1.0 bitcast_dynamic-update-slice_fusion.22
  38.7 15.7 %collective-permute-done.1 = bf16[144,1152]{1,0:T(8,128)(2,1)} collective-permute-done((bf16[144,1152]{1,0:T(8,128)(2,1)}, bf16[144,1152]{1,0:T(8,128)(2,1)}, u32[]{:S(2)}, u32[]{:S(2)}) %collective-permute-start.1) | collective-permute-done | bytes 331808 | tf_op jit(solution)/shard_map/ppermute | solution.py:28
  54.4 1.0 bitcast_dynamic-update-slice_fusion.21
  55.4 1.2 collective-permute-start.7
  56.7 1.0 bitcast_dynamic-update-slice_fusion.20
  57.7 1.0 bitcast_dynamic-update-slice_fusion.19
  58.7 6.4 %collective-permute-done.4 = bf16[144,1152]{1,0:T(8,128)(2,1)} collective-permute-done((bf16[144,1152]{1,0:T(8,128)(2,1)}, bf16[144,1152]{1,0:T(8,128)(2,1)}, u32[]{:S(2)}, u32[]{:S(2)}) %collective-permute-start.4) | collective-permute-done | bytes 331808 | tf_op jit(solution)/shard_map/ppermute | solution.py:28
  65.1 1.0 bitcast_dynamic-update-slice_fusion.18
  66.1 4.9 %collective-permute-done.5 = bf16[144,1152]{1,0:T(8,128)(2,1)S(1)} collective-permute-done((bf16[144,1152]{1,0:T(8,128)(2,1)}, bf16[144,1152]{1,0:T(8,128)(2,1)S(1)}, u32[]{:S(2)}, u32[]{:S(2)}) %collective-permute-start.5) | collective-permute-done | bytes 331808 | tf_op jit(solution)/shard_map/ppermute | solution.py:28
  71.5 0.9 dynamic-slice_bitcast_fusion
  72.4 1.4 collective-permute-start.8
  74.2 2.2 collective-permute-done.8.refs_2_
  77.1 1.8 collective-permute-start.25
  78.8 2.4 collective-permute-start.26
  81.2 1.1 pad_maximum_fusion.2.refs_0_
  82.4 1.3 collective-permute-start.9
  83.8 2.7 %collective-permute-start.28 = (bf16[128,512]{1,0:T(8,128)(2,1)S(1)}, bf16[128,512]{1,0:T(8,128)(2,1)S(1)}, u32[]{:S(2)}, u32[]{:S(2)}) collective-permute-start(bf16[128,512]{1,0:T(8,128)(2,1)S(1)} %collective-permute-done.26), channel_id=1, source_target_pairs={{0,112},{16,0},{32,16},{48,32},{64,48},{80,64},{96,80},{112,96},{1... | collective-permute-start | bytes 393224 | tf_op jit(solution)/shard_map/ppermute | solution.py:28
  87.8 1.0 collective-permute-done.27
  88.9 2.7 %collective-permute-start.30 = (bf16[128,512]{1,0:T(8,128)(2,1)S(1)}, bf16[128,512]{1,0:T(8,128)(2,1)S(1)}, u32[]{:S(2)}, u32[]{:S(2)}) collective-permute-start(bf16[128,512]{1,0:T(8,128)(2,1)S(1)} %collective-permute-done.28), channel_id=1, source_target_pairs={{0,112},{16,0},{32,16},{48,32},{64,48},{80,64},{96,80},{112,96},{1... | collective-permute-start | bytes 393224 | tf_op jit(solution)/shard_map/ppermute | solution.py:28
  92.9 0.8 bitcast_dynamic-update-slice_fusion.15
  93.7 2.7 %collective-permute-start.12 = (bf16[144,1152]{1,0:T(8,128)(2,1)S(1)}, bf16[144,1152]{1,0:T(8,128)(2,1)S(1)}, u32[]{:S(2)}, u32[]{:S(2)}) collective-permute-start(bf16[144,1152]{1,0:T(8,128)(2,1)S(1)} %get-tuple-element.58), channel_id=1, source_target_pairs={{0,112},{16,0},{32,16},{48,32},{64,48},{80,64},{96,80},{112,96},{1... | collective-permute-start | bytes 995336 | tf_op jit(solution)/shard_map/ppermute | solution.py:28
  96.4 0.8 collective-permute-done.10
  97.2 0.8 bitcast_dynamic-update-slice_fusion.14
  98.7 2.7 %collective-permute-start.14 = (bf16[144,1152]{1,0:T(8,128)(2,1)S(1)}, bf16[144,1152]{1,0:T(8,128)(2,1)S(1)}, u32[]{:S(2)}, u32[]{:S(2)}) collective-permute-start(bf16[144,1152]{1,0:T(8,128)(2,1)S(1)} %get-tuple-element.56), channel_id=1, source_target_pairs={{0,112},{16,0},{32,16},{48,32},{64,48},{80,64},{96,80},{112,96},{1... | collective-permute-start | bytes 995336 | tf_op jit(solution)/shard_map/ppermute | solution.py:28
  102.1 9.6 %collective-permute-done.31 = bf16[128,512]{1,0:T(8,128)(2,1)S(1)} collective-permute-done((bf16[128,512]{1,0:T(8,128)(2,1)S(1)}, bf16[128,512]{1,0:T(8,128)(2,1)S(1)}, u32[]{:S(2)}, u32[]{:S(2)}) %collective-permute-start.31) | collective-permute-done | bytes 131104 | tf_op jit(solution)/shard_map/ppermute | solution.py:28
  112.4 1.2 collective-permute-start.32
  113.6 2.7 %collective-permute-start.16 = (bf16[144,1152]{1,0:T(8,128)(2,1)S(1)}, bf16[144,1152]{1,0:T(8,128)(2,1)S(1)}, u32[]{:S(2)}, u32[]{:S(2)}) collective-permute-start(bf16[144,1152]{1,0:T(8,128)(2,1)S(1)} %collective-permute-done.12), channel_id=1, source_target_pairs={{0,112},{16,0},{32,16},{48,32},{64,48},{80,64},{96,80},{112,96},{1... | collective-permute-start | bytes 995336 | tf_op jit(solution)/shard_map/ppermute | solution.py:28
  118.5 2.7 %collective-permute-start.18 = (bf16[144,1152]{1,0:T(8,128)(2,1)S(1)}, bf16[144,1152]{1,0:T(8,128)(2,1)S(1)}, u32[]{:S(2)}, u32[]{:S(2)}) collective-permute-start(bf16[144,1152]{1,0:T(8,128)(2,1)S(1)} %collective-permute-done.14), channel_id=1, source_target_pairs={{0,112},{16,0},{32,16},{48,32},{64,48},{80,64},{96,80},{112,96},{1... | collective-permute-start | bytes 995336 | tf_op jit(solution)/shard_map/ppermute | solution.py:28
  122.0 2.7 %collective-permute-start.20 = (bf16[144,1152]{1,0:T(8,128)(2,1)S(1)}, bf16[144,1152]{1,0:T(8,128)(2,1)S(1)}, u32[]{:S(2)}, u32[]{:S(2)}) collective-permute-start(bf16[144,1152]{1,0:T(8,128)(2,1)S(1)} %collective-permute-done.16), channel_id=1, source_target_pairs={{0,112},{16,0},{32,16},{48,32},{64,48},{80,64},{96,80},{112,96},{1... | collective-permute-start | bytes 995336 | tf_op jit(solution)/shard_map/ppermute | solution.py:28
  124.7 2.1 collective-permute-done.17
  126.8 0.8 bitcast_dynamic-update-slice_fusion.9
  128.3 0.8 bitcast_dynamic-update-slice_fusion.7
  129.1 3.0 %collective-permute-start.22 = (bf16[144,1152]{1,0:T(8,128)(2,1)S(1)}, bf16[144,1152]{1,0:T(8,128)(2,1)S(1)}, u32[]{:S(2)}, u32[]{:S(2)}) collective-permute-start(bf16[144,1152]{1,0:T(8,128)(2,1)S(1)} %collective-permute-done.18), channel_id=1, source_target_pairs={{0,112},{16,0},{32,16},{48,32},{64,48},{80,64},{96,80},{112,96},{1... | collective-permute-start | bytes 995336 | tf_op jit(solution)/shard_map/ppermute | solution.py:28
  132.8 1.1 collective-permute-done.19
  133.9 9.0 %collective-permute-done.22 = bf16[144,1152]{1,0:T(8,128)(2,1)S(1)} collective-permute-done((bf16[144,1152]{1,0:T(8,128)(2,1)S(1)}, bf16[144,1152]{1,0:T(8,128)(2,1)S(1)}, u32[]{:S(2)}, u32[]{:S(2)}) %collective-permute-start.22) | collective-permute-done | bytes 331808 | tf_op jit(solution)/shard_map/ppermute | solution.py:28
  142.9 3.4 %collective-permute-start.24 = (bf16[144,1152]{1,0:T(8,128)(2,1)S(1)}, bf16[144,1152]{1,0:T(8,128)(2,1)S(1)}, u32[]{:S(2)}, u32[]{:S(2)}) collective-permute-start(bf16[144,1152]{1,0:T(8,128)(2,1)S(1)} %collective-permute-done.22), channel_id=1, source_target_pairs={{0,112},{16,0},{32,16},{48,32},{64,48},{80,64},{96,80},{112,96},{1... | collective-permute-start | bytes 995336 | tf_op jit(solution)/shard_map/ppermute | solution.py:28
  147.1 0.8 bitcast_dynamic-update-slice_fusion.4
  147.8 0.8 bitcast_dynamic-update-slice_fusion.3
  149.4 1.0 copy-done.6
  151.1 0.8 bitcast_dynamic-update-slice_fusion.blocks
  151.9 6.1 %convolution_convert_fusion = bf16[2,1152,256]{2,1,0:T(8,128)(2,1)} fusion(bf16[2,1152,1152]{2,1,0:T(8,128)(2,1)} %bitcast_dynamic-update-slice_fusion.blocks, bf16[2,256,1152]{2,1,0:T(8,128)(2,1)} %shard_map.89), kind=kOutput, calls=%fused_computation | convolution fusion | flops 1359544320 | bytes 7667712 | tf_op jit(solution)/shard_map/bkr,bck->brc/dot_general | solution.py:281
  158.0 4.4 %all-to-all-start = ((bf16[8,288,256]{2,1,0:T(8,128)(2,1)}), bf16[8,288,256]{2,1,0:T(8,128)(2,1)S(1)}, u32[]{:S(2)}, u32[]{:S(2)}) async-start(bf16[8,288,256]{2,1,0:T(8,128)(2,1)} %bitcast.134), calls=%async_computation | async-start | bytes 2359296 | tf_op jit(solution)/shard_map/all_to_all | solution.py:36
  162.4 2.2 pad_maximum_fusion
  164.8 24.9 %all-to-all-done.values = bf16[8,288,256]{2,1,0:T(8,128)(2,1)S(1)} async-done(((bf16[8,288,256]{2,1,0:T(8,128)(2,1)}), bf16[8,288,256]{2,1,0:T(8,128)(2,1)S(1)}, u32[]{:S(2)}, u32[]{:S(2)}) %all-to-all-start) | async-done | bytes 1179680 | tf_op jit(solution)/shard_map/all_to_all | solution.py:36
  189.7 1.3 copy-done.1
  191.0 4.4 %shard_map.90 = (f32[288,1024]{1,0:T(8,128)}, bf16[8,288,128]{2,1,0:T(8,128)(2,1)S(1)}) custom-call(bf16[8,288,256]{2,1,0:T(8,128)(2,1)S(1)} %all-to-all-done.values, bf16[1024,1024]{1,0:T(8,128)(2,1)S(1)} %bitcast.125, f32[288,1024]{1,0:T(8,128)S(1)} %bitcast.127), custom_call_target="tpu_custom_call" | custom-call | tf_op jit(solution)/shard_map/pallas_call | solution.py:203
  195.4 15.4 %all_to_all.21 = bf16[8,288,128]{2,1,0:T(8,128)(2,1)S(1)} all-to-all(bf16[8,288,128]{2,1,0:T(8,128)(2,1)S(1)} %get-tuple-element.33), channel_id=1, replica_groups={{0,16,32,48,64,80,96,112},{128,144,160,176,192,208,224,240},{1,17,33,49..., dimensions={0} | all-to-all | bytes 1179648 | tf_op jit(solution)/shard_map/all_to_all | solution.py:36
  210.8 2.5 %copy-done = bf16[2,1152,1152]{2,1,0:T(8,128)(2,1)S(1)} copy-done((bf16[2,1152,1152]{2,1,0:T(8,128)(2,1)S(1)}, bf16[2,1152,1152]{2,1,0:T(8,128)(2,1)}, u32[]{:S(2)}) %copy-start) | copy-done | bytes 5308440
  213.3 2.3 shard_map.91
  215.6 14.1 %all-to-all-start.2 = ((f32[256,1,128]{2,1,0:T(1,128)}), f32[256,1,128]{2,1,0:T(1,128)S(1)}, u32[]{:S(2)}, u32[]{:S(2)}) async-start(f32[256,1,128]{2,1,0:T(1,128)} %bitcast.60), calls=%async_computation.2 | async-start | bytes 262144 | tf_op jit(solution)/shard_map/all_to_all | solution.py:290
  229.7 1.5 collective-permute-start.33
  231.2 1.2 multiply_add_fusion
  232.4 10.3 %all-to-all-done.2 = f32[256,1,128]{2,1,0:T(1,128)S(1)} async-done(((f32[256,1,128]{2,1,0:T(1,128)}), f32[256,1,128]{2,1,0:T(1,128)S(1)}, u32[]{:S(2)}, u32[]{:S(2)}) %all-to-all-start.2) | async-done | bytes 131104 | tf_op jit(solution)/shard_map/all_to_all | solution.py:290
  242.8 1.1 shard_map.92
  (87 shorter events, 14.7 us)
Async XLA Ops:
  0.6 0.7 copy-start.11
  0.6 1.8 copy-start.8
  5.7 31.2 %collective-permute-start = (bf16[144,1152]{1,0:T(8,128)(2,1)}, bf16[144,1152]{1,0:T(8,128)(2,1)}, u32[]{:S(2)}, u32[]{:S(2)}) collective-permute-start(bf16[144,1152]{1,0:T(8,128)(2,1)} %get-tuple-element.40), channel_id=1, source_target_pairs={{0,64},{16,80},{32,96},{48,112},{64,0},{80,16},{96,32},{112,48},{1... | collective-permute-start | bytes 995336 | tf_op jit(solution)/shard_map/ppermute | solution.py:28
  13.4 41.0 %collective-permute-start.1 = (bf16[144,1152]{1,0:T(8,128)(2,1)}, bf16[144,1152]{1,0:T(8,128)(2,1)}, u32[]{:S(2)}, u32[]{:S(2)}) collective-permute-start(bf16[144,1152]{1,0:T(8,128)(2,1)} %get-tuple-element.42), channel_id=1, source_target_pairs={{0,48},{16,64},{32,80},{48,96},{64,112},{80,0},{96,16},{112,32},{1... | collective-permute-start | bytes 995336 | tf_op jit(solution)/shard_map/ppermute | solution.py:28
  15.1 40.3 %collective-permute-start.2 = (bf16[144,1152]{1,0:T(8,128)(2,1)}, bf16[144,1152]{1,0:T(8,128)(2,1)}, u32[]{:S(2)}, u32[]{:S(2)}) collective-permute-start(bf16[144,1152]{1,0:T(8,128)(2,1)} %get-tuple-element.44), channel_id=1, source_target_pairs={{0,80},{16,96},{32,112},{48,0},{64,16},{80,32},{96,48},{112,64},{1... | collective-permute-start | bytes 995336 | tf_op jit(solution)/shard_map/ppermute | solution.py:28
  17.9 39.8 %collective-permute-start.3 = (bf16[144,1152]{1,0:T(8,128)(2,1)}, bf16[144,1152]{1,0:T(8,128)(2,1)}, u32[]{:S(2)}, u32[]{:S(2)}) collective-permute-start(bf16[144,1152]{1,0:T(8,128)(2,1)} %get-tuple-element.46), channel_id=1, source_target_pairs={{0,32},{16,48},{32,64},{48,80},{64,96},{80,112},{96,0},{112,16},{1... | collective-permute-start | bytes 995336 | tf_op jit(solution)/shard_map/ppermute | solution.py:28
  19.1 11.3 %copy-start.3 = (bf16[1,4608,64]{1,2,0:T(8,128)(2,1)S(1)}, bf16[1,4608,64]{1,2,0:T(8,128)(2,1)}, u32[]{:S(2)}) copy-start(bf16[1,4608,64]{1,2,0:T(8,128)(2,1)} %param.6) | copy-start | bytes 1769476
  19.1 46.0 %collective-permute-start.4 = (bf16[144,1152]{1,0:T(8,128)(2,1)}, bf16[144,1152]{1,0:T(8,128)(2,1)}, u32[]{:S(2)}, u32[]{:S(2)}) collective-permute-start(bf16[144,1152]{1,0:T(8,128)(2,1)} %get-tuple-element.48), channel_id=1, source_target_pairs={{0,96},{16,112},{32,0},{48,16},{64,32},{80,48},{96,64},{112,80},{1... | collective-permute-start | bytes 995336 | tf_op jit(solution)/shard_map/ppermute | solution.py:28
  28.2 9.5 %copy-start.2 = (bf16[8,144,1152]{2,1,0:T(8,128)(2,1)S(1)}, bf16[8,144,1152]{2,1,0:T(8,128)(2,1)}, u32[]{:S(2)}) copy-start(bf16[8,144,1152]{2,1,0:T(8,128)(2,1)} %get-tuple-element.39) | copy-start | bytes 7962628
  35.7 18.7 %copy-start.10 = (bf16[144,1152]{1,0:T(8,128)(2,1)S(1)}, bf16[144,1152]{1,0:T(8,128)(2,1)}, u32[]{:S(2)}) copy-start(bf16[144,1152]{1,0:T(8,128)(2,1)} %get-tuple-element.52) | copy-start | bytes 995332
  36.9 34.2 %collective-permute-start.5 = (bf16[144,1152]{1,0:T(8,128)(2,1)}, bf16[144,1152]{1,0:T(8,128)(2,1)S(1)}, u32[]{:S(2)}, u32[]{:S(2)}) collective-permute-start(bf16[144,1152]{1,0:T(8,128)(2,1)} %get-tuple-element.50), channel_id=1, source_target_pairs={{0,16},{16,32},{32,48},{48,64},{64,80},{80,96},{96,112},{112,0},{1... | collective-permute-start | bytes 995336 | tf_op jit(solution)/shard_map/ppermute | solution.py:28
  54.4 17.0 %collective-permute-start.6 = (bf16[144,1152]{1,0:T(8,128)(2,1)S(1)}, bf16[144,1152]{1,0:T(8,128)(2,1)S(1)}, u32[]{:S(2)}, u32[]{:S(2)}) collective-permute-start(bf16[144,1152]{1,0:T(8,128)(2,1)S(1)} %copy-done.10), channel_id=1, source_target_pairs={{0,112},{16,0},{32,16},{48,32},{64,48},{80,64},{96,80},{112,96},{1... | collective-permute-start | bytes 995336 | tf_op jit(solution)/shard_map/ppermute | solution.py:28
  55.4 16.0 %collective-permute-start.7 = (bf16[2,64,2304]{2,1,0:T(8,128)(2,1)S(1)}, bf16[2,64,2304]{2,1,0:T(8,128)(2,1)S(1)}, u32[]{:S(2)}, u32[]{:S(2)}) collective-permute-start(bf16[2,64,2304]{2,1,0:T(8,128)(2,1)S(1)} %get-tuple-element.67), channel_id=1, source_target_pairs={{0,128},{16,144},{32,160},{48,176},{64,192},{80,208},{96,224},{112... | collective-permute-start | bytes 1769480 | tf_op jit(solution)/shard_map/ppermute | solution.py:32
  72.4 3.9 %collective-permute-start.8 = (bf16[128,512]{1,0:T(8,128)(2,1)S(1)}, bf16[128,512]{1,0:T(8,128)(2,1)S(1)}, u32[]{:S(2)}, u32[]{:S(2)}) collective-permute-start(bf16[128,512]{1,0:T(8,128)(2,1)S(1)} %constant_dynamic-slice_fusion), channel_id=1, source_target_pairs={{0,128},{16,144},{32,160},{48,176},{64,192},{80,208},{96,224},{112... | collective-permute-start | bytes 393224 | tf_op jit(solution)/shard_map/ppermute | solution.py:32
  76.4 6.0 %copy-start.9 = (bf16[128,512]{1,0:T(8,128)(2,1)}, bf16[128,512]{1,0:T(8,128)(2,1)S(1)}, u32[]{:S(2)}) copy-start(bf16[128,512]{1,0:T(8,128)(2,1)S(1)} %collective-permute-done.8.refs_2_) | copy-start | bytes 393220
  77.1 6.8 %collective-permute-start.25 = (bf16[128,512]{1,0:T(8,128)(2,1)S(1)}, bf16[128,512]{1,0:T(8,128)(2,1)S(1)}, u32[]{:S(2)}, u32[]{:S(2)}) collective-permute-start(bf16[128,512]{1,0:T(8,128)(2,1)S(1)} %get-tuple-element.54), channel_id=1, source_target_pairs={{0,16},{16,32},{32,48},{48,64},{64,80},{80,96},{96,112},{112,0},{1... | collective-permute-start | bytes 393224 | tf_op jit(solution)/shard_map/ppermute | solution.py:28
  78.8 5.0 %collective-permute-start.26 = (bf16[128,512]{1,0:T(8,128)(2,1)S(1)}, bf16[128,512]{1,0:T(8,128)(2,1)S(1)}, u32[]{:S(2)}, u32[]{:S(2)}) collective-permute-start(bf16[128,512]{1,0:T(8,128)(2,1)S(1)} %get-tuple-element.54), channel_id=1, source_target_pairs={{0,112},{16,0},{32,16},{48,32},{64,48},{80,64},{96,80},{112,96},{1... | collective-permute-start | bytes 393224 | tf_op jit(solution)/shard_map/ppermute | solution.py:28
  82.4 10.5 %collective-permute-start.9 = (bf16[144,1152]{1,0:T(8,128)(2,1)}, bf16[144,1152]{1,0:T(8,128)(2,1)S(1)}, u32[]{:S(2)}, u32[]{:S(2)}) collective-permute-start(bf16[144,1152]{1,0:T(8,128)(2,1)} %get-tuple-element.29), channel_id=1, source_target_pairs={{0,128},{16,144},{32,160},{48,176},{64,192},{80,208},{96,224},{112... | collective-permute-start | bytes 995336 | tf_op jit(solution)/shard_map/ppermute | solution.py:32
  83.7 13.6 %collective-permute-start.10 = (bf16[144,1152]{1,0:T(8,128)(2,1)}, bf16[144,1152]{1,0:T(8,128)(2,1)S(1)}, u32[]{:S(2)}, u32[]{:S(2)}) collective-permute-start(bf16[144,1152]{1,0:T(8,128)(2,1)} %get-tuple-element.30), channel_id=1, source_target_pairs={{0,128},{16,144},{32,160},{48,176},{64,192},{80,208},{96,224},{112... | collective-permute-start | bytes 995336 | tf_op jit(solution)/shard_map/ppermute | solution.py:32
  83.8 5.0 %collective-permute-start.27 = (bf16[128,512]{1,0:T(8,128)(2,1)S(1)}, bf16[128,512]{1,0:T(8,128)(2,1)S(1)}, u32[]{:S(2)}, u32[]{:S(2)}) collective-permute-start(bf16[128,512]{1,0:T(8,128)(2,1)S(1)} %collective-permute-done.25), channel_id=1, source_target_pairs={{0,16},{16,32},{32,48},{48,64},{64,80},{80,96},{96,112},{112,0},{1... | collective-permute-start | bytes 393224 | tf_op jit(solution)/shard_map/ppermute | solution.py:28
  83.8 5.0 %collective-permute-start.28 = (bf16[128,512]{1,0:T(8,128)(2,1)S(1)}, bf16[128,512]{1,0:T(8,128)(2,1)S(1)}, u32[]{:S(2)}, u32[]{:S(2)}) collective-permute-start(bf16[128,512]{1,0:T(8,128)(2,1)S(1)} %collective-permute-done.26), channel_id=1, source_target_pairs={{0,112},{16,0},{32,16},{48,32},{64,48},{80,64},{96,80},{112,96},{1... | collective-permute-start | bytes 393224 | tf_op jit(solution)/shard_map/ppermute | solution.py:28
  88.9 9.2 %collective-permute-start.29 = (bf16[128,512]{1,0:T(8,128)(2,1)S(1)}, bf16[128,512]{1,0:T(8,128)(2,1)S(1)}, u32[]{:S(2)}, u32[]{:S(2)}) collective-permute-start(bf16[128,512]{1,0:T(8,128)(2,1)S(1)} %collective-permute-done.27), channel_id=1, source_target_pairs={{0,16},{16,32},{32,48},{48,64},{64,80},{80,96},{96,112},{112,0},{1... | collective-permute-start | bytes 393224 | tf_op jit(solution)/shard_map/ppermute | solution.py:28
  88.9 9.8 %collective-permute-start.30 = (bf16[128,512]{1,0:T(8,128)(2,1)S(1)}, bf16[128,512]{1,0:T(8,128)(2,1)S(1)}, u32[]{:S(2)}, u32[]{:S(2)}) collective-permute-start(bf16[128,512]{1,0:T(8,128)(2,1)S(1)} %collective-permute-done.28), channel_id=1, source_target_pairs={{0,112},{16,0},{32,16},{48,32},{64,48},{80,64},{96,80},{112,96},{1... | collective-permute-start | bytes 393224 | tf_op jit(solution)/shard_map/ppermute | solution.py:28
  93.7 19.9 %collective-permute-start.11 = (bf16[144,1152]{1,0:T(8,128)(2,1)S(1)}, bf16[144,1152]{1,0:T(8,128)(2,1)S(1)}, u32[]{:S(2)}, u32[]{:S(2)}) collective-permute-start(bf16[144,1152]{1,0:T(8,128)(2,1)S(1)} %get-tuple-element.58), channel_id=1, source_target_pairs={{0,16},{16,32},{32,48},{48,64},{64,80},{80,96},{96,112},{112,0},{1... | collective-permute-start | bytes 995336 | tf_op jit(solution)/shard_map/ppermute | solution.py:28
  93.7 19.9 %collective-permute-start.12 = (bf16[144,1152]{1,0:T(8,128)(2,1)S(1)}, bf16[144,1152]{1,0:T(8,128)(2,1)S(1)}, u32[]{:S(2)}, u32[]{:S(2)}) collective-permute-start(bf16[144,1152]{1,0:T(8,128)(2,1)S(1)} %get-tuple-element.58), channel_id=1, source_target_pairs={{0,112},{16,0},{32,16},{48,32},{64,48},{80,64},{96,80},{112,96},{1... | collective-permute-start | bytes 995336 | tf_op jit(solution)/shard_map/ppermute | solution.py:28
  98.0 18.3 %collective-permute-start.13 = (bf16[144,1152]{1,0:T(8,128)(2,1)S(1)}, bf16[144,1152]{1,0:T(8,128)(2,1)S(1)}, u32[]{:S(2)}, u32[]{:S(2)}) collective-permute-start(bf16[144,1152]{1,0:T(8,128)(2,1)S(1)} %get-tuple-element.56), channel_id=1, source_target_pairs={{0,16},{16,32},{32,48},{48,64},{64,80},{80,96},{96,112},{112,0},{1... | collective-permute-start | bytes 995336 | tf_op jit(solution)/shard_map/ppermute | solution.py:28
  98.0 13.7 %collective-permute-start.31 = (bf16[128,512]{1,0:T(8,128)(2,1)S(1)}, bf16[128,512]{1,0:T(8,128)(2,1)S(1)}, u32[]{:S(2)}, u32[]{:S(2)}) collective-permute-start(bf16[128,512]{1,0:T(8,128)(2,1)S(1)} %collective-permute-done.29), channel_id=1, source_target_pairs={{0,16},{16,32},{32,48},{48,64},{64,80},{80,96},{96,112},{112,0},{1... | collective-permute-start | bytes 393224 | tf_op jit(solution)/shard_map/ppermute | solution.py:28
  98.7 19.8 %collective-permute-start.14 = (bf16[144,1152]{1,0:T(8,128)(2,1)S(1)}, bf16[144,1152]{1,0:T(8,128)(2,1)S(1)}, u32[]{:S(2)}, u32[]{:S(2)}) collective-permute-start(bf16[144,1152]{1,0:T(8,128)(2,1)S(1)} %get-tuple-element.56), channel_id=1, source_target_pairs={{0,112},{16,0},{32,16},{48,32},{64,48},{80,64},{96,80},{112,96},{1... | collective-permute-start | bytes 995336 | tf_op jit(solution)/shard_map/ppermute | solution.py:28
  112.4 37.0 %collective-permute-start.32 = (bf16[1024,512]{1,0:T(8,128)(2,1)}, bf16[1024,512]{1,0:T(8,128)(2,1)S(1)}, u32[]{:S(2)}, u32[]{:S(2)}) collective-permute-start(bf16[1024,512]{1,0:T(8,128)(2,1)} %constant_dynamic-update-slice_fusion), channel_id=1, source_target_pairs={{0,128},{16,144},{32,160},{48,176},{64,192},{80,208},{96,224},{112... | collective-permute-start | bytes 3145736 | tf_op jit(solution)/shard_map/ppermute | solution.py:32
  113.6 8.4 %collective-permute-start.15 = (bf16[144,1152]{1,0:T(8,128)(2,1)S(1)}, bf16[144,1152]{1,0:T(8,128)(2,1)S(1)}, u32[]{:S(2)}, u32[]{:S(2)}) collective-permute-start(bf16[144,1152]{1,0:T(8,128)(2,1)S(1)} %collective-permute-done.11), channel_id=1, source_target_pairs={{0,16},{16,32},{32,48},{48,64},{64,80},{80,96},{96,112},{112,0},{1... | collective-permute-start | bytes 995336 | tf_op jit(solution)/shard_map/ppermute | solution.py:28
  113.6 8.4 %collective-permute-start.16 = (bf16[144,1152]{1,0:T(8,128)(2,1)S(1)}, bf16[144,1152]{1,0:T(8,128)(2,1)S(1)}, u32[]{:S(2)}, u32[]{:S(2)}) collective-permute-start(bf16[144,1152]{1,0:T(8,128)(2,1)S(1)} %collective-permute-done.12), channel_id=1, source_target_pairs={{0,112},{16,0},{32,16},{48,32},{64,48},{80,64},{96,80},{112,96},{1... | collective-permute-start | bytes 995336 | tf_op jit(solution)/shard_map/ppermute | solution.py:28
  116.3 10.5 %collective-permute-start.17 = (bf16[144,1152]{1,0:T(8,128)(2,1)S(1)}, bf16[144,1152]{1,0:T(8,128)(2,1)S(1)}, u32[]{:S(2)}, u32[]{:S(2)}) collective-permute-start(bf16[144,1152]{1,0:T(8,128)(2,1)S(1)} %collective-permute-done.13), channel_id=1, source_target_pairs={{0,16},{16,32},{32,48},{48,64},{64,80},{80,96},{96,112},{112,0},{1... | collective-permute-start | bytes 995336 | tf_op jit(solution)/shard_map/ppermute | solution.py:28
  118.5 10.5 %collective-permute-start.18 = (bf16[144,1152]{1,0:T(8,128)(2,1)S(1)}, bf16[144,1152]{1,0:T(8,128)(2,1)S(1)}, u32[]{:S(2)}, u32[]{:S(2)}) collective-permute-start(bf16[144,1152]{1,0:T(8,128)(2,1)S(1)} %collective-permute-done.14), channel_id=1, source_target_pairs={{0,112},{16,0},{32,16},{48,32},{64,48},{80,64},{96,80},{112,96},{1... | collective-permute-start | bytes 995336 | tf_op jit(solution)/shard_map/ppermute | solution.py:28
  122.0 11.9 %collective-permute-start.19 = (bf16[144,1152]{1,0:T(8,128)(2,1)S(1)}, bf16[144,1152]{1,0:T(8,128)(2,1)S(1)}, u32[]{:S(2)}, u32[]{:S(2)}) collective-permute-start(bf16[144,1152]{1,0:T(8,128)(2,1)S(1)} %collective-permute-done.15), channel_id=1, source_target_pairs={{0,16},{16,32},{32,48},{48,64},{64,80},{80,96},{96,112},{112,0},{1... | collective-permute-start | bytes 995336 | tf_op jit(solution)/shard_map/ppermute | solution.py:28
  122.0 25.1 %collective-permute-start.20 = (bf16[144,1152]{1,0:T(8,128)(2,1)S(1)}, bf16[144,1152]{1,0:T(8,128)(2,1)S(1)}, u32[]{:S(2)}, u32[]{:S(2)}) collective-permute-start(bf16[144,1152]{1,0:T(8,128)(2,1)S(1)} %collective-permute-done.16), channel_id=1, source_target_pairs={{0,112},{16,0},{32,16},{48,32},{64,48},{80,64},{96,80},{112,96},{1... | collective-permute-start | bytes 995336 | tf_op jit(solution)/shard_map/ppermute | solution.py:28
  126.8 21.1 %collective-permute-start.21 = (bf16[144,1152]{1,0:T(8,128)(2,1)S(1)}, bf16[144,1152]{1,0:T(8,128)(2,1)S(1)}, u32[]{:S(2)}, u32[]{:S(2)}) collective-permute-start(bf16[144,1152]{1,0:T(8,128)(2,1)S(1)} %collective-permute-done.17), channel_id=1, source_target_pairs={{0,16},{16,32},{32,48},{48,64},{64,80},{80,96},{96,112},{112,0},{1... | collective-permute-start | bytes 995336 | tf_op jit(solution)/shard_map/ppermute | solution.py:28
  129.1 13.8 %collective-permute-start.22 = (bf16[144,1152]{1,0:T(8,128)(2,1)S(1)}, bf16[144,1152]{1,0:T(8,128)(2,1)S(1)}, u32[]{:S(2)}, u32[]{:S(2)}) collective-permute-start(bf16[144,1152]{1,0:T(8,128)(2,1)S(1)} %collective-permute-done.18), channel_id=1, source_target_pairs={{0,112},{16,0},{32,16},{48,32},{64,48},{80,64},{96,80},{112,96},{1... | collective-permute-start | bytes 995336 | tf_op jit(solution)/shard_map/ppermute | solution.py:28
  133.9 16.5 %collective-permute-start.23 = (bf16[144,1152]{1,0:T(8,128)(2,1)S(1)}, bf16[144,1152]{1,0:T(8,128)(2,1)S(1)}, u32[]{:S(2)}, u32[]{:S(2)}) collective-permute-start(bf16[144,1152]{1,0:T(8,128)(2,1)S(1)} %collective-permute-done.19), channel_id=1, source_target_pairs={{0,16},{16,32},{32,48},{48,64},{64,80},{80,96},{96,112},{112,0},{1... | collective-permute-start | bytes 995336 | tf_op jit(solution)/shard_map/ppermute | solution.py:28
  142.9 8.2 %collective-permute-start.24 = (bf16[144,1152]{1,0:T(8,128)(2,1)S(1)}, bf16[144,1152]{1,0:T(8,128)(2,1)S(1)}, u32[]{:S(2)}, u32[]{:S(2)}) collective-permute-start(bf16[144,1152]{1,0:T(8,128)(2,1)S(1)} %collective-permute-done.22), channel_id=1, source_target_pairs={{0,112},{16,0},{32,16},{48,32},{64,48},{80,64},{96,80},{112,96},{1... | collective-permute-start | bytes 995336 | tf_op jit(solution)/shard_map/ppermute | solution.py:28
  149.4 1.0 copy-start.6
  158.0 4.4 %copy-start.7 = (bf16[1024,512]{1,0:T(8,128)(2,1)S(1)}, bf16[1024,512]{1,0:T(8,128)(2,1)}, u32[]{:S(2)}) copy-start(bf16[1024,512]{1,0:T(8,128)(2,1)} %copy-done.6) | copy-start | bytes 3145732
  158.0 31.7 %all-to-all-start = ((bf16[8,288,256]{2,1,0:T(8,128)(2,1)}), bf16[8,288,256]{2,1,0:T(8,128)(2,1)S(1)}, u32[]{:S(2)}, u32[]{:S(2)}) async-start(bf16[8,288,256]{2,1,0:T(8,128)(2,1)} %bitcast.134), calls=%async_computation | async-start | bytes 2359296 | tf_op jit(solution)/shard_map/all_to_all | solution.py:36
  189.7 1.3 copy-start.1
  210.8 2.5 %copy-start = (bf16[2,1152,1152]{2,1,0:T(8,128)(2,1)S(1)}, bf16[2,1152,1152]{2,1,0:T(8,128)(2,1)}, u32[]{:S(2)}) copy-start(bf16[2,1152,1152]{2,1,0:T(8,128)(2,1)} %bitcast_dynamic-update-slice_fusion.blocks) | copy-start | bytes 15925252
  213.3 17.9 %copy-start.4 = (bf16[1,4608,64]{1,2,0:T(8,128)(2,1)S(1)}, bf16[1,4608,64]{1,2,0:T(8,128)(2,1)}, u32[]{:S(2)}) copy-start(bf16[1,4608,64]{1,2,0:T(8,128)(2,1)} %param.6) | copy-start | bytes 1769476
  213.3 17.9 %copy-start.5 = (f32[1,4608,64]{1,2,0:T(8,128)S(1)}, f32[1,4608,64]{1,2,0:T(8,128)}, u32[]{:S(2)}) copy-start(f32[1,4608,64]{1,2,0:T(8,128)} %param.7) | copy-start | bytes 3538948
  215.6 27.1 %all-to-all-start.2 = ((f32[256,1,128]{2,1,0:T(1,128)}), f32[256,1,128]{2,1,0:T(1,128)S(1)}, u32[]{:S(2)}, u32[]{:S(2)}) async-start(f32[256,1,128]{2,1,0:T(1,128)} %bitcast.60), calls=%async_computation.2 | async-start | bytes 262144 | tf_op jit(solution)/shard_map/all_to_all | solution.py:290
  229.7 13.0 %collective-permute-start.33 = (bf16[2,64,1152]{2,1,0:T(8,128)(2,1)S(1)}, bf16[2,64,1152]{2,1,0:T(8,128)(2,1)S(1)}, u32[]{:S(2)}, u32[]{:S(2)}) collective-permute-start(bf16[2,64,1152]{2,1,0:T(8,128)(2,1)S(1)} %get-tuple-element.36), channel_id=1, source_target_pairs={{0,128},{16,144},{32,160},{48,176},{64,192},{80,208},{96,224},{112... | collective-permute-start | bytes 884744 | tf_op jit(solution)/shard_map/ppermute | solution.py:32

commit v4 on v3

--- a/solution.py
+++ b/solution.py
@@ -63,7 +63,8 @@
     return pl.pallas_call(
         lambda out: None,
         out_shape=jax.ShapeDtypeStruct(shape, dtype),
-        out_specs=pl.BlockSpec(memory_space=pl.ANY),
+        out_specs=pl.BlockSpec(memory_space=pltpu.VMEM),
+        compiler_params=pltpu.CompilerParams(vmem_limit_bytes=8 * 1024 * 1024),
     )()
 
 
@@ -233,7 +234,7 @@
         right_slots[0, 0].reshape(RING, SIDES * cols, width),
     )
     eighths = unset((RING, piece, BLK), jnp.bfloat16)
-    for step in (0, 4, 3, 5, 2, 6, 1, 7):
+    for step in (0, 1, 7, 4, 3, 5, 2, 6):
         part = pieces[step]
         if step:
             part = ring_shift(part, step)
@@ -269,7 +270,7 @@
     right_half = ring_gather([right_chunk], z)[0]
     blocks = ring_gather(chunk, z)
     right_other = cross(right_half)
-    (both,) = after([both], [right_other])
+    both, right_other = lax.optimization_barrier((both, right_other))
     right_all = jnp.where(
         first,
         jnp.concatenate([right_half, right_other], 1),

time: 245 us -> 241 us (0.984)
  waiting for transfers between devices: 88.5 us -> 82.1 us
    ppermute x28, waiting for transfers between devices: 50.2 us -> 45.2 us  [ring_shift(): return lax.ppermute(value, 'shard', pairs)]
    unnamed x24 -> x20, local copies, waits for them, and re-layouts: 6.51 us -> 6.76 us
  transfers between devices with their start and end apart: 36 -> 36, of which waited for: 13 -> 14; matrix products, arithmetic and copies ran while one was open for 12% -> 13% of each run, Pallas kernels for 0% -> 0%
where the time goes in v4:
time: 241 us; the launch traced here: 240 us
  waiting for transfers between devices  82.1 us (34%)
  starting transfers between devices  72.5 us (30%)
  local copies, waits for them, and re-layouts  32.9 us (14%)
  blocking collectives  15.2 us (6%)
  between operations  12.4 us (5%)
  other arithmetic  10.7 us (4%)
  Pallas kernels  8.83 us (4%)
  matrix products  5.8 us (2%)
    ppermute x28, starting transfers between devices, ring_shift(): return lax.ppermute(value, 'shard', pairs)  46.3 us
    ppermute x28, waiting for transfers between devices, ring_shift(): return lax.ppermute(value, 'shard', pairs)  45.2 us
    all_to_all x1, waiting for transfers between devices, ring_all_to_all(): return lax.all_to_all(value, 'shard', 0, 0, axis_index_groups=rings())  24.4 us
    dynamic_update_slice x21, local copies, waits for them, and re-layouts, put(): lax.dynamic_update_slice(whole, piece[None], (i, (place + RING) % RING *...  15.2 us
    all_to_all x1, blocking collectives, ring_all_to_all(): return lax.all_to_all(value, 'shard', 0, 0, axis_index_groups=rings())  15.2 us
    all_to_all x1, starting transfers between devices, body(): sums = lax.all_to_all(sums, ('shard', 'layer'), 0, 0)  14.7 us
    all_to_all x1, waiting for transfers between devices, body(): sums = lax.all_to_all(sums, ('shard', 'layer'), 0, 0)  10.3 us
    ppermute x6, starting transfers between devices, cross(): lax.ppermute(value, 'shard', [(s, (s + RING) % (RING * SIDES)) for s in r...  7.04 us
  transfers between devices with their start and end apart: 36, of which 14 were waited for; matrix products, arithmetic and copies ran while one was open for 13% of the time, Pallas kernels for 0%

profile of v4, /device:TPU:1, one launch (start us, length us, event | category | flops | bytes accessed | tf_op | source)
XLA Modules:
  0.0 240.4 jit_solution(9240099125029171726)
XLA Ops:
  1.3 4.0 %shard_map.92 = (bf16[8,144,1152]{2,1,0:T(8,128)(2,1)S(1)}, bf16[144,1152]{1,0:T(8,128)(2,1)}, bf16[144,1152]{1,0:T(8,128)(2,1)}, bf16[144,1152]{1,0:T(8,128)(2,...) fusion(bf16[8,144,1152]{2,1,0:T(8,128)(2,1)S(1)} %shard_map.86,, ...), kind=kCustom, calls=%fused_computation.43 | custom fusion | bytes 7406084 | tf_op jit(solution)/shard_map/pallas_call | solution.py:100
  5.3 2.5 %collective-permute-start = (bf16[144,1152]{1,0:T(8,128)(2,1)}, bf16[144,1152]{1,0:T(8,128)(2,1)}, u32[]{:S(2)}, u32[]{:S(2)}) collective-permute-start(bf16[144,1152]{1,0:T(8,128)(2,1)} %get-tuple-element.44), channel_id=1, source_target_pairs={{0,16},{16,32},{32,48},{48,64},{64,80},{80,96},{96,112},{112,0},{1... | collective-permute-start | bytes 995336 | tf_op jit(solution)/shard_map/ppermute | solution.py:28
  7.7 3.9 %collective-permute-start.1 = (bf16[144,1152]{1,0:T(8,128)(2,1)}, bf16[144,1152]{1,0:T(8,128)(2,1)}, u32[]{:S(2)}, u32[]{:S(2)}) collective-permute-start(bf16[144,1152]{1,0:T(8,128)(2,1)} %get-tuple-element.46), channel_id=1, source_target_pairs={{0,112},{16,0},{32,16},{48,32},{64,48},{80,64},{96,80},{112,96},{1... | collective-permute-start | bytes 995336 | tf_op jit(solution)/shard_map/ppermute | solution.py:28
  11.7 4.0 %collective-permute-start.2 = (bf16[144,1152]{1,0:T(8,128)(2,1)}, bf16[144,1152]{1,0:T(8,128)(2,1)}, u32[]{:S(2)}, u32[]{:S(2)}) collective-permute-start(bf16[144,1152]{1,0:T(8,128)(2,1)} %get-tuple-element.48), channel_id=1, source_target_pairs={{0,64},{16,80},{32,96},{48,112},{64,0},{80,16},{96,32},{112,48},{1... | collective-permute-start | bytes 995336 | tf_op jit(solution)/shard_map/ppermute | solution.py:28
  16.1 4.0 %collective-permute-start.4 = (bf16[144,1152]{1,0:T(8,128)(2,1)}, bf16[144,1152]{1,0:T(8,128)(2,1)}, u32[]{:S(2)}, u32[]{:S(2)}) collective-permute-start(bf16[144,1152]{1,0:T(8,128)(2,1)} %get-tuple-element.52), channel_id=1, source_target_pairs={{0,80},{16,96},{32,112},{48,0},{64,16},{80,32},{96,48},{112,64},{1... | collective-permute-start | bytes 995336 | tf_op jit(solution)/shard_map/ppermute | solution.py:28
  20.2 2.4 copy-done
  29.7 1.0 shard_map.88
  32.5 2.3 fusion.1
  38.0 1.2 fusion.2
  39.3 1.0 bitcast_dynamic-update-slice_fusion.22
  40.4 3.6 %collective-permute-start.6 = (bf16[144,1152]{1,0:T(8,128)(2,1)S(1)}, bf16[144,1152]{1,0:T(8,128)(2,1)S(1)}, u32[]{:S(2)}, u32[]{:S(2)}) collective-permute-start(bf16[144,1152]{1,0:T(8,128)(2,1)S(1)} %copy-done.8), channel_id=1, source_target_pairs={{0,96},{16,112},{32,0},{48,16},{64,32},{80,48},{96,64},{112,80},{1... | collective-permute-start | bytes 995336 | tf_op jit(solution)/shard_map/ppermute | solution.py:28
  44.0 1.0 bitcast_dynamic-update-slice_fusion.21
  45.0 1.4 collective-permute-start.7
  46.4 1.0 bitcast_dynamic-update-slice_fusion.20
  47.4 6.5 %collective-permute-done.3 = bf16[144,1152]{1,0:T(8,128)(2,1)} collective-permute-done((bf16[144,1152]{1,0:T(8,128)(2,1)}, bf16[144,1152]{1,0:T(8,128)(2,1)}, u32[]{:S(2)}, u32[]{:S(2)}) %collective-permute-start.3) | collective-permute-done | bytes 331808 | tf_op jit(solution)/shard_map/ppermute | solution.py:28
  53.9 1.0 bitcast_dynamic-update-slice_fusion.19
  54.9 4.3 %collective-permute-done.4 = bf16[144,1152]{1,0:T(8,128)(2,1)} collective-permute-done((bf16[144,1152]{1,0:T(8,128)(2,1)}, bf16[144,1152]{1,0:T(8,128)(2,1)}, u32[]{:S(2)}, u32[]{:S(2)}) %collective-permute-start.4) | collective-permute-done | bytes 331808 | tf_op jit(solution)/shard_map/ppermute | solution.py:28
  59.3 1.0 bitcast_dynamic-update-slice_fusion.18
  60.3 3.7 %collective-permute-done.5 = bf16[144,1152]{1,0:T(8,128)(2,1)S(1)} collective-permute-done((bf16[144,1152]{1,0:T(8,128)(2,1)}, bf16[144,1152]{1,0:T(8,128)(2,1)S(1)}, u32[]{:S(2)}, u32[]{:S(2)}) %collective-permute-start.5) | collective-permute-done | bytes 331808 | tf_op jit(solution)/shard_map/ppermute | solution.py:28
  64.0 6.2 %collective-permute-done.6 = bf16[144,1152]{1,0:T(8,128)(2,1)S(1)} collective-permute-done((bf16[144,1152]{1,0:T(8,128)(2,1)S(1)}, bf16[144,1152]{1,0:T(8,128)(2,1)S(1)}, u32[]{:S(2)}, u32[]{:S(2)}) %collective-permute-start.6) | collective-permute-done | bytes 331808 | tf_op jit(solution)/shard_map/ppermute | solution.py:28
  70.2 0.9 dynamic-slice_bitcast_fusion
  71.2 1.4 collective-permute-start.8
  72.9 2.2 collective-permute-done.8.refs_2_
  76.2 2.3 collective-permute-start.26
  78.5 1.1 pad_maximum_fusion.2
  79.6 1.3 collective-permute-start.9
  81.4 2.4 %collective-permute-start.28 = (bf16[128,512]{1,0:T(8,128)(2,1)S(1)}, bf16[128,512]{1,0:T(8,128)(2,1)S(1)}, u32[]{:S(2)}, u32[]{:S(2)}) collective-permute-start(bf16[128,512]{1,0:T(8,128)(2,1)S(1)} %collective-permute-done.26), channel_id=1, source_target_pairs={{0,112},{16,0},{32,16},{48,32},{64,48},{80,64},{96,80},{112,96},{1... | collective-permute-start | bytes 393224 | tf_op jit(solution)/shard_map/ppermute | solution.py:28
  85.1 1.0 collective-permute-done.27
  86.3 2.5 %collective-permute-start.30 = (bf16[128,512]{1,0:T(8,128)(2,1)S(1)}, bf16[128,512]{1,0:T(8,128)(2,1)S(1)}, u32[]{:S(2)}, u32[]{:S(2)}) collective-permute-start(bf16[128,512]{1,0:T(8,128)(2,1)S(1)} %collective-permute-done.28), channel_id=1, source_target_pairs={{0,112},{16,0},{32,16},{48,32},{64,48},{80,64},{96,80},{112,96},{1... | collective-permute-start | bytes 393224 | tf_op jit(solution)/shard_map/ppermute | solution.py:28
  90.2 0.8 bitcast_dynamic-update-slice_fusion.15
  91.0 2.7 %collective-permute-start.12 = (bf16[144,1152]{1,0:T(8,128)(2,1)S(1)}, bf16[144,1152]{1,0:T(8,128)(2,1)S(1)}, u32[]{:S(2)}, u32[]{:S(2)}) collective-permute-start(bf16[144,1152]{1,0:T(8,128)(2,1)S(1)} %get-tuple-element.62), channel_id=1, source_target_pairs={{0,112},{16,0},{32,16},{48,32},{64,48},{80,64},{96,80},{112,96},{1... | collective-permute-start | bytes 995336 | tf_op jit(solution)/shard_map/ppermute | solution.py:28
  93.6 0.8 bitcast_dynamic-update-slice_fusion.14
  95.9 2.0 collective-permute-start.14
  98.5 10.0 %collective-permute-done.31 = bf16[128,512]{1,0:T(8,128)(2,1)S(1)} collective-permute-done((bf16[128,512]{1,0:T(8,128)(2,1)S(1)}, bf16[128,512]{1,0:T(8,128)(2,1)S(1)}, u32[]{:S(2)}, u32[]{:S(2)}) %collective-permute-start.31) | collective-permute-done | bytes 131104 | tf_op jit(solution)/shard_map/ppermute | solution.py:28
  109.2 1.3 collective-permute-start.32
  110.5 2.7 %collective-permute-start.16 = (bf16[144,1152]{1,0:T(8,128)(2,1)S(1)}, bf16[144,1152]{1,0:T(8,128)(2,1)S(1)}, u32[]{:S(2)}, u32[]{:S(2)}) collective-permute-start(bf16[144,1152]{1,0:T(8,128)(2,1)S(1)} %collective-permute-done.12), channel_id=1, source_target_pairs={{0,112},{16,0},{32,16},{48,32},{64,48},{80,64},{96,80},{112,96},{1... | collective-permute-start | bytes 995336 | tf_op jit(solution)/shard_map/ppermute | solution.py:28
  113.9 0.8 bitcast_dynamic-update-slice_fusion.12
  114.7 0.8 bitcast_dynamic-update-slice_fusion.11
  115.5 2.7 %collective-permute-start.18 = (bf16[144,1152]{1,0:T(8,128)(2,1)S(1)}, bf16[144,1152]{1,0:T(8,128)(2,1)S(1)}, u32[]{:S(2)}, u32[]{:S(2)}) collective-permute-start(bf16[144,1152]{1,0:T(8,128)(2,1)S(1)} %collective-permute-done.14), channel_id=1, source_target_pairs={{0,112},{16,0},{32,16},{48,32},{64,48},{80,64},{96,80},{112,96},{1... | collective-permute-start | bytes 995336 | tf_op jit(solution)/shard_map/ppermute | solution.py:28
  118.9 2.7 %collective-permute-start.20 = (bf16[144,1152]{1,0:T(8,128)(2,1)S(1)}, bf16[144,1152]{1,0:T(8,128)(2,1)S(1)}, u32[]{:S(2)}, u32[]{:S(2)}) collective-permute-start(bf16[144,1152]{1,0:T(8,128)(2,1)S(1)} %collective-permute-done.16), channel_id=1, source_target_pairs={{0,112},{16,0},{32,16},{48,32},{64,48},{80,64},{96,80},{112,96},{1... | collective-permute-start | bytes 995336 | tf_op jit(solution)/shard_map/ppermute | solution.py:28
  121.6 1.1 collective-permute-done.17
  122.7 0.8 bitcast_dynamic-update-slice_fusion.9
  124.2 0.8 bitcast_dynamic-update-slice_fusion.7
  124.9 3.0 %collective-permute-start.22 = (bf16[144,1152]{1,0:T(8,128)(2,1)S(1)}, bf16[144,1152]{1,0:T(8,128)(2,1)S(1)}, u32[]{:S(2)}, u32[]{:S(2)}) collective-permute-start(bf16[144,1152]{1,0:T(8,128)(2,1)S(1)} %collective-permute-done.18), channel_id=1, source_target_pairs={{0,112},{16,0},{32,16},{48,32},{64,48},{80,64},{96,80},{112,96},{1... | collective-permute-start | bytes 995336 | tf_op jit(solution)/shard_map/ppermute | solution.py:28
  128.7 1.3 collective-permute-done.19
  130.0 8.7 %collective-permute-done.22 = bf16[144,1152]{1,0:T(8,128)(2,1)S(1)} collective-permute-done((bf16[144,1152]{1,0:T(8,128)(2,1)S(1)}, bf16[144,1152]{1,0:T(8,128)(2,1)S(1)}, u32[]{:S(2)}, u32[]{:S(2)}) %collective-permute-start.22) | collective-permute-done | bytes 331808 | tf_op jit(solution)/shard_map/ppermute | solution.py:28
  138.8 3.4 %collective-permute-start.24 = (bf16[144,1152]{1,0:T(8,128)(2,1)S(1)}, bf16[144,1152]{1,0:T(8,128)(2,1)S(1)}, u32[]{:S(2)}, u32[]{:S(2)}) collective-permute-start(bf16[144,1152]{1,0:T(8,128)(2,1)S(1)} %collective-permute-done.22), channel_id=1, source_target_pairs={{0,112},{16,0},{32,16},{48,32},{64,48},{80,64},{96,80},{112,96},{1... | collective-permute-start | bytes 995336 | tf_op jit(solution)/shard_map/ppermute | solution.py:28
  142.9 0.8 bitcast_dynamic-update-slice_fusion.4
  143.7 0.8 bitcast_dynamic-update-slice_fusion.3
  146.0 2.1 collective-permute-done.24
  148.9 5.8 %convolution_convert_fusion = bf16[2,1152,256]{2,1,0:T(8,128)(2,1)} fusion(bf16[2,1152,1152]{2,1,0:T(8,128)(2,1)} %bitcast_dynamic-update-slice_fusion.blocks, bf16[2,256,1152]{2,1,0:T(8,128)(2,1)S(1)} %copy-done.6), kind=kOutput, calls=%fused_computation | convolution fusion | flops 1359544320 | bytes 7667712 | tf_op jit(solution)/shard_map/bkr,bck->brc/dot_general | solution.py:282
  154.7 4.4 %all-to-all-start = ((bf16[8,288,256]{2,1,0:T(8,128)(2,1)}), bf16[8,288,256]{2,1,0:T(8,128)(2,1)S(1)}, u32[]{:S(2)}, u32[]{:S(2)}) async-start(bf16[8,288,256]{2,1,0:T(8,128)(2,1)} %bitcast.51), calls=%async_computation | async-start | bytes 2359296 | tf_op jit(solution)/shard_map/all_to_all | solution.py:36
  159.1 2.1 pad_maximum_fusion
  161.4 24.4 %all-to-all-done.values = bf16[8,288,256]{2,1,0:T(8,128)(2,1)S(1)} async-done(((bf16[8,288,256]{2,1,0:T(8,128)(2,1)}), bf16[8,288,256]{2,1,0:T(8,128)(2,1)S(1)}, u32[]{:S(2)}, u32[]{:S(2)}) %all-to-all-start) | async-done | bytes 1179680 | tf_op jit(solution)/shard_map/all_to_all | solution.py:36
  185.8 1.3 copy-done.2
  187.1 4.4 %shard_map.89 = (f32[288,1024]{1,0:T(8,128)}, bf16[8,288,128]{2,1,0:T(8,128)(2,1)S(1)}) custom-call(bf16[8,288,256]{2,1,0:T(8,128)(2,1)S(1)} %all-to-all-done.values, bf16[1024,1024]{1,0:T(8,128)(2,1)S(1)} %bitcast.125, f32[288,1024]{1,0:T(8,128)S(1)} %bitcast.127), custom_call_target="tpu_custom_call" | custom-call | tf_op jit(solution)/shard_map/pallas_call | solution.py:204
  191.5 15.2 %all_to_all.21 = bf16[8,288,128]{2,1,0:T(8,128)(2,1)S(1)} all-to-all(bf16[8,288,128]{2,1,0:T(8,128)(2,1)S(1)} %get-tuple-element.37), channel_id=1, replica_groups={{0,16,32,48,64,80,96,112},{128,144,160,176,192,208,224,240},{1,17,33,49..., dimensions={0} | all-to-all | bytes 1179648 | tf_op jit(solution)/shard_map/all_to_all | solution.py:36
  206.7 2.5 %copy-done.1 = bf16[2,1152,1152]{2,1,0:T(8,128)(2,1)S(1)} copy-done((bf16[2,1152,1152]{2,1,0:T(8,128)(2,1)S(1)}, bf16[2,1152,1152]{2,1,0:T(8,128)(2,1)}, u32[]{:S(2)}) %copy-start.1) | copy-done | bytes 5308440
  209.2 2.3 shard_map.90
  211.5 14.7 %all-to-all-start.2 = ((f32[256,1,128]{2,1,0:T(1,128)}), f32[256,1,128]{2,1,0:T(1,128)S(1)}, u32[]{:S(2)}, u32[]{:S(2)}) async-start(f32[256,1,128]{2,1,0:T(1,128)} %bitcast.60), calls=%async_computation.2 | async-start | bytes 262144 | tf_op jit(solution)/shard_map/all_to_all | solution.py:291
  226.2 1.5 collective-permute-start.33
  227.7 1.2 multiply_add_fusion
  228.9 10.3 %all-to-all-done.2 = f32[256,1,128]{2,1,0:T(1,128)S(1)} async-done(((f32[256,1,128]{2,1,0:T(1,128)}), f32[256,1,128]{2,1,0:T(1,128)S(1)}, u32[]{:S(2)}, u32[]{:S(2)}) %all-to-all-start.2) | async-done | bytes 131104 | tf_op jit(solution)/shard_map/all_to_all | solution.py:291
  239.3 1.1 shard_map.91
  (82 shorter events, 15.6 us)
Async XLA Ops:
  0.6 0.7 copy-start.9
  5.3 34.0 %collective-permute-start = (bf16[144,1152]{1,0:T(8,128)(2,1)}, bf16[144,1152]{1,0:T(8,128)(2,1)}, u32[]{:S(2)}, u32[]{:S(2)}) collective-permute-start(bf16[144,1152]{1,0:T(8,128)(2,1)} %get-tuple-element.44), channel_id=1, source_target_pairs={{0,16},{16,32},{32,48},{48,64},{64,80},{80,96},{96,112},{112,0},{1... | collective-permute-start | bytes 995336 | tf_op jit(solution)/shard_map/ppermute | solution.py:28
  7.7 32.6 %collective-permute-start.1 = (bf16[144,1152]{1,0:T(8,128)(2,1)}, bf16[144,1152]{1,0:T(8,128)(2,1)}, u32[]{:S(2)}, u32[]{:S(2)}) collective-permute-start(bf16[144,1152]{1,0:T(8,128)(2,1)} %get-tuple-element.46), channel_id=1, source_target_pairs={{0,112},{16,0},{32,16},{48,32},{64,48},{80,64},{96,80},{112,96},{1... | collective-permute-start | bytes 995336 | tf_op jit(solution)/shard_map/ppermute | solution.py:28
  11.7 33.3 %collective-permute-start.2 = (bf16[144,1152]{1,0:T(8,128)(2,1)}, bf16[144,1152]{1,0:T(8,128)(2,1)}, u32[]{:S(2)}, u32[]{:S(2)}) collective-permute-start(bf16[144,1152]{1,0:T(8,128)(2,1)} %get-tuple-element.48), channel_id=1, source_target_pairs={{0,64},{16,80},{32,96},{48,112},{64,0},{80,16},{96,32},{112,48},{1... | collective-permute-start | bytes 995336 | tf_op jit(solution)/shard_map/ppermute | solution.py:28
  15.7 38.2 %collective-permute-start.3 = (bf16[144,1152]{1,0:T(8,128)(2,1)}, bf16[144,1152]{1,0:T(8,128)(2,1)}, u32[]{:S(2)}, u32[]{:S(2)}) collective-permute-start(bf16[144,1152]{1,0:T(8,128)(2,1)} %get-tuple-element.50), channel_id=1, source_target_pairs={{0,48},{16,64},{32,80},{48,96},{64,112},{80,0},{96,16},{112,32},{1... | collective-permute-start | bytes 995336 | tf_op jit(solution)/shard_map/ppermute | solution.py:28
  16.1 16.4 %copy-start.3 = (bf16[1,4608,64]{1,2,0:T(8,128)(2,1)S(1)}, bf16[1,4608,64]{1,2,0:T(8,128)(2,1)}, u32[]{:S(2)}) copy-start(bf16[1,4608,64]{1,2,0:T(8,128)(2,1)} %param.6) | copy-start | bytes 1769476
  16.1 43.1 %collective-permute-start.4 = (bf16[144,1152]{1,0:T(8,128)(2,1)}, bf16[144,1152]{1,0:T(8,128)(2,1)}, u32[]{:S(2)}, u32[]{:S(2)}) collective-permute-start(bf16[144,1152]{1,0:T(8,128)(2,1)} %get-tuple-element.52), channel_id=1, source_target_pairs={{0,80},{16,96},{32,112},{48,0},{64,16},{80,32},{96,48},{112,64},{1... | collective-permute-start | bytes 995336 | tf_op jit(solution)/shard_map/ppermute | solution.py:28
  20.2 2.4 copy-start
  38.0 2.3 copy-start.8
  39.2 24.7 %collective-permute-start.5 = (bf16[144,1152]{1,0:T(8,128)(2,1)}, bf16[144,1152]{1,0:T(8,128)(2,1)S(1)}, u32[]{:S(2)}, u32[]{:S(2)}) collective-permute-start(bf16[144,1152]{1,0:T(8,128)(2,1)} %get-tuple-element.54), channel_id=1, source_target_pairs={{0,32},{16,48},{32,64},{48,80},{64,96},{80,112},{96,0},{112,16},{1... | collective-permute-start | bytes 995336 | tf_op jit(solution)/shard_map/ppermute | solution.py:28
  40.4 29.8 %collective-permute-start.6 = (bf16[144,1152]{1,0:T(8,128)(2,1)S(1)}, bf16[144,1152]{1,0:T(8,128)(2,1)S(1)}, u32[]{:S(2)}, u32[]{:S(2)}) collective-permute-start(bf16[144,1152]{1,0:T(8,128)(2,1)S(1)} %copy-done.8), channel_id=1, source_target_pairs={{0,96},{16,112},{32,0},{48,16},{64,32},{80,48},{96,64},{112,80},{1... | collective-permute-start | bytes 995336 | tf_op jit(solution)/shard_map/ppermute | solution.py:28
  45.0 25.2 %collective-permute-start.7 = (bf16[2,64,2304]{2,1,0:T(8,128)(2,1)S(1)}, bf16[2,64,2304]{2,1,0:T(8,128)(2,1)S(1)}, u32[]{:S(2)}, u32[]{:S(2)}) collective-permute-start(bf16[2,64,2304]{2,1,0:T(8,128)(2,1)S(1)} %get-tuple-element.71), channel_id=1, source_target_pairs={{0,128},{16,144},{32,160},{48,176},{64,192},{80,208},{96,224},{112... | collective-permute-start | bytes 1769480 | tf_op jit(solution)/shard_map/ppermute | solution.py:32
  71.2 3.9 %collective-permute-start.8 = (bf16[128,512]{1,0:T(8,128)(2,1)S(1)}, bf16[128,512]{1,0:T(8,128)(2,1)S(1)}, u32[]{:S(2)}, u32[]{:S(2)}) collective-permute-start(bf16[128,512]{1,0:T(8,128)(2,1)S(1)} %constant_dynamic-slice_fusion), channel_id=1, source_target_pairs={{0,128},{16,144},{32,160},{48,176},{64,192},{80,208},{96,224},{112... | collective-permute-start | bytes 393224 | tf_op jit(solution)/shard_map/ppermute | solution.py:32
  75.1 4.5 %copy-start.7 = (bf16[128,512]{1,0:T(8,128)(2,1)}, bf16[128,512]{1,0:T(8,128)(2,1)S(1)}, u32[]{:S(2)}) copy-start(bf16[128,512]{1,0:T(8,128)(2,1)S(1)} %collective-permute-done.8.refs_2_) | copy-start | bytes 393220
  75.8 5.3 %collective-permute-start.25 = (bf16[128,512]{1,0:T(8,128)(2,1)S(1)}, bf16[128,512]{1,0:T(8,128)(2,1)S(1)}, u32[]{:S(2)}, u32[]{:S(2)}) collective-permute-start(bf16[128,512]{1,0:T(8,128)(2,1)S(1)} %get-tuple-element.58), channel_id=1, source_target_pairs={{0,16},{16,32},{32,48},{48,64},{64,80},{80,96},{96,112},{112,0},{1... | collective-permute-start | bytes 393224 | tf_op jit(solution)/shard_map/ppermute | solution.py:28
  76.2 5.1 %collective-permute-start.26 = (bf16[128,512]{1,0:T(8,128)(2,1)S(1)}, bf16[128,512]{1,0:T(8,128)(2,1)S(1)}, u32[]{:S(2)}, u32[]{:S(2)}) collective-permute-start(bf16[128,512]{1,0:T(8,128)(2,1)S(1)} %get-tuple-element.58), channel_id=1, source_target_pairs={{0,112},{16,0},{32,16},{48,32},{64,48},{80,64},{96,80},{112,96},{1... | collective-permute-start | bytes 393224 | tf_op jit(solution)/shard_map/ppermute | solution.py:28
  79.6 10.5 %collective-permute-start.9 = (bf16[144,1152]{1,0:T(8,128)(2,1)}, bf16[144,1152]{1,0:T(8,128)(2,1)S(1)}, u32[]{:S(2)}, u32[]{:S(2)}) collective-permute-start(bf16[144,1152]{1,0:T(8,128)(2,1)} %get-tuple-element.31), channel_id=1, source_target_pairs={{0,128},{16,144},{32,160},{48,176},{64,192},{80,208},{96,224},{112... | collective-permute-start | bytes 995336 | tf_op jit(solution)/shard_map/ppermute | solution.py:32
  80.9 12.7 %collective-permute-start.10 = (bf16[144,1152]{1,0:T(8,128)(2,1)}, bf16[144,1152]{1,0:T(8,128)(2,1)S(1)}, u32[]{:S(2)}, u32[]{:S(2)}) collective-permute-start(bf16[144,1152]{1,0:T(8,128)(2,1)} %get-tuple-element.32), channel_id=1, source_target_pairs={{0,128},{16,144},{32,160},{48,176},{64,192},{80,208},{96,224},{112... | collective-permute-start | bytes 995336 | tf_op jit(solution)/shard_map/ppermute | solution.py:32
  81.1 5.0 %collective-permute-start.27 = (bf16[128,512]{1,0:T(8,128)(2,1)S(1)}, bf16[128,512]{1,0:T(8,128)(2,1)S(1)}, u32[]{:S(2)}, u32[]{:S(2)}) collective-permute-start(bf16[128,512]{1,0:T(8,128)(2,1)S(1)} %collective-permute-done.25), channel_id=1, source_target_pairs={{0,16},{16,32},{32,48},{48,64},{64,80},{80,96},{96,112},{112,0},{1... | collective-permute-start | bytes 393224 | tf_op jit(solution)/shard_map/ppermute | solution.py:28
  81.4 4.9 %collective-permute-start.28 = (bf16[128,512]{1,0:T(8,128)(2,1)S(1)}, bf16[128,512]{1,0:T(8,128)(2,1)S(1)}, u32[]{:S(2)}, u32[]{:S(2)}) collective-permute-start(bf16[128,512]{1,0:T(8,128)(2,1)S(1)} %collective-permute-done.26), channel_id=1, source_target_pairs={{0,112},{16,0},{32,16},{48,32},{64,48},{80,64},{96,80},{112,96},{1... | collective-permute-start | bytes 393224 | tf_op jit(solution)/shard_map/ppermute | solution.py:28
  86.1 8.3 %collective-permute-start.29 = (bf16[128,512]{1,0:T(8,128)(2,1)S(1)}, bf16[128,512]{1,0:T(8,128)(2,1)S(1)}, u32[]{:S(2)}, u32[]{:S(2)}) collective-permute-start(bf16[128,512]{1,0:T(8,128)(2,1)S(1)} %collective-permute-done.27), channel_id=1, source_target_pairs={{0,16},{16,32},{32,48},{48,64},{64,80},{80,96},{96,112},{112,0},{1... | collective-permute-start | bytes 393224 | tf_op jit(solution)/shard_map/ppermute | solution.py:28
  86.3 9.6 %collective-permute-start.30 = (bf16[128,512]{1,0:T(8,128)(2,1)S(1)}, bf16[128,512]{1,0:T(8,128)(2,1)S(1)}, u32[]{:S(2)}, u32[]{:S(2)}) collective-permute-start(bf16[128,512]{1,0:T(8,128)(2,1)S(1)} %collective-permute-done.28), channel_id=1, source_target_pairs={{0,112},{16,0},{32,16},{48,32},{64,48},{80,64},{96,80},{112,96},{1... | collective-permute-start | bytes 393224 | tf_op jit(solution)/shard_map/ppermute | solution.py:28
  91.0 19.5 %collective-permute-start.11 = (bf16[144,1152]{1,0:T(8,128)(2,1)S(1)}, bf16[144,1152]{1,0:T(8,128)(2,1)S(1)}, u32[]{:S(2)}, u32[]{:S(2)}) collective-permute-start(bf16[144,1152]{1,0:T(8,128)(2,1)S(1)} %get-tuple-element.62), channel_id=1, source_target_pairs={{0,16},{16,32},{32,48},{48,64},{64,80},{80,96},{96,112},{112,0},{1... | collective-permute-start | bytes 995336 | tf_op jit(solution)/shard_map/ppermute | solution.py:28
  91.0 19.6 %collective-permute-start.12 = (bf16[144,1152]{1,0:T(8,128)(2,1)S(1)}, bf16[144,1152]{1,0:T(8,128)(2,1)S(1)}, u32[]{:S(2)}, u32[]{:S(2)}) collective-permute-start(bf16[144,1152]{1,0:T(8,128)(2,1)S(1)} %get-tuple-element.62), channel_id=1, source_target_pairs={{0,112},{16,0},{32,16},{48,32},{64,48},{80,64},{96,80},{112,96},{1... | collective-permute-start | bytes 995336 | tf_op jit(solution)/shard_map/ppermute | solution.py:28
  94.5 18.7 %collective-permute-start.13 = (bf16[144,1152]{1,0:T(8,128)(2,1)S(1)}, bf16[144,1152]{1,0:T(8,128)(2,1)S(1)}, u32[]{:S(2)}, u32[]{:S(2)}) collective-permute-start(bf16[144,1152]{1,0:T(8,128)(2,1)S(1)} %get-tuple-element.60), channel_id=1, source_target_pairs={{0,16},{16,32},{32,48},{48,64},{64,80},{80,96},{96,112},{112,0},{1... | collective-permute-start | bytes 995336 | tf_op jit(solution)/shard_map/ppermute | solution.py:28
  94.5 14.1 %collective-permute-start.31 = (bf16[128,512]{1,0:T(8,128)(2,1)S(1)}, bf16[128,512]{1,0:T(8,128)(2,1)S(1)}, u32[]{:S(2)}, u32[]{:S(2)}) collective-permute-start(bf16[128,512]{1,0:T(8,128)(2,1)S(1)} %collective-permute-done.29), channel_id=1, source_target_pairs={{0,16},{16,32},{32,48},{48,64},{64,80},{80,96},{96,112},{112,0},{1... | collective-permute-start | bytes 393224 | tf_op jit(solution)/shard_map/ppermute | solution.py:28
  95.9 19.6 %collective-permute-start.14 = (bf16[144,1152]{1,0:T(8,128)(2,1)S(1)}, bf16[144,1152]{1,0:T(8,128)(2,1)S(1)}, u32[]{:S(2)}, u32[]{:S(2)}) collective-permute-start(bf16[144,1152]{1,0:T(8,128)(2,1)S(1)} %get-tuple-element.60), channel_id=1, source_target_pairs={{0,112},{16,0},{32,16},{48,32},{64,48},{80,64},{96,80},{112,96},{1... | collective-permute-start | bytes 995336 | tf_op jit(solution)/shard_map/ppermute | solution.py:28
  109.2 36.0 %collective-permute-start.32 = (bf16[1024,512]{1,0:T(8,128)(2,1)}, bf16[1024,512]{1,0:T(8,128)(2,1)S(1)}, u32[]{:S(2)}, u32[]{:S(2)}) collective-permute-start(bf16[1024,512]{1,0:T(8,128)(2,1)} %constant_dynamic-update-slice_fusion), channel_id=1, source_target_pairs={{0,128},{16,144},{32,160},{48,176},{64,192},{80,208},{96,224},{112... | collective-permute-start | bytes 3145736 | tf_op jit(solution)/shard_map/ppermute | solution.py:32
  110.5 8.4 %collective-permute-start.15 = (bf16[144,1152]{1,0:T(8,128)(2,1)S(1)}, bf16[144,1152]{1,0:T(8,128)(2,1)S(1)}, u32[]{:S(2)}, u32[]{:S(2)}) collective-permute-start(bf16[144,1152]{1,0:T(8,128)(2,1)S(1)} %collective-permute-done.11), channel_id=1, source_target_pairs={{0,16},{16,32},{32,48},{48,64},{64,80},{80,96},{96,112},{112,0},{1... | collective-permute-start | bytes 995336 | tf_op jit(solution)/shard_map/ppermute | solution.py:28
  110.5 8.4 %collective-permute-start.16 = (bf16[144,1152]{1,0:T(8,128)(2,1)S(1)}, bf16[144,1152]{1,0:T(8,128)(2,1)S(1)}, u32[]{:S(2)}, u32[]{:S(2)}) collective-permute-start(bf16[144,1152]{1,0:T(8,128)(2,1)S(1)} %collective-permute-done.12), channel_id=1, source_target_pairs={{0,112},{16,0},{32,16},{48,32},{64,48},{80,64},{96,80},{112,96},{1... | collective-permute-start | bytes 995336 | tf_op jit(solution)/shard_map/ppermute | solution.py:28
  113.2 9.5 %collective-permute-start.17 = (bf16[144,1152]{1,0:T(8,128)(2,1)S(1)}, bf16[144,1152]{1,0:T(8,128)(2,1)S(1)}, u32[]{:S(2)}, u32[]{:S(2)}) collective-permute-start(bf16[144,1152]{1,0:T(8,128)(2,1)S(1)} %collective-permute-done.13), channel_id=1, source_target_pairs={{0,16},{16,32},{32,48},{48,64},{64,80},{80,96},{96,112},{112,0},{1... | collective-permute-start | bytes 995336 | tf_op jit(solution)/shard_map/ppermute | solution.py:28
  115.5 9.5 %collective-permute-start.18 = (bf16[144,1152]{1,0:T(8,128)(2,1)S(1)}, bf16[144,1152]{1,0:T(8,128)(2,1)S(1)}, u32[]{:S(2)}, u32[]{:S(2)}) collective-permute-start(bf16[144,1152]{1,0:T(8,128)(2,1)S(1)} %collective-permute-done.14), channel_id=1, source_target_pairs={{0,112},{16,0},{32,16},{48,32},{64,48},{80,64},{96,80},{112,96},{1... | collective-permute-start | bytes 995336 | tf_op jit(solution)/shard_map/ppermute | solution.py:28
  118.9 11.1 %collective-permute-start.19 = (bf16[144,1152]{1,0:T(8,128)(2,1)S(1)}, bf16[144,1152]{1,0:T(8,128)(2,1)S(1)}, u32[]{:S(2)}, u32[]{:S(2)}) collective-permute-start(bf16[144,1152]{1,0:T(8,128)(2,1)S(1)} %collective-permute-done.15), channel_id=1, source_target_pairs={{0,16},{16,32},{32,48},{48,64},{64,80},{80,96},{96,112},{112,0},{1... | collective-permute-start | bytes 995336 | tf_op jit(solution)/shard_map/ppermute | solution.py:28
  118.9 24.0 %collective-permute-start.20 = (bf16[144,1152]{1,0:T(8,128)(2,1)S(1)}, bf16[144,1152]{1,0:T(8,128)(2,1)S(1)}, u32[]{:S(2)}, u32[]{:S(2)}) collective-permute-start(bf16[144,1152]{1,0:T(8,128)(2,1)S(1)} %collective-permute-done.16), channel_id=1, source_target_pairs={{0,112},{16,0},{32,16},{48,32},{64,48},{80,64},{96,80},{112,96},{1... | collective-permute-start | bytes 995336 | tf_op jit(solution)/shard_map/ppermute | solution.py:28
  122.7 21.0 %collective-permute-start.21 = (bf16[144,1152]{1,0:T(8,128)(2,1)S(1)}, bf16[144,1152]{1,0:T(8,128)(2,1)S(1)}, u32[]{:S(2)}, u32[]{:S(2)}) collective-permute-start(bf16[144,1152]{1,0:T(8,128)(2,1)S(1)} %collective-permute-done.17), channel_id=1, source_target_pairs={{0,16},{16,32},{32,48},{48,64},{64,80},{80,96},{96,112},{112,0},{1... | collective-permute-start | bytes 995336 | tf_op jit(solution)/shard_map/ppermute | solution.py:28
  124.2 24.7 %copy-start.6 = (bf16[2,256,1152]{2,1,0:T(8,128)(2,1)S(1)}, bf16[2,256,1152]{2,1,0:T(8,128)(2,1)}, u32[]{:S(2)}) copy-start(bf16[2,256,1152]{2,1,0:T(8,128)(2,1)} %pad_maximum_fusion.2) | copy-start | bytes 3538948
  124.9 13.8 %collective-permute-start.22 = (bf16[144,1152]{1,0:T(8,128)(2,1)S(1)}, bf16[144,1152]{1,0:T(8,128)(2,1)S(1)}, u32[]{:S(2)}, u32[]{:S(2)}) collective-permute-start(bf16[144,1152]{1,0:T(8,128)(2,1)S(1)} %collective-permute-done.18), channel_id=1, source_target_pairs={{0,112},{16,0},{32,16},{48,32},{64,48},{80,64},{96,80},{112,96},{1... | collective-permute-start | bytes 995336 | tf_op jit(solution)/shard_map/ppermute | solution.py:28
  130.0 15.2 %collective-permute-start.23 = (bf16[144,1152]{1,0:T(8,128)(2,1)S(1)}, bf16[144,1152]{1,0:T(8,128)(2,1)S(1)}, u32[]{:S(2)}, u32[]{:S(2)}) collective-permute-start(bf16[144,1152]{1,0:T(8,128)(2,1)S(1)} %collective-permute-done.19), channel_id=1, source_target_pairs={{0,16},{16,32},{32,48},{48,64},{64,80},{80,96},{96,112},{112,0},{1... | collective-permute-start | bytes 995336 | tf_op jit(solution)/shard_map/ppermute | solution.py:28
  138.8 9.4 %collective-permute-start.24 = (bf16[144,1152]{1,0:T(8,128)(2,1)S(1)}, bf16[144,1152]{1,0:T(8,128)(2,1)S(1)}, u32[]{:S(2)}, u32[]{:S(2)}) collective-permute-start(bf16[144,1152]{1,0:T(8,128)(2,1)S(1)} %collective-permute-done.22), channel_id=1, source_target_pairs={{0,112},{16,0},{32,16},{48,32},{64,48},{80,64},{96,80},{112,96},{1... | collective-permute-start | bytes 995336 | tf_op jit(solution)/shard_map/ppermute | solution.py:28
  154.7 31.1 %all-to-all-start = ((bf16[8,288,256]{2,1,0:T(8,128)(2,1)}), bf16[8,288,256]{2,1,0:T(8,128)(2,1)S(1)}, u32[]{:S(2)}, u32[]{:S(2)}) async-start(bf16[8,288,256]{2,1,0:T(8,128)(2,1)} %bitcast.51), calls=%async_computation | async-start | bytes 2359296 | tf_op jit(solution)/shard_map/all_to_all | solution.py:36
  185.8 1.3 copy-start.2
  206.7 2.5 %copy-start.1 = (bf16[2,1152,1152]{2,1,0:T(8,128)(2,1)S(1)}, bf16[2,1152,1152]{2,1,0:T(8,128)(2,1)}, u32[]{:S(2)}) copy-start(bf16[2,1152,1152]{2,1,0:T(8,128)(2,1)} %bitcast_dynamic-update-slice_fusion.blocks) | copy-start | bytes 15925252
  209.2 18.6 %copy-start.4 = (bf16[1,4608,64]{1,2,0:T(8,128)(2,1)S(1)}, bf16[1,4608,64]{1,2,0:T(8,128)(2,1)}, u32[]{:S(2)}) copy-start(bf16[1,4608,64]{1,2,0:T(8,128)(2,1)} %param.6) | copy-start | bytes 1769476
  209.2 18.6 %copy-start.5 = (f32[1,4608,64]{1,2,0:T(8,128)S(1)}, f32[1,4608,64]{1,2,0:T(8,128)}, u32[]{:S(2)}) copy-start(f32[1,4608,64]{1,2,0:T(8,128)} %param.7) | copy-start | bytes 3538948
  211.5 27.8 %all-to-all-start.2 = ((f32[256,1,128]{2,1,0:T(1,128)}), f32[256,1,128]{2,1,0:T(1,128)S(1)}, u32[]{:S(2)}, u32[]{:S(2)}) async-start(f32[256,1,128]{2,1,0:T(1,128)} %bitcast.60), calls=%async_computation.2 | async-start | bytes 262144 | tf_op jit(solution)/shard_map/all_to_all | solution.py:291
  226.2 13.0 %collective-permute-start.33 = (bf16[2,64,1152]{2,1,0:T(8,128)(2,1)S(1)}, bf16[2,64,1152]{2,1,0:T(8,128)(2,1)S(1)}, u32[]{:S(2)}, u32[]{:S(2)}) collective-permute-start(bf16[2,64,1152]{2,1,0:T(8,128)(2,1)S(1)} %get-tuple-element.40), channel_id=1, source_target_pairs={{0,128},{16,144},{32,160},{48,176},{64,192},{80,208},{96,224},{112... | collective-permute-start | bytes 884744 | tf_op jit(solution)/shard_map/ppermute | solution.py:32

commit v5 on v4

--- a/solution.py
+++ b/solution.py
@@ -66,17 +66,6 @@
         out_specs=pl.BlockSpec(memory_space=pltpu.VMEM),
         compiler_params=pltpu.CompilerParams(vmem_limit_bytes=8 * 1024 * 1024),
     )()
-
-
-def after(values, ready):
-    count = len(values)
-    return pl.pallas_call(
-        lambda *refs: None,
-        out_shape=[jax.ShapeDtypeStruct(value.shape, value.dtype) for value in values],
-        in_specs=[pl.BlockSpec(memory_space=pl.ANY)] * (count + len(ready)),
-        out_specs=[pl.BlockSpec(memory_space=pl.ANY)] * count,
-        input_output_aliases={i: i for i in range(count)},
-    )(*values, *ready)
 
 
 def cut_kernel(owners, left, right, *pieces):
@@ -261,7 +250,7 @@
     took_right = cross(give_right)
     right_chunk = jnp.where(own_y[SIDES * count] == y, keep_right, took_right)
     give = [pick((1 - y) * count + i) for i in range(count)]
-    give = after(give, [took_right])
+    give, took_right = lax.optimization_barrier((give, took_right))
     took = [cross(value) for value in give]
     chunk = [
         jnp.where(own_y[y * count + i] == y, pick(y * count + i), took[i]) for i in range(count)

time: 241 us -> 232 us (0.963)
  local copies, waits for them, and re-layouts: 32.9 us -> 18.4 us
  waiting for transfers between devices: 82.1 us -> 91.2 us
  other arithmetic: 10.7 us -> 6.01 us
  starting transfers between devices: 72.5 us -> 76.5 us
  matrix products: 5.8 us -> 3.32 us
    dynamic_update_slice x21, local copies, waits for them, and re-layouts: 15.2 us -> 0.61 us  [put(): lax.dynamic_update_slice(whole, piece[None], (i, (place + RING) % RING *...]
    ppermute x28, waiting for transfers between devices: 45.2 us -> 55.4 us  [ring_shift(): return lax.ppermute(value, 'shard', pairs)]
    all_to_all x1, starting transfers between devices: 14.7 us -> 18.4 us  [body(): sums = lax.all_to_all(sums, ('shard', 'layer'), 0, 0)]
    dot_general x1, matrix products: 5.8 us -> 3.32 us  [body(): jnp.einsum('bkr,bck->brc', blocks, both, preferred_element_type=jnp.float32)]
    unnamed x20 -> x30, local copies, waits for them, and re-layouts: 6.76 us -> 7.75 us
  transfers between devices with their start and end apart: 36 -> 36, of which waited for: 14 -> 19; matrix products, arithmetic and copies ran while one was open for 13% -> 5% of each run, Pallas kernels for 0% -> 0%
where the time goes in v5:
time: 232 us; the launch traced here: 231 us
  waiting for transfers between devices  91.2 us (39%)
  starting transfers between devices  76.5 us (33%)
  local copies, waits for them, and re-layouts  18.4 us (8%)
  blocking collectives  15.2 us (7%)
  between operations  12.8 us (6%)
  Pallas kernels  7.86 us (3%)
  other arithmetic  6.01 us (3%)
  matrix products  3.32 us (1%)
    ppermute x28, waiting for transfers between devices, ring_shift(): return lax.ppermute(value, 'shard', pairs)  55.4 us
    ppermute x28, starting transfers between devices, ring_shift(): return lax.ppermute(value, 'shard', pairs)  46.3 us
    all_to_all x1, waiting for transfers between devices, ring_all_to_all(): return lax.all_to_all(value, 'shard', 0, 0, axis_index_groups=rings())  22.5 us
    all_to_all x1, starting transfers between devices, body(): sums = lax.all_to_all(sums, ('shard', 'layer'), 0, 0)  18.4 us
    all_to_all x1, blocking collectives, ring_all_to_all(): return lax.all_to_all(value, 'shard', 0, 0, axis_index_groups=rings())  15.2 us
    all_to_all x1, waiting for transfers between devices, body(): sums = lax.all_to_all(sums, ('shard', 'layer'), 0, 0)  10.3 us
    unnamed x30, local copies, waits for them, and re-layouts  7.75 us
    ppermute x6, starting transfers between devices, cross(): lax.ppermute(value, 'shard', [(s, (s + RING) % (RING * SIDES)) for s in r...  7.06 us
  transfers between devices with their start and end apart: 36, of which 19 were waited for; matrix products, arithmetic and copies ran while one was open for 5% of the time, Pallas kernels for 0%

profile of v5, /device:TPU:1, one launch (start us, length us, event | category | flops | bytes accessed | tf_op | source)
XLA Modules:
  0.0 231.4 jit_solution(7598861640591260181)
XLA Ops:
  0.7 0.6 copy-done.12
  1.3 4.0 %shard_map.91 = (bf16[8,144,1152]{2,1,0:T(8,128)(2,1)S(1)}, bf16[144,1152]{1,0:T(8,128)(2,1)}, bf16[144,1152]{1,0:T(8,128)(2,1)}, bf16[144,1152]{1,0:T(8,128)(2,...) fusion(bf16[8,144,1152]{2,1,0:T(8,128)(2,1)S(1)} %shard_map.86,, ...), kind=kCustom, calls=%fused_computation.43 | custom fusion | bytes 7406084 | tf_op jit(solution)/shard_map/pallas_call | solution.py:89
  5.3 2.5 %collective-permute-start = (bf16[144,1152]{1,0:T(8,128)(2,1)}, bf16[144,1152]{1,0:T(8,128)(2,1)}, u32[]{:S(2)}, u32[]{:S(2)}) collective-permute-start(bf16[144,1152]{1,0:T(8,128)(2,1)} %get-tuple-element.44), channel_id=1, source_target_pairs={{0,16},{16,32},{32,48},{48,64},{64,80},{80,96},{96,112},{112,0},{1... | collective-permute-start | bytes 995336 | tf_op jit(solution)/shard_map/ppermute | solution.py:28
  7.8 3.9 %collective-permute-start.1 = (bf16[144,1152]{1,0:T(8,128)(2,1)}, bf16[144,1152]{1,0:T(8,128)(2,1)}, u32[]{:S(2)}, u32[]{:S(2)}) collective-permute-start(bf16[144,1152]{1,0:T(8,128)(2,1)} %get-tuple-element.46), channel_id=1, source_target_pairs={{0,112},{16,0},{32,16},{48,32},{64,48},{80,64},{96,80},{112,96},{1... | collective-permute-start | bytes 995336 | tf_op jit(solution)/shard_map/ppermute | solution.py:28
  11.7 4.0 %collective-permute-start.2 = (bf16[144,1152]{1,0:T(8,128)(2,1)}, bf16[144,1152]{1,0:T(8,128)(2,1)}, u32[]{:S(2)}, u32[]{:S(2)}) collective-permute-start(bf16[144,1152]{1,0:T(8,128)(2,1)} %get-tuple-element.48), channel_id=1, source_target_pairs={{0,64},{16,80},{32,96},{48,112},{64,0},{80,16},{96,32},{112,48},{1... | collective-permute-start | bytes 995336 | tf_op jit(solution)/shard_map/ppermute | solution.py:28
  15.7 0.4 collective-permute-start.3
  16.1 4.0 %collective-permute-start.4 = (bf16[144,1152]{1,0:T(8,128)(2,1)}, bf16[144,1152]{1,0:T(8,128)(2,1)}, u32[]{:S(2)}, u32[]{:S(2)}) collective-permute-start(bf16[144,1152]{1,0:T(8,128)(2,1)} %get-tuple-element.52), channel_id=1, source_target_pairs={{0,80},{16,96},{32,112},{48,0},{64,16},{80,32},{96,48},{112,64},{1... | collective-permute-start | bytes 995336 | tf_op jit(solution)/shard_map/ppermute | solution.py:28
  20.2 2.4 %copy-done = bf16[2,1152,1152]{2,1,0:T(8,128)(2,1)} copy-done((bf16[2,1152,1152]{2,1,0:T(8,128)(2,1)}, bf16[2,1152,1152]{2,1,0:T(8,128)(2,1)S(1)}, u32[]{:S(2)}) %copy-start) | copy-done | bytes 5308440
  22.6 0.7 fusion.13
  29.7 1.0 copy-done.3
  32.7 2.3 fusion.1
  38.2 1.2 fusion.2
  39.5 1.0 bitcast_dynamic-update-slice_fusion.22
  40.5 3.6 %collective-permute-start.6 = (bf16[144,1152]{1,0:T(8,128)(2,1)S(1)}, bf16[144,1152]{1,0:T(8,128)(2,1)S(1)}, u32[]{:S(2)}, u32[]{:S(2)}) collective-permute-start(bf16[144,1152]{1,0:T(8,128)(2,1)S(1)} %copy-done.11), channel_id=1, source_target_pairs={{0,96},{16,112},{32,0},{48,16},{64,32},{80,48},{96,64},{112,80},{1... | collective-permute-start | bytes 995336 | tf_op jit(solution)/shard_map/ppermute | solution.py:28
  44.2 1.0 bitcast_dynamic-update-slice_fusion.21
  45.2 1.4 collective-permute-start.7
  46.6 1.0 bitcast_dynamic-update-slice_fusion.20
  47.6 6.3 %collective-permute-done.3 = bf16[144,1152]{1,0:T(8,128)(2,1)} collective-permute-done((bf16[144,1152]{1,0:T(8,128)(2,1)}, bf16[144,1152]{1,0:T(8,128)(2,1)}, u32[]{:S(2)}, u32[]{:S(2)}) %collective-permute-start.3) | collective-permute-done | bytes 331808 | tf_op jit(solution)/shard_map/ppermute | solution.py:28
  53.9 1.0 bitcast_dynamic-update-slice_fusion.19
  54.9 4.4 %collective-permute-done.4 = bf16[144,1152]{1,0:T(8,128)(2,1)} collective-permute-done((bf16[144,1152]{1,0:T(8,128)(2,1)}, bf16[144,1152]{1,0:T(8,128)(2,1)}, u32[]{:S(2)}, u32[]{:S(2)}) %collective-permute-start.4) | collective-permute-done | bytes 331808 | tf_op jit(solution)/shard_map/ppermute | solution.py:28
  59.4 1.0 bitcast_dynamic-update-slice_fusion.18
  60.4 3.6 %collective-permute-done.5 = bf16[144,1152]{1,0:T(8,128)(2,1)S(1)} collective-permute-done((bf16[144,1152]{1,0:T(8,128)(2,1)}, bf16[144,1152]{1,0:T(8,128)(2,1)S(1)}, u32[]{:S(2)}, u32[]{:S(2)}) %collective-permute-start.5) | collective-permute-done | bytes 331808 | tf_op jit(solution)/shard_map/ppermute | solution.py:28
  64.0 6.3 %collective-permute-done.6 = bf16[144,1152]{1,0:T(8,128)(2,1)S(1)} collective-permute-done((bf16[144,1152]{1,0:T(8,128)(2,1)S(1)}, bf16[144,1152]{1,0:T(8,128)(2,1)S(1)}, u32[]{:S(2)}, u32[]{:S(2)}) %collective-permute-start.6) | collective-permute-done | bytes 331808 | tf_op jit(solution)/shard_map/ppermute | solution.py:28
  70.4 1.4 collective-permute-start.8
  72.1 2.2 collective-permute-done.8
  74.4 0.4 collective-permute-start.25
  74.8 2.3 collective-permute-start.26
  77.3 1.3 collective-permute-start.9
  78.8 0.7 collective-permute-done.25
  79.7 2.5 %collective-permute-start.28 = (bf16[128,512]{1,0:T(8,128)(2,1)S(1)}, bf16[128,512]{1,0:T(8,128)(2,1)S(1)}, u32[]{:S(2)}, u32[]{:S(2)}) collective-permute-start(bf16[128,512]{1,0:T(8,128)(2,1)S(1)} %collective-permute-done.26), channel_id=1, source_target_pairs={{0,112},{16,0},{32,16},{48,32},{64,48},{80,64},{96,80},{112,96},{1... | collective-permute-start | bytes 393224 | tf_op jit(solution)/shard_map/ppermute | solution.py:28
  82.2 2.3 collective-permute-done.27
  84.5 0.4 collective-permute-done.28
  84.9 2.3 collective-permute-start.30
  87.5 2.7 %collective-permute-start.12 = (bf16[144,1152]{1,0:T(8,128)(2,1)S(1)}, bf16[144,1152]{1,0:T(8,128)(2,1)S(1)}, u32[]{:S(2)}, u32[]{:S(2)}) collective-permute-start(bf16[144,1152]{1,0:T(8,128)(2,1)S(1)} %get-tuple-element.62), channel_id=1, source_target_pairs={{0,112},{16,0},{32,16},{48,32},{64,48},{80,64},{96,80},{112,96},{1... | collective-permute-start | bytes 995336 | tf_op jit(solution)/shard_map/ppermute | solution.py:28
  90.2 0.8 collective-permute-done.10
  91.2 0.9 collective-permute-start.31
  92.1 1.9 collective-permute-start.14
  94.0 11.0 %collective-permute-done.31 = bf16[128,512]{1,0:T(8,128)(2,1)S(1)} collective-permute-done((bf16[128,512]{1,0:T(8,128)(2,1)S(1)}, bf16[128,512]{1,0:T(8,128)(2,1)S(1)}, u32[]{:S(2)}, u32[]{:S(2)}) %collective-permute-start.31) | collective-permute-done | bytes 131104 | tf_op jit(solution)/shard_map/ppermute | solution.py:28
  105.1 1.3 collective-permute-start.32
  106.4 2.7 %collective-permute-start.16 = (bf16[144,1152]{1,0:T(8,128)(2,1)S(1)}, bf16[144,1152]{1,0:T(8,128)(2,1)S(1)}, u32[]{:S(2)}, u32[]{:S(2)}) collective-permute-start(bf16[144,1152]{1,0:T(8,128)(2,1)S(1)} %collective-permute-done.12), channel_id=1, source_target_pairs={{0,112},{16,0},{32,16},{48,32},{64,48},{80,64},{96,80},{112,96},{1... | collective-permute-start | bytes 995336 | tf_op jit(solution)/shard_map/ppermute | solution.py:28
  109.2 2.7 %collective-permute-start.18 = (bf16[144,1152]{1,0:T(8,128)(2,1)S(1)}, bf16[144,1152]{1,0:T(8,128)(2,1)S(1)}, u32[]{:S(2)}, u32[]{:S(2)}) collective-permute-start(bf16[144,1152]{1,0:T(8,128)(2,1)S(1)} %collective-permute-done.14), channel_id=1, source_target_pairs={{0,112},{16,0},{32,16},{48,32},{64,48},{80,64},{96,80},{112,96},{1... | collective-permute-start | bytes 995336 | tf_op jit(solution)/shard_map/ppermute | solution.py:28
  112.0 1.6 collective-permute-done.15
  113.6 2.7 %collective-permute-start.20 = (bf16[144,1152]{1,0:T(8,128)(2,1)S(1)}, bf16[144,1152]{1,0:T(8,128)(2,1)S(1)}, u32[]{:S(2)}, u32[]{:S(2)}) collective-permute-start(bf16[144,1152]{1,0:T(8,128)(2,1)S(1)} %collective-permute-done.16), channel_id=1, source_target_pairs={{0,112},{16,0},{32,16},{48,32},{64,48},{80,64},{96,80},{112,96},{1... | collective-permute-start | bytes 995336 | tf_op jit(solution)/shard_map/ppermute | solution.py:28
  116.2 1.8 collective-permute-done.17
  118.2 3.0 %collective-permute-start.22 = (bf16[144,1152]{1,0:T(8,128)(2,1)S(1)}, bf16[144,1152]{1,0:T(8,128)(2,1)S(1)}, u32[]{:S(2)}, u32[]{:S(2)}) collective-permute-start(bf16[144,1152]{1,0:T(8,128)(2,1)S(1)} %collective-permute-done.18), channel_id=1, source_target_pairs={{0,112},{16,0},{32,16},{48,32},{64,48},{80,64},{96,80},{112,96},{1... | collective-permute-start | bytes 995336 | tf_op jit(solution)/shard_map/ppermute | solution.py:28
  121.2 3.9 %collective-permute-done.19 = bf16[144,1152]{1,0:T(8,128)(2,1)S(1)} collective-permute-done((bf16[144,1152]{1,0:T(8,128)(2,1)S(1)}, bf16[144,1152]{1,0:T(8,128)(2,1)S(1)}, u32[]{:S(2)}, u32[]{:S(2)}) %collective-permute-start.19) | collective-permute-done | bytes 331808 | tf_op jit(solution)/shard_map/ppermute | solution.py:28
  125.1 6.1 %collective-permute-done.22 = bf16[144,1152]{1,0:T(8,128)(2,1)S(1)} collective-permute-done((bf16[144,1152]{1,0:T(8,128)(2,1)S(1)}, bf16[144,1152]{1,0:T(8,128)(2,1)S(1)}, u32[]{:S(2)}, u32[]{:S(2)}) %collective-permute-start.22) | collective-permute-done | bytes 331808 | tf_op jit(solution)/shard_map/ppermute | solution.py:28
  131.2 3.4 %collective-permute-start.24 = (bf16[144,1152]{1,0:T(8,128)(2,1)S(1)}, bf16[144,1152]{1,0:T(8,128)(2,1)S(1)}, u32[]{:S(2)}, u32[]{:S(2)}) collective-permute-start(bf16[144,1152]{1,0:T(8,128)(2,1)S(1)} %collective-permute-done.22), channel_id=1, source_target_pairs={{0,112},{16,0},{32,16},{48,32},{64,48},{80,64},{96,80},{112,96},{1... | collective-permute-start | bytes 995336 | tf_op jit(solution)/shard_map/ppermute | solution.py:28
  134.9 4.5 %collective-permute-done.23 = bf16[144,1152]{1,0:T(8,128)(2,1)S(1)} collective-permute-done((bf16[144,1152]{1,0:T(8,128)(2,1)S(1)}, bf16[144,1152]{1,0:T(8,128)(2,1)S(1)}, u32[]{:S(2)}, u32[]{:S(2)}) %collective-permute-start.23) | collective-permute-done | bytes 331808 | tf_op jit(solution)/shard_map/ppermute | solution.py:28
  139.4 2.3 collective-permute-done.24
  141.7 3.3 %convolution_convert_fusion = bf16[2,1152,256]{2,1,0:T(8,128)(2,1)} fusion(bf16[2,1152,1152]{2,1,0:T(8,128)(2,1)S(1)} %bitcast_dynamic-update-slice_fusion.blocks, bf16[2,256,1152]{2,1,0:T(8,128)(2,1)S(1)} %pad_maximum_fusion.2), kind=kOutput, calls=%fused_computation | convolution fusion | flops 1359544320 | bytes 7667712 | tf_op jit(solution)/shard_map/bkr,bck->brc/dot_general | solution.py:271
  145.1 4.8 %all-to-all-start = ((bf16[8,288,256]{2,1,0:T(8,128)(2,1)}), bf16[8,288,256]{2,1,0:T(8,128)(2,1)S(1)}, u32[]{:S(2)}, u32[]{:S(2)}) async-start(bf16[8,288,256]{2,1,0:T(8,128)(2,1)} %bitcast.137), calls=%async_computation | async-start | bytes 2359296 | tf_op jit(solution)/shard_map/all_to_all | solution.py:36
  149.9 0.5 pad_maximum_fusion
  150.7 22.5 %all-to-all-done.values = bf16[8,288,256]{2,1,0:T(8,128)(2,1)S(1)} async-done(((bf16[8,288,256]{2,1,0:T(8,128)(2,1)}), bf16[8,288,256]{2,1,0:T(8,128)(2,1)S(1)}, u32[]{:S(2)}, u32[]{:S(2)}) %all-to-all-start) | async-done | bytes 1179680 | tf_op jit(solution)/shard_map/all_to_all | solution.py:36
  173.1 1.3 copy-done.7
  174.4 4.4 %shard_map.88 = (f32[288,1024]{1,0:T(8,128)}, bf16[8,288,128]{2,1,0:T(8,128)(2,1)S(1)}) custom-call(bf16[8,288,256]{2,1,0:T(8,128)(2,1)S(1)} %all-to-all-done.values, bf16[1024,1024]{1,0:T(8,128)(2,1)S(1)} %bitcast.127, f32[288,1024]{1,0:T(8,128)S(1)} %bitcast.131), custom_call_target="tpu_custom_call" | custom-call | tf_op jit(solution)/shard_map/pallas_call | solution.py:193
  178.8 15.2 %all_to_all.21 = bf16[8,288,128]{2,1,0:T(8,128)(2,1)S(1)} all-to-all(bf16[8,288,128]{2,1,0:T(8,128)(2,1)S(1)} %get-tuple-element.37), channel_id=1, replica_groups={{0,16,32,48,64,80,96,112},{128,144,160,176,192,208,224,240},{1,17,33,49..., dimensions={0} | all-to-all | bytes 1179648 | tf_op jit(solution)/shard_map/all_to_all | solution.py:36
  194.0 2.5 %copy-done.2 = bf16[2,1152,1152]{2,1,0:T(8,128)(2,1)S(1)} copy-done((bf16[2,1152,1152]{2,1,0:T(8,128)(2,1)S(1)}, bf16[2,1152,1152]{2,1,0:T(8,128)(2,1)}, u32[]{:S(2)}) %copy-start.2) | copy-done | bytes 5308440
  196.5 2.3 %shard_map.89 = (f32[2,64,1152]{2,1,0:T(8,128)S(1)}, bf16[2,64,1152]{2,1,0:T(8,128)(2,1)S(1)}, f32[256,128]{1,0:T(8,128)}) custom-call(bf16[2,1152,128]{2,1,0:T(8,128)(2,1)S(1)} %bitcast.130, bf16[2,1152,1152]{2,1,0:T(8,128)(2,1)S(1)} %copy-done.2), custom_call_target="tpu_custom_call" | custom-call | tf_op jit(solution)/shard_map/pallas_call | solution.py:126
  198.8 18.4 %all-to-all-start.2 = ((f32[256,1,128]{2,1,0:T(1,128)}), f32[256,1,128]{2,1,0:T(1,128)S(1)}, u32[]{:S(2)}, u32[]{:S(2)}) async-start(f32[256,1,128]{2,1,0:T(1,128)} %bitcast.60), calls=%async_computation.2 | async-start | bytes 262144 | tf_op jit(solution)/shard_map/all_to_all | solution.py:280
  217.2 1.5 collective-permute-start.33
  218.7 1.2 multiply_add_fusion
  219.9 10.3 %all-to-all-done.2 = f32[256,1,128]{2,1,0:T(1,128)S(1)} async-done(((f32[256,1,128]{2,1,0:T(1,128)}), f32[256,1,128]{2,1,0:T(1,128)S(1)}, u32[]{:S(2)}, u32[]{:S(2)}) %all-to-all-start.2) | async-done | bytes 131104 | tf_op jit(solution)/shard_map/all_to_all | solution.py:280
  230.2 1.1 shard_map.90
  (92 shorter events, 2.5 us)
Async XLA Ops:
  0.6 0.7 copy-start.12
  5.3 34.1 %collective-permute-start = (bf16[144,1152]{1,0:T(8,128)(2,1)}, bf16[144,1152]{1,0:T(8,128)(2,1)}, u32[]{:S(2)}, u32[]{:S(2)}) collective-permute-start(bf16[144,1152]{1,0:T(8,128)(2,1)} %get-tuple-element.44), channel_id=1, source_target_pairs={{0,16},{16,32},{32,48},{48,64},{64,80},{80,96},{96,112},{112,0},{1... | collective-permute-start | bytes 995336 | tf_op jit(solution)/shard_map/ppermute | solution.py:28
  7.8 32.8 %collective-permute-start.1 = (bf16[144,1152]{1,0:T(8,128)(2,1)}, bf16[144,1152]{1,0:T(8,128)(2,1)}, u32[]{:S(2)}, u32[]{:S(2)}) collective-permute-start(bf16[144,1152]{1,0:T(8,128)(2,1)} %get-tuple-element.46), channel_id=1, source_target_pairs={{0,112},{16,0},{32,16},{48,32},{64,48},{80,64},{96,80},{112,96},{1... | collective-permute-start | bytes 995336 | tf_op jit(solution)/shard_map/ppermute | solution.py:28
  11.7 33.5 %collective-permute-start.2 = (bf16[144,1152]{1,0:T(8,128)(2,1)}, bf16[144,1152]{1,0:T(8,128)(2,1)}, u32[]{:S(2)}, u32[]{:S(2)}) collective-permute-start(bf16[144,1152]{1,0:T(8,128)(2,1)} %get-tuple-element.48), channel_id=1, source_target_pairs={{0,64},{16,80},{32,96},{48,112},{64,0},{80,16},{96,32},{112,48},{1... | collective-permute-start | bytes 995336 | tf_op jit(solution)/shard_map/ppermute | solution.py:28
  15.7 38.2 %collective-permute-start.3 = (bf16[144,1152]{1,0:T(8,128)(2,1)}, bf16[144,1152]{1,0:T(8,128)(2,1)}, u32[]{:S(2)}, u32[]{:S(2)}) collective-permute-start(bf16[144,1152]{1,0:T(8,128)(2,1)} %get-tuple-element.50), channel_id=1, source_target_pairs={{0,48},{16,64},{32,80},{48,96},{64,112},{80,0},{96,16},{112,32},{1... | collective-permute-start | bytes 995336 | tf_op jit(solution)/shard_map/ppermute | solution.py:28
  16.1 16.6 %copy-start.8 = (bf16[1,4608,64]{1,2,0:T(8,128)(2,1)S(1)}, bf16[1,4608,64]{1,2,0:T(8,128)(2,1)}, u32[]{:S(2)}) copy-start(bf16[1,4608,64]{1,2,0:T(8,128)(2,1)} %param.6) | copy-start | bytes 1769476
  16.1 43.2 %collective-permute-start.4 = (bf16[144,1152]{1,0:T(8,128)(2,1)}, bf16[144,1152]{1,0:T(8,128)(2,1)}, u32[]{:S(2)}, u32[]{:S(2)}) collective-permute-start(bf16[144,1152]{1,0:T(8,128)(2,1)} %get-tuple-element.52), channel_id=1, source_target_pairs={{0,80},{16,96},{32,112},{48,0},{64,16},{80,32},{96,48},{112,64},{1... | collective-permute-start | bytes 995336 | tf_op jit(solution)/shard_map/ppermute | solution.py:28
  20.2 2.4 %copy-start = (bf16[2,1152,1152]{2,1,0:T(8,128)(2,1)}, bf16[2,1152,1152]{2,1,0:T(8,128)(2,1)S(1)}, u32[]{:S(2)}) copy-start(bf16[2,1152,1152]{2,1,0:T(8,128)(2,1)S(1)} %shard_map.85) | copy-start | bytes 15925252
  29.7 1.0 copy-start.3
  38.2 2.3 %copy-start.11 = (bf16[144,1152]{1,0:T(8,128)(2,1)S(1)}, bf16[144,1152]{1,0:T(8,128)(2,1)}, u32[]{:S(2)}) copy-start(bf16[144,1152]{1,0:T(8,128)(2,1)} %get-tuple-element.56) | copy-start | bytes 995332
  39.4 24.5 %collective-permute-start.5 = (bf16[144,1152]{1,0:T(8,128)(2,1)}, bf16[144,1152]{1,0:T(8,128)(2,1)S(1)}, u32[]{:S(2)}, u32[]{:S(2)}) collective-permute-start(bf16[144,1152]{1,0:T(8,128)(2,1)} %get-tuple-element.54), channel_id=1, source_target_pairs={{0,32},{16,48},{32,64},{48,80},{64,96},{80,112},{96,0},{112,16},{1... | collective-permute-start | bytes 995336 | tf_op jit(solution)/shard_map/ppermute | solution.py:28
  40.5 29.7 %collective-permute-start.6 = (bf16[144,1152]{1,0:T(8,128)(2,1)S(1)}, bf16[144,1152]{1,0:T(8,128)(2,1)S(1)}, u32[]{:S(2)}, u32[]{:S(2)}) collective-permute-start(bf16[144,1152]{1,0:T(8,128)(2,1)S(1)} %copy-done.11), channel_id=1, source_target_pairs={{0,96},{16,112},{32,0},{48,16},{64,32},{80,48},{96,64},{112,80},{1... | collective-permute-start | bytes 995336 | tf_op jit(solution)/shard_map/ppermute | solution.py:28
  45.2 25.1 %collective-permute-start.7 = (bf16[2,64,2304]{2,1,0:T(8,128)(2,1)S(1)}, bf16[2,64,2304]{2,1,0:T(8,128)(2,1)S(1)}, u32[]{:S(2)}, u32[]{:S(2)}) collective-permute-start(bf16[2,64,2304]{2,1,0:T(8,128)(2,1)S(1)} %get-tuple-element.71), channel_id=1, source_target_pairs={{0,128},{16,144},{32,160},{48,176},{64,192},{80,208},{96,224},{112... | collective-permute-start | bytes 1769480 | tf_op jit(solution)/shard_map/ppermute | solution.py:32
  63.9 23.3 %slice-start = ((s8[5308416]{0:T(1024)(128)(4,1)}), s8[4194304]{0:T(1024)(128)(4,1)S(1)}, s32[]{:S(2)}) async-start(s8[5308416]{0:T(1024)(128)(4,1)} %bitcast.125), calls=%async_computation.3 | async-start | bytes 8388608
  70.4 4.0 %copy-start.4 = (bf16[1,1024,512]{2,1,0:T(8,128)(2,1)S(1)}, bf16[1,1024,512]{2,1,0:T(8,128)(2,1)}, u32[]{:S(2)}) copy-start(bf16[1,1024,512]{2,1,0:T(8,128)(2,1)} %copy-done.3) | copy-start | bytes 3145732
  70.4 3.9 %collective-permute-start.8 = (bf16[128,512]{1,0:T(8,128)(2,1)S(1)}, bf16[128,512]{1,0:T(8,128)(2,1)S(1)}, u32[]{:S(2)}, u32[]{:S(2)}) collective-permute-start(bf16[128,512]{1,0:T(8,128)(2,1)S(1)} %constant_dynamic-slice_fusion), channel_id=1, source_target_pairs={{0,128},{16,144},{32,160},{48,176},{64,192},{80,208},{96,224},{112... | collective-permute-start | bytes 393224 | tf_op jit(solution)/shard_map/ppermute | solution.py:32
  71.8 15.5 %slice-start.1 = ((s8[5308416]{0:T(1024)(128)(4,1)}), s8[1114112]{0:T(1024)(128)(4,1)S(1)}, s32[]{:S(2)}) async-start(s8[5308416]{0:T(1024)(128)(4,1)} %bitcast.125), calls=%async_computation.4 | async-start | bytes 2228224
  74.4 5.1 %collective-permute-start.25 = (bf16[128,512]{1,0:T(8,128)(2,1)S(1)}, bf16[128,512]{1,0:T(8,128)(2,1)S(1)}, u32[]{:S(2)}, u32[]{:S(2)}) collective-permute-start(bf16[128,512]{1,0:T(8,128)(2,1)S(1)} %get-tuple-element.58), channel_id=1, source_target_pairs={{0,16},{16,32},{32,48},{48,64},{64,80},{80,96},{96,112},{112,0},{1... | collective-permute-start | bytes 393224 | tf_op jit(solution)/shard_map/ppermute | solution.py:28
  74.8 4.9 %collective-permute-start.26 = (bf16[128,512]{1,0:T(8,128)(2,1)S(1)}, bf16[128,512]{1,0:T(8,128)(2,1)S(1)}, u32[]{:S(2)}, u32[]{:S(2)}) collective-permute-start(bf16[128,512]{1,0:T(8,128)(2,1)S(1)} %get-tuple-element.58), channel_id=1, source_target_pairs={{0,112},{16,0},{32,16},{48,32},{64,48},{80,64},{96,80},{112,96},{1... | collective-permute-start | bytes 393224 | tf_op jit(solution)/shard_map/ppermute | solution.py:28
  77.3 10.0 %collective-permute-start.9 = (bf16[144,1152]{1,0:T(8,128)(2,1)S(1)}, bf16[144,1152]{1,0:T(8,128)(2,1)S(1)}, u32[]{:S(2)}, u32[]{:S(2)}) collective-permute-start(bf16[144,1152]{1,0:T(8,128)(2,1)S(1)} %get-tuple-element.31), channel_id=1, source_target_pairs={{0,128},{16,144},{32,160},{48,176},{64,192},{80,208},{96,224},{112... | collective-permute-start | bytes 995336 | tf_op jit(solution)/shard_map/ppermute | solution.py:32
  78.6 12.3 %collective-permute-start.10 = (bf16[144,1152]{1,0:T(8,128)(2,1)S(1)}, bf16[144,1152]{1,0:T(8,128)(2,1)S(1)}, u32[]{:S(2)}, u32[]{:S(2)}) collective-permute-start(bf16[144,1152]{1,0:T(8,128)(2,1)S(1)} %get-tuple-element.32), channel_id=1, source_target_pairs={{0,128},{16,144},{32,160},{48,176},{64,192},{80,208},{96,224},{112... | collective-permute-start | bytes 995336 | tf_op jit(solution)/shard_map/ppermute | solution.py:32
  79.5 5.0 %collective-permute-start.27 = (bf16[128,512]{1,0:T(8,128)(2,1)S(1)}, bf16[128,512]{1,0:T(8,128)(2,1)S(1)}, u32[]{:S(2)}, u32[]{:S(2)}) collective-permute-start(bf16[128,512]{1,0:T(8,128)(2,1)S(1)} %collective-permute-done.25), channel_id=1, source_target_pairs={{0,16},{16,32},{32,48},{48,64},{64,80},{80,96},{96,112},{112,0},{1... | collective-permute-start | bytes 393224 | tf_op jit(solution)/shard_map/ppermute | solution.py:28
  79.7 5.2 %collective-permute-start.28 = (bf16[128,512]{1,0:T(8,128)(2,1)S(1)}, bf16[128,512]{1,0:T(8,128)(2,1)S(1)}, u32[]{:S(2)}, u32[]{:S(2)}) collective-permute-start(bf16[128,512]{1,0:T(8,128)(2,1)S(1)} %collective-permute-done.26), channel_id=1, source_target_pairs={{0,112},{16,0},{32,16},{48,32},{64,48},{80,64},{96,80},{112,96},{1... | collective-permute-start | bytes 393224 | tf_op jit(solution)/shard_map/ppermute | solution.py:28
  84.5 6.6 %collective-permute-start.29 = (bf16[128,512]{1,0:T(8,128)(2,1)S(1)}, bf16[128,512]{1,0:T(8,128)(2,1)S(1)}, u32[]{:S(2)}, u32[]{:S(2)}) collective-permute-start(bf16[128,512]{1,0:T(8,128)(2,1)S(1)} %collective-permute-done.27), channel_id=1, source_target_pairs={{0,16},{16,32},{32,48},{48,64},{64,80},{80,96},{96,112},{112,0},{1... | collective-permute-start | bytes 393224 | tf_op jit(solution)/shard_map/ppermute | solution.py:28
  84.9 7.2 %collective-permute-start.30 = (bf16[128,512]{1,0:T(8,128)(2,1)S(1)}, bf16[128,512]{1,0:T(8,128)(2,1)S(1)}, u32[]{:S(2)}, u32[]{:S(2)}) collective-permute-start(bf16[128,512]{1,0:T(8,128)(2,1)S(1)} %collective-permute-done.28), channel_id=1, source_target_pairs={{0,112},{16,0},{32,16},{48,32},{64,48},{80,64},{96,80},{112,96},{1... | collective-permute-start | bytes 393224 | tf_op jit(solution)/shard_map/ppermute | solution.py:28
  87.4 19.0 %collective-permute-start.11 = (bf16[144,1152]{1,0:T(8,128)(2,1)S(1)}, bf16[144,1152]{1,0:T(8,128)(2,1)S(1)}, u32[]{:S(2)}, u32[]{:S(2)}) collective-permute-start(bf16[144,1152]{1,0:T(8,128)(2,1)S(1)} %get-tuple-element.62), channel_id=1, source_target_pairs={{0,16},{16,32},{32,48},{48,64},{64,80},{80,96},{96,112},{112,0},{1... | collective-permute-start | bytes 995336 | tf_op jit(solution)/shard_map/ppermute | solution.py:28
  87.5 18.9 %collective-permute-start.12 = (bf16[144,1152]{1,0:T(8,128)(2,1)S(1)}, bf16[144,1152]{1,0:T(8,128)(2,1)S(1)}, u32[]{:S(2)}, u32[]{:S(2)}) collective-permute-start(bf16[144,1152]{1,0:T(8,128)(2,1)S(1)} %get-tuple-element.62), channel_id=1, source_target_pairs={{0,112},{16,0},{32,16},{48,32},{64,48},{80,64},{96,80},{112,96},{1... | collective-permute-start | bytes 995336 | tf_op jit(solution)/shard_map/ppermute | solution.py:28
  91.1 18.0 %collective-permute-start.13 = (bf16[144,1152]{1,0:T(8,128)(2,1)S(1)}, bf16[144,1152]{1,0:T(8,128)(2,1)S(1)}, u32[]{:S(2)}, u32[]{:S(2)}) collective-permute-start(bf16[144,1152]{1,0:T(8,128)(2,1)S(1)} %get-tuple-element.60), channel_id=1, source_target_pairs={{0,16},{16,32},{32,48},{48,64},{64,80},{80,96},{96,112},{112,0},{1... | collective-permute-start | bytes 995336 | tf_op jit(solution)/shard_map/ppermute | solution.py:28
  91.2 13.9 %collective-permute-start.31 = (bf16[128,512]{1,0:T(8,128)(2,1)S(1)}, bf16[128,512]{1,0:T(8,128)(2,1)S(1)}, u32[]{:S(2)}, u32[]{:S(2)}) collective-permute-start(bf16[128,512]{1,0:T(8,128)(2,1)S(1)} %collective-permute-done.29), channel_id=1, source_target_pairs={{0,16},{16,32},{32,48},{48,64},{64,80},{80,96},{96,112},{112,0},{1... | collective-permute-start | bytes 393224 | tf_op jit(solution)/shard_map/ppermute | solution.py:28
  92.1 17.1 %collective-permute-start.14 = (bf16[144,1152]{1,0:T(8,128)(2,1)S(1)}, bf16[144,1152]{1,0:T(8,128)(2,1)S(1)}, u32[]{:S(2)}, u32[]{:S(2)}) collective-permute-start(bf16[144,1152]{1,0:T(8,128)(2,1)S(1)} %get-tuple-element.60), channel_id=1, source_target_pairs={{0,112},{16,0},{32,16},{48,32},{64,48},{80,64},{96,80},{112,96},{1... | collective-permute-start | bytes 995336 | tf_op jit(solution)/shard_map/ppermute | solution.py:28
  105.1 16.1 %copy-start.5 = (bf16[1024,512]{1,0:T(8,128)(2,1)}, bf16[1024,512]{1,0:T(8,128)(2,1)S(1)}, u32[]{:S(2)}) copy-start(bf16[1024,512]{1,0:T(8,128)(2,1)S(1)} %constant_dynamic-update-slice_fusion) | copy-start | bytes 3145732
  105.1 29.7 %collective-permute-start.32 = (bf16[1024,512]{1,0:T(8,128)(2,1)S(1)}, bf16[1024,512]{1,0:T(8,128)(2,1)S(1)}, u32[]{:S(2)}, u32[]{:S(2)}) collective-permute-start(bf16[1024,512]{1,0:T(8,128)(2,1)S(1)} %constant_dynamic-update-slice_fusion), channel_id=1, source_target_pairs={{0,128},{16,144},{32,160},{48,176},{64,192},{80,208},{96,224},{112... | collective-permute-start | bytes 3145736 | tf_op jit(solution)/shard_map/ppermute | solution.py:32
  106.4 7.2 %collective-permute-start.15 = (bf16[144,1152]{1,0:T(8,128)(2,1)S(1)}, bf16[144,1152]{1,0:T(8,128)(2,1)S(1)}, u32[]{:S(2)}, u32[]{:S(2)}) collective-permute-start(bf16[144,1152]{1,0:T(8,128)(2,1)S(1)} %collective-permute-done.11), channel_id=1, source_target_pairs={{0,16},{16,32},{32,48},{48,64},{64,80},{80,96},{96,112},{112,0},{1... | collective-permute-start | bytes 995336 | tf_op jit(solution)/shard_map/ppermute | solution.py:28
  106.4 7.2 %collective-permute-start.16 = (bf16[144,1152]{1,0:T(8,128)(2,1)S(1)}, bf16[144,1152]{1,0:T(8,128)(2,1)S(1)}, u32[]{:S(2)}, u32[]{:S(2)}) collective-permute-start(bf16[144,1152]{1,0:T(8,128)(2,1)S(1)} %collective-permute-done.12), channel_id=1, source_target_pairs={{0,112},{16,0},{32,16},{48,32},{64,48},{80,64},{96,80},{112,96},{1... | collective-permute-start | bytes 995336 | tf_op jit(solution)/shard_map/ppermute | solution.py:28
  109.1 9.0 %collective-permute-start.17 = (bf16[144,1152]{1,0:T(8,128)(2,1)S(1)}, bf16[144,1152]{1,0:T(8,128)(2,1)S(1)}, u32[]{:S(2)}, u32[]{:S(2)}) collective-permute-start(bf16[144,1152]{1,0:T(8,128)(2,1)S(1)} %collective-permute-done.13), channel_id=1, source_target_pairs={{0,16},{16,32},{32,48},{48,64},{64,80},{80,96},{96,112},{112,0},{1... | collective-permute-start | bytes 995336 | tf_op jit(solution)/shard_map/ppermute | solution.py:28
  109.2 9.0 %collective-permute-start.18 = (bf16[144,1152]{1,0:T(8,128)(2,1)S(1)}, bf16[144,1152]{1,0:T(8,128)(2,1)S(1)}, u32[]{:S(2)}, u32[]{:S(2)}) collective-permute-start(bf16[144,1152]{1,0:T(8,128)(2,1)S(1)} %collective-permute-done.14), channel_id=1, source_target_pairs={{0,112},{16,0},{32,16},{48,32},{64,48},{80,64},{96,80},{112,96},{1... | collective-permute-start | bytes 995336 | tf_op jit(solution)/shard_map/ppermute | solution.py:28
  113.6 11.6 %collective-permute-start.19 = (bf16[144,1152]{1,0:T(8,128)(2,1)S(1)}, bf16[144,1152]{1,0:T(8,128)(2,1)S(1)}, u32[]{:S(2)}, u32[]{:S(2)}) collective-permute-start(bf16[144,1152]{1,0:T(8,128)(2,1)S(1)} %collective-permute-done.15), channel_id=1, source_target_pairs={{0,16},{16,32},{32,48},{48,64},{64,80},{80,96},{96,112},{112,0},{1... | collective-permute-start | bytes 995336 | tf_op jit(solution)/shard_map/ppermute | solution.py:28
  113.6 21.1 %collective-permute-start.20 = (bf16[144,1152]{1,0:T(8,128)(2,1)S(1)}, bf16[144,1152]{1,0:T(8,128)(2,1)S(1)}, u32[]{:S(2)}, u32[]{:S(2)}) collective-permute-start(bf16[144,1152]{1,0:T(8,128)(2,1)S(1)} %collective-permute-done.16), channel_id=1, source_target_pairs={{0,112},{16,0},{32,16},{48,32},{64,48},{80,64},{96,80},{112,96},{1... | collective-permute-start | bytes 995336 | tf_op jit(solution)/shard_map/ppermute | solution.py:28
  118.0 16.7 %collective-permute-start.21 = (bf16[144,1152]{1,0:T(8,128)(2,1)S(1)}, bf16[144,1152]{1,0:T(8,128)(2,1)S(1)}, u32[]{:S(2)}, u32[]{:S(2)}) collective-permute-start(bf16[144,1152]{1,0:T(8,128)(2,1)S(1)} %collective-permute-done.17), channel_id=1, source_target_pairs={{0,16},{16,32},{32,48},{48,64},{64,80},{80,96},{96,112},{112,0},{1... | collective-permute-start | bytes 995336 | tf_op jit(solution)/shard_map/ppermute | solution.py:28
  118.2 13.1 %collective-permute-start.22 = (bf16[144,1152]{1,0:T(8,128)(2,1)S(1)}, bf16[144,1152]{1,0:T(8,128)(2,1)S(1)}, u32[]{:S(2)}, u32[]{:S(2)}) collective-permute-start(bf16[144,1152]{1,0:T(8,128)(2,1)S(1)} %collective-permute-done.18), channel_id=1, source_target_pairs={{0,112},{16,0},{32,16},{48,32},{64,48},{80,64},{96,80},{112,96},{1... | collective-permute-start | bytes 995336 | tf_op jit(solution)/shard_map/ppermute | solution.py:28
  125.1 14.2 %collective-permute-start.23 = (bf16[144,1152]{1,0:T(8,128)(2,1)S(1)}, bf16[144,1152]{1,0:T(8,128)(2,1)S(1)}, u32[]{:S(2)}, u32[]{:S(2)}) collective-permute-start(bf16[144,1152]{1,0:T(8,128)(2,1)S(1)} %collective-permute-done.19), channel_id=1, source_target_pairs={{0,16},{16,32},{32,48},{48,64},{64,80},{80,96},{96,112},{112,0},{1... | collective-permute-start | bytes 995336 | tf_op jit(solution)/shard_map/ppermute | solution.py:28
  131.2 10.5 %collective-permute-start.24 = (bf16[144,1152]{1,0:T(8,128)(2,1)S(1)}, bf16[144,1152]{1,0:T(8,128)(2,1)S(1)}, u32[]{:S(2)}, u32[]{:S(2)}) collective-permute-start(bf16[144,1152]{1,0:T(8,128)(2,1)S(1)} %collective-permute-done.22), channel_id=1, source_target_pairs={{0,112},{16,0},{32,16},{48,32},{64,48},{80,64},{96,80},{112,96},{1... | collective-permute-start | bytes 995336 | tf_op jit(solution)/shard_map/ppermute | solution.py:28
  141.7 3.3 %copy-start.1 = (bf16[2,1152,1152]{2,1,0:T(8,128)(2,1)}, bf16[2,1152,1152]{2,1,0:T(8,128)(2,1)S(1)}, u32[]{:S(2)}) copy-start(bf16[2,1152,1152]{2,1,0:T(8,128)(2,1)S(1)} %bitcast_dynamic-update-slice_fusion.blocks) | copy-start | bytes 15925252
  145.1 4.8 %copy-start.6 = (bf16[1024,512]{1,0:T(8,128)(2,1)S(1)}, bf16[1024,512]{1,0:T(8,128)(2,1)}, u32[]{:S(2)}) copy-start(bf16[1024,512]{1,0:T(8,128)(2,1)} %copy-done.5) | copy-start | bytes 3145732
  145.1 28.1 %all-to-all-start = ((bf16[8,288,256]{2,1,0:T(8,128)(2,1)}), bf16[8,288,256]{2,1,0:T(8,128)(2,1)S(1)}, u32[]{:S(2)}, u32[]{:S(2)}) async-start(bf16[8,288,256]{2,1,0:T(8,128)(2,1)} %bitcast.137), calls=%async_computation | async-start | bytes 2359296 | tf_op jit(solution)/shard_map/all_to_all | solution.py:36
  173.1 1.3 copy-start.7
  194.0 2.5 %copy-start.2 = (bf16[2,1152,1152]{2,1,0:T(8,128)(2,1)S(1)}, bf16[2,1152,1152]{2,1,0:T(8,128)(2,1)}, u32[]{:S(2)}) copy-start(bf16[2,1152,1152]{2,1,0:T(8,128)(2,1)} %copy-done.1) | copy-start | bytes 15925252
  196.5 22.2 %copy-start.9 = (bf16[1,4608,64]{1,2,0:T(8,128)(2,1)S(1)}, bf16[1,4608,64]{1,2,0:T(8,128)(2,1)}, u32[]{:S(2)}) copy-start(bf16[1,4608,64]{1,2,0:T(8,128)(2,1)} %param.6) | copy-start | bytes 1769476
  196.5 22.2 %copy-start.10 = (f32[1,4608,64]{1,2,0:T(8,128)S(1)}, f32[1,4608,64]{1,2,0:T(8,128)}, u32[]{:S(2)}) copy-start(f32[1,4608,64]{1,2,0:T(8,128)} %param.7) | copy-start | bytes 3538948
  198.8 31.4 %all-to-all-start.2 = ((f32[256,1,128]{2,1,0:T(1,128)}), f32[256,1,128]{2,1,0:T(1,128)S(1)}, u32[]{:S(2)}, u32[]{:S(2)}) async-start(f32[256,1,128]{2,1,0:T(1,128)} %bitcast.60), calls=%async_computation.2 | async-start | bytes 262144 | tf_op jit(solution)/shard_map/all_to_all | solution.py:280
  217.2 13.0 %collective-permute-start.33 = (bf16[2,64,1152]{2,1,0:T(8,128)(2,1)S(1)}, bf16[2,64,1152]{2,1,0:T(8,128)(2,1)S(1)}, u32[]{:S(2)}, u32[]{:S(2)}) collective-permute-start(bf16[2,64,1152]{2,1,0:T(8,128)(2,1)S(1)} %get-tuple-element.40), channel_id=1, source_target_pairs={{0,128},{16,144},{32,160},{48,176},{64,192},{80,208},{96,224},{112... | collective-permute-start | bytes 884744 | tf_op jit(solution)/shard_map/ppermute | solution.py:32

commit v6 on v5

--- a/solution.py
+++ b/solution.py
@@ -98,63 +98,65 @@
     )(owners, left, right)
 
 
-def raw_kernel(values, blocks, mine, other, sums):
+def raw_kernel(i, values, blocks, before, mine, other, sums):
     y = lax.div(lax.axis_index("shard"), RING)
-    cols, order = mine.shape[1:]
+    cols, order = mine.shape
     step = order // 3
-    total = jnp.zeros((1, 128), jnp.float32)
-    for i in range(COUNT):
-        back = values[i].T
-        for j in range(3):
-            lanes = slice(j * step, (j + 1) * step)
-            raw = lax.dot_general(
-                back, blocks[i, lanes, :], (((1,), (1,)), ((), ())), preferred_element_type=jnp.float32
-            )
-            low = raw[:cols]
-            high = raw[cols:]
-            mine[i, :, lanes] = jnp.where(y == 0, low, high)
-            other[i, :, lanes] = jnp.where(y == 0, high, low).astype(jnp.bfloat16)
-            squares = jnp.sum(raw * raw, 0, keepdims=True)
-            for k in range(step // 128):
-                total += squares[:, k * 128 : (k + 1) * 128]
+    total = before[...]
+    back = values[i].T
+    for j in range(3):
+        lanes = slice(j * step, (j + 1) * step)
+        raw = lax.dot_general(
+            back, blocks[i, lanes, :], (((1,), (1,)), ((), ())), preferred_element_type=jnp.float32
+        )
+        low = raw[:cols]
+        high = raw[cols:]
+        mine[:, lanes] = jnp.where(y == 0, low, high)
+        other[:, lanes] = jnp.where(y == 0, high, low).astype(jnp.bfloat16)
+        squares = jnp.sum(raw * raw, 0, keepdims=True)
+        for k in range(step // 128):
+            total += squares[:, k * 128 : (k + 1) * 128]
     sums[...] = jnp.broadcast_to(total, sums.shape)
 
 
-def raw_stage(values, blocks, devices):
-    count, order, pairs = values.shape
+def raw_stage(i, values, blocks, before, copies):
+    _, order, pairs = values.shape
     cols = pairs // SIDES
     return pl.pallas_call(
-        raw_kernel,
+        functools.partial(raw_kernel, i),
         out_shape=(
-            jax.ShapeDtypeStruct((count, cols, order), jnp.float32),
-            jax.ShapeDtypeStruct((count, cols, order), jnp.bfloat16),
-            jax.ShapeDtypeStruct((devices, 128), jnp.float32),
+            jax.ShapeDtypeStruct((cols, order), jnp.float32),
+            jax.ShapeDtypeStruct((cols, order), jnp.bfloat16),
+            jax.ShapeDtypeStruct((copies, 128), jnp.float32),
         ),
         compiler_params=pltpu.CompilerParams(vmem_limit_bytes=24 * 1024 * 1024),
-    )(values, blocks)
-
-
-def clip_kernel(cells, sums, mine, other, out):
+    )(values, blocks, before)
+
+
+def clip_kernel(cells, sums, *refs):
+    mine = refs[:COUNT]
+    other = refs[COUNT : 2 * COUNT]
+    out = refs[2 * COUNT]
     y = lax.div(lax.axis_index("shard"), RING)
-    count, _, order = mine.shape
+    order = mine[0].shape[1]
     total = jnp.sum(jnp.sum(sums[...], 0, keepdims=True), 1, keepdims=True)
     factor = jnp.minimum(1.0, clip_limit / jnp.sqrt(total / cells + 1e-06))
-    for i in range(count):
-        own = factor * mine[i]
-        far = factor * other[i].astype(jnp.float32)
+    for i in range(COUNT):
+        own = factor * mine[i][...]
+        far = factor * other[i][...].astype(jnp.float32)
         low = slice(i * order, (i + 1) * order)
-        high = slice((count + i) * order, (count + i + 1) * order)
+        high = slice((COUNT + i) * order, (COUNT + i + 1) * order)
         out[:, low] = jnp.where(y == 0, own, far).astype(jnp.bfloat16)
         out[:, high] = jnp.where(y == 0, far, own).astype(jnp.bfloat16)
 
 
 def clip_stage(sums, mine, other, cells):
-    count, cols, order = mine.shape
+    cols, order = mine[0].shape
     return pl.pallas_call(
         functools.partial(clip_kernel, cells),
-        out_shape=jax.ShapeDtypeStruct((cols, SIDES * count * order), jnp.bfloat16),
+        out_shape=jax.ShapeDtypeStruct((cols, SIDES * COUNT * order), jnp.bfloat16),
         compiler_params=pltpu.CompilerParams(vmem_limit_bytes=24 * 1024 * 1024),
-    )(sums, mine, other)
+    )(sums, *mine, *other)
 
 
 def right_kernel(values, right, second, second_out, out, scaled):
@@ -275,8 +277,12 @@
     second_new, returning = right_stage(values, right_all, second[0])
     values = ring_all_to_all(returning).reshape(count, BLK, SIDES * cols)
     devices = lax.axis_size("shard") * lax.axis_size("layer")
-    raw_mine, raw_give, sums = raw_stage(values, blocks, devices)
-    raw_other = cross(raw_give)
+    raw_mine, raw_other = [], []
+    sums = jnp.zeros((1, 128), jnp.float32)
+    for i in range(count):
+        raw, give, sums = raw_stage(i, values, blocks, sums, 1 if i < count - 1 else devices)
+        raw_mine.append(raw)
+        raw_other.append(cross(give))
     sums = lax.all_to_all(sums, ("shard", "layer"), 0, 0)
     cells = lax.axis_size("layer") * grad.shape[0] * rows_all * cols * RING * SIDES
     direction = clip_stage(sums, raw_mine, raw_other, float(cells))

time: 232 us -> 232 us (level)
    all_to_all x1, waiting for transfers between devices: 10.3 us -> 4.43 us  [body(): sums = lax.all_to_all(sums, ('shard', 'layer'), 0, 0)]
    ppermute x6 -> x7, waiting for transfers between devices: 3 us -> 8.75 us  [cross(): lax.ppermute(value, 'shard', [(s, (s + RING) % (RING * SIDES)) for s in r...]
    ppermute x6 -> x7, starting transfers between devices: 7.06 us -> 7.32 us  [cross(): lax.ppermute(value, 'shard', [(s, (s + RING) % (RING * SIDES)) for s in r...]
  transfers between devices with their start and end apart: 36 -> 37, of which waited for: 19 -> 21; matrix products, arithmetic and copies ran while one was open for 5% -> 5% of each run, Pallas kernels for 0% -> 0%
where the time goes in v6:
time: 232 us
  waiting for transfers between devices  90.6 us (39%)
  starting transfers between devices  77.6 us (33%)
  local copies, waits for them, and re-layouts  18.4 us (8%)
  blocking collectives  15.2 us (7%)
  between operations  12.5 us (5%)
  Pallas kernels  8.03 us (3%)
  other arithmetic  6.01 us (3%)
  matrix products  3.32 us (1%)
    ppermute x28, waiting for transfers between devices, ring_shift(): return lax.ppermute(value, 'shard', pairs)  55.4 us
    ppermute x28, starting transfers between devices, ring_shift(): return lax.ppermute(value, 'shard', pairs)  46.2 us
    all_to_all x1, waiting for transfers between devices, ring_all_to_all(): return lax.all_to_all(value, 'shard', 0, 0, axis_index_groups=rings())  22 us
    all_to_all x1, starting transfers between devices, body(): sums = lax.all_to_all(sums, ('shard', 'layer'), 0, 0)  19.2 us
    all_to_all x1, blocking collectives, ring_all_to_all(): return lax.all_to_all(value, 'shard', 0, 0, axis_index_groups=rings())  15.2 us
    ppermute x7, waiting for transfers between devices, cross(): lax.ppermute(value, 'shard', [(s, (s + RING) % (RING * SIDES)) for s in r...  8.75 us
    unnamed x30, local copies, waits for them, and re-layouts  7.77 us
    ppermute x7, starting transfers between devices, cross(): lax.ppermute(value, 'shard', [(s, (s + RING) % (RING * SIDES)) for s in r...  7.32 us
  transfers between devices with their start and end apart: 37, of which 21 were waited for; matrix products, arithmetic and copies ran while one was open for 5% of the time, Pallas kernels for 0%

profile of v6, /device:TPU:1, one launch (start us, length us, event | category | flops | bytes accessed | tf_op | source)
XLA Modules:
  0.0 231.6 jit_solution(18409492700332675005)
XLA Ops:
  0.7 0.6 copy-done.12
  1.3 4.0 %shard_map.92 = (bf16[8,144,1152]{2,1,0:T(8,128)(2,1)S(1)}, bf16[144,1152]{1,0:T(8,128)(2,1)}, bf16[144,1152]{1,0:T(8,128)(2,1)}, bf16[144,1152]{1,0:T(8,128)(2,...) fusion(bf16[8,144,1152]{2,1,0:T(8,128)(2,1)S(1)} %shard_map.86,, ...), kind=kCustom, calls=%fused_computation.43 | custom fusion | bytes 7406084 | tf_op jit(solution)/shard_map/pallas_call | solution.py:89
  5.3 2.5 %collective-permute-start = (bf16[144,1152]{1,0:T(8,128)(2,1)}, bf16[144,1152]{1,0:T(8,128)(2,1)}, u32[]{:S(2)}, u32[]{:S(2)}) collective-permute-start(bf16[144,1152]{1,0:T(8,128)(2,1)} %get-tuple-element.50), channel_id=1, source_target_pairs={{0,16},{16,32},{32,48},{48,64},{64,80},{80,96},{96,112},{112,0},{1... | collective-permute-start | bytes 995336 | tf_op jit(solution)/shard_map/ppermute | solution.py:28
  7.7 3.9 %collective-permute-start.1 = (bf16[144,1152]{1,0:T(8,128)(2,1)}, bf16[144,1152]{1,0:T(8,128)(2,1)}, u32[]{:S(2)}, u32[]{:S(2)}) collective-permute-start(bf16[144,1152]{1,0:T(8,128)(2,1)} %get-tuple-element.52), channel_id=1, source_target_pairs={{0,112},{16,0},{32,16},{48,32},{64,48},{80,64},{96,80},{112,96},{1... | collective-permute-start | bytes 995336 | tf_op jit(solution)/shard_map/ppermute | solution.py:28
  11.7 4.0 %collective-permute-start.2 = (bf16[144,1152]{1,0:T(8,128)(2,1)}, bf16[144,1152]{1,0:T(8,128)(2,1)}, u32[]{:S(2)}, u32[]{:S(2)}) collective-permute-start(bf16[144,1152]{1,0:T(8,128)(2,1)} %get-tuple-element.54), channel_id=1, source_target_pairs={{0,64},{16,80},{32,96},{48,112},{64,0},{80,16},{96,32},{112,48},{1... | collective-permute-start | bytes 995336 | tf_op jit(solution)/shard_map/ppermute | solution.py:28
  16.1 4.0 %collective-permute-start.4 = (bf16[144,1152]{1,0:T(8,128)(2,1)}, bf16[144,1152]{1,0:T(8,128)(2,1)}, u32[]{:S(2)}, u32[]{:S(2)}) collective-permute-start(bf16[144,1152]{1,0:T(8,128)(2,1)} %get-tuple-element.58), channel_id=1, source_target_pairs={{0,80},{16,96},{32,112},{48,0},{64,16},{80,32},{96,48},{112,64},{1... | collective-permute-start | bytes 995336 | tf_op jit(solution)/shard_map/ppermute | solution.py:28
  20.2 2.4 %copy-done = bf16[2,1152,1152]{2,1,0:T(8,128)(2,1)} copy-done((bf16[2,1152,1152]{2,1,0:T(8,128)(2,1)}, bf16[2,1152,1152]{2,1,0:T(8,128)(2,1)S(1)}, u32[]{:S(2)}) %copy-start) | copy-done | bytes 5308440
  22.6 0.7 fusion.13
  29.5 1.0 copy-done.3
  32.4 2.3 fusion.1
  37.8 1.2 fusion.2
  39.1 1.0 bitcast_dynamic-update-slice_fusion.22
  40.2 3.6 %collective-permute-start.6 = (bf16[144,1152]{1,0:T(8,128)(2,1)S(1)}, bf16[144,1152]{1,0:T(8,128)(2,1)S(1)}, u32[]{:S(2)}, u32[]{:S(2)}) collective-permute-start(bf16[144,1152]{1,0:T(8,128)(2,1)S(1)} %copy-done.11), channel_id=1, source_target_pairs={{0,96},{16,112},{32,0},{48,16},{64,32},{80,48},{96,64},{112,80},{1... | collective-permute-start | bytes 995336 | tf_op jit(solution)/shard_map/ppermute | solution.py:28
  43.8 1.0 bitcast_dynamic-update-slice_fusion.21
  44.8 1.4 collective-permute-start.7
  46.2 1.0 bitcast_dynamic-update-slice_fusion.20
  47.2 6.7 %collective-permute-done.3 = bf16[144,1152]{1,0:T(8,128)(2,1)} collective-permute-done((bf16[144,1152]{1,0:T(8,128)(2,1)}, bf16[144,1152]{1,0:T(8,128)(2,1)}, u32[]{:S(2)}, u32[]{:S(2)}) %collective-permute-start.3) | collective-permute-done | bytes 331808 | tf_op jit(solution)/shard_map/ppermute | solution.py:28
  53.9 1.0 bitcast_dynamic-update-slice_fusion.19
  54.9 4.3 %collective-permute-done.4 = bf16[144,1152]{1,0:T(8,128)(2,1)} collective-permute-done((bf16[144,1152]{1,0:T(8,128)(2,1)}, bf16[144,1152]{1,0:T(8,128)(2,1)}, u32[]{:S(2)}, u32[]{:S(2)}) %collective-permute-start.4) | collective-permute-done | bytes 331808 | tf_op jit(solution)/shard_map/ppermute | solution.py:28
  59.3 1.0 bitcast_dynamic-update-slice_fusion.18
  60.3 3.7 %collective-permute-done.5 = bf16[144,1152]{1,0:T(8,128)(2,1)S(1)} collective-permute-done((bf16[144,1152]{1,0:T(8,128)(2,1)}, bf16[144,1152]{1,0:T(8,128)(2,1)S(1)}, u32[]{:S(2)}, u32[]{:S(2)}) %collective-permute-start.5) | collective-permute-done | bytes 331808 | tf_op jit(solution)/shard_map/ppermute | solution.py:28
  64.0 6.2 %collective-permute-done.6 = bf16[144,1152]{1,0:T(8,128)(2,1)S(1)} collective-permute-done((bf16[144,1152]{1,0:T(8,128)(2,1)S(1)}, bf16[144,1152]{1,0:T(8,128)(2,1)S(1)}, u32[]{:S(2)}, u32[]{:S(2)}) %collective-permute-start.6) | collective-permute-done | bytes 331808 | tf_op jit(solution)/shard_map/ppermute | solution.py:28
  70.4 1.4 collective-permute-start.8
  72.1 2.2 collective-permute-done.8
  74.8 2.3 collective-permute-start.26
  77.2 1.4 collective-permute-start.9
  78.8 0.7 collective-permute-done.25
  79.7 2.4 %collective-permute-start.28 = (bf16[128,512]{1,0:T(8,128)(2,1)S(1)}, bf16[128,512]{1,0:T(8,128)(2,1)S(1)}, u32[]{:S(2)}, u32[]{:S(2)}) collective-permute-start(bf16[128,512]{1,0:T(8,128)(2,1)S(1)} %collective-permute-done.26), channel_id=1, source_target_pairs={{0,112},{16,0},{32,16},{48,32},{64,48},{80,64},{96,80},{112,96},{1... | collective-permute-start | bytes 393224 | tf_op jit(solution)/shard_map/ppermute | solution.py:28
  82.2 2.3 collective-permute-done.27
  84.9 2.3 collective-permute-start.30
  87.5 2.7 %collective-permute-start.12 = (bf16[144,1152]{1,0:T(8,128)(2,1)S(1)}, bf16[144,1152]{1,0:T(8,128)(2,1)S(1)}, u32[]{:S(2)}, u32[]{:S(2)}) collective-permute-start(bf16[144,1152]{1,0:T(8,128)(2,1)S(1)} %get-tuple-element.68), channel_id=1, source_target_pairs={{0,112},{16,0},{32,16},{48,32},{64,48},{80,64},{96,80},{112,96},{1... | collective-permute-start | bytes 995336 | tf_op jit(solution)/shard_map/ppermute | solution.py:28
  90.1 0.7 collective-permute-done.10
  91.1 1.0 collective-permute-start.31
  92.1 1.9 collective-permute-start.14
  93.9 11.0 %collective-permute-done.31 = bf16[128,512]{1,0:T(8,128)(2,1)S(1)} collective-permute-done((bf16[128,512]{1,0:T(8,128)(2,1)S(1)}, bf16[128,512]{1,0:T(8,128)(2,1)S(1)}, u32[]{:S(2)}, u32[]{:S(2)}) %collective-permute-start.31) | collective-permute-done | bytes 131104 | tf_op jit(solution)/shard_map/ppermute | solution.py:28
  105.0 1.4 collective-permute-start.32
  106.4 2.7 %collective-permute-start.16 = (bf16[144,1152]{1,0:T(8,128)(2,1)S(1)}, bf16[144,1152]{1,0:T(8,128)(2,1)S(1)}, u32[]{:S(2)}, u32[]{:S(2)}) collective-permute-start(bf16[144,1152]{1,0:T(8,128)(2,1)S(1)} %collective-permute-done.12), channel_id=1, source_target_pairs={{0,112},{16,0},{32,16},{48,32},{64,48},{80,64},{96,80},{112,96},{1... | collective-permute-start | bytes 995336 | tf_op jit(solution)/shard_map/ppermute | solution.py:28
  109.2 2.7 %collective-permute-start.18 = (bf16[144,1152]{1,0:T(8,128)(2,1)S(1)}, bf16[144,1152]{1,0:T(8,128)(2,1)S(1)}, u32[]{:S(2)}, u32[]{:S(2)}) collective-permute-start(bf16[144,1152]{1,0:T(8,128)(2,1)S(1)} %collective-permute-done.14), channel_id=1, source_target_pairs={{0,112},{16,0},{32,16},{48,32},{64,48},{80,64},{96,80},{112,96},{1... | collective-permute-start | bytes 995336 | tf_op jit(solution)/shard_map/ppermute | solution.py:28
  112.0 1.6 collective-permute-done.15
  113.6 2.7 %collective-permute-start.20 = (bf16[144,1152]{1,0:T(8,128)(2,1)S(1)}, bf16[144,1152]{1,0:T(8,128)(2,1)S(1)}, u32[]{:S(2)}, u32[]{:S(2)}) collective-permute-start(bf16[144,1152]{1,0:T(8,128)(2,1)S(1)} %collective-permute-done.16), channel_id=1, source_target_pairs={{0,112},{16,0},{32,16},{48,32},{64,48},{80,64},{96,80},{112,96},{1... | collective-permute-start | bytes 995336 | tf_op jit(solution)/shard_map/ppermute | solution.py:28
  116.2 1.7 collective-permute-done.17
  118.0 3.0 %collective-permute-start.22 = (bf16[144,1152]{1,0:T(8,128)(2,1)S(1)}, bf16[144,1152]{1,0:T(8,128)(2,1)S(1)}, u32[]{:S(2)}, u32[]{:S(2)}) collective-permute-start(bf16[144,1152]{1,0:T(8,128)(2,1)S(1)} %collective-permute-done.18), channel_id=1, source_target_pairs={{0,112},{16,0},{32,16},{48,32},{64,48},{80,64},{96,80},{112,96},{1... | collective-permute-start | bytes 995336 | tf_op jit(solution)/shard_map/ppermute | solution.py:28
  121.1 3.9 %collective-permute-done.19 = bf16[144,1152]{1,0:T(8,128)(2,1)S(1)} collective-permute-done((bf16[144,1152]{1,0:T(8,128)(2,1)S(1)}, bf16[144,1152]{1,0:T(8,128)(2,1)S(1)}, u32[]{:S(2)}, u32[]{:S(2)}) %collective-permute-start.19) | collective-permute-done | bytes 331808 | tf_op jit(solution)/shard_map/ppermute | solution.py:28
  125.0 6.1 %collective-permute-done.22 = bf16[144,1152]{1,0:T(8,128)(2,1)S(1)} collective-permute-done((bf16[144,1152]{1,0:T(8,128)(2,1)S(1)}, bf16[144,1152]{1,0:T(8,128)(2,1)S(1)}, u32[]{:S(2)}, u32[]{:S(2)}) %collective-permute-start.22) | collective-permute-done | bytes 331808 | tf_op jit(solution)/shard_map/ppermute | solution.py:28
  131.1 3.4 %collective-permute-start.24 = (bf16[144,1152]{1,0:T(8,128)(2,1)S(1)}, bf16[144,1152]{1,0:T(8,128)(2,1)S(1)}, u32[]{:S(2)}, u32[]{:S(2)}) collective-permute-start(bf16[144,1152]{1,0:T(8,128)(2,1)S(1)} %collective-permute-done.22), channel_id=1, source_target_pairs={{0,112},{16,0},{32,16},{48,32},{64,48},{80,64},{96,80},{112,96},{1... | collective-permute-start | bytes 995336 | tf_op jit(solution)/shard_map/ppermute | solution.py:28
  134.7 4.5 %collective-permute-done.23 = bf16[144,1152]{1,0:T(8,128)(2,1)S(1)} collective-permute-done((bf16[144,1152]{1,0:T(8,128)(2,1)S(1)}, bf16[144,1152]{1,0:T(8,128)(2,1)S(1)}, u32[]{:S(2)}, u32[]{:S(2)}) %collective-permute-start.23) | collective-permute-done | bytes 331808 | tf_op jit(solution)/shard_map/ppermute | solution.py:28
  139.3 2.0 collective-permute-done.24
  141.3 3.3 %convolution_convert_fusion = bf16[2,1152,256]{2,1,0:T(8,128)(2,1)} fusion(bf16[2,1152,1152]{2,1,0:T(8,128)(2,1)S(1)} %bitcast_dynamic-update-slice_fusion.blocks, bf16[2,256,1152]{2,1,0:T(8,128)(2,1)S(1)} %pad_maximum_fusion.2), kind=kOutput, calls=%fused_computation | convolution fusion | flops 1359544320 | bytes 7667712 | tf_op jit(solution)/shard_map/bkr,bck->brc/dot_general | solution.py:273
  144.7 4.8 %all-to-all-start = ((bf16[8,288,256]{2,1,0:T(8,128)(2,1)}), bf16[8,288,256]{2,1,0:T(8,128)(2,1)S(1)}, u32[]{:S(2)}, u32[]{:S(2)}) async-start(bf16[8,288,256]{2,1,0:T(8,128)(2,1)} %bitcast.138), calls=%async_computation | async-start | bytes 2359296 | tf_op jit(solution)/shard_map/all_to_all | solution.py:36
  149.5 0.5 pad_maximum_fusion
  150.3 22.0 %all-to-all-done.values = bf16[8,288,256]{2,1,0:T(8,128)(2,1)S(1)} async-done(((bf16[8,288,256]{2,1,0:T(8,128)(2,1)}), bf16[8,288,256]{2,1,0:T(8,128)(2,1)S(1)}, u32[]{:S(2)}, u32[]{:S(2)}) %all-to-all-start) | async-done | bytes 1179680 | tf_op jit(solution)/shard_map/all_to_all | solution.py:36
  172.3 1.3 copy-done.7
  173.6 4.4 %shard_map.88 = (f32[288,1024]{1,0:T(8,128)}, bf16[8,288,128]{2,1,0:T(8,128)(2,1)S(1)}) custom-call(bf16[8,288,256]{2,1,0:T(8,128)(2,1)S(1)} %all-to-all-done.values, bf16[1024,1024]{1,0:T(8,128)(2,1)S(1)} %bitcast.127, f32[288,1024]{1,0:T(8,128)S(1)} %bitcast.132), custom_call_target="tpu_custom_call" | custom-call | tf_op jit(solution)/shard_map/pallas_call | solution.py:195
  178.0 15.2 %all_to_all.21 = bf16[8,288,128]{2,1,0:T(8,128)(2,1)S(1)} all-to-all(bf16[8,288,128]{2,1,0:T(8,128)(2,1)S(1)} %get-tuple-element.40), channel_id=1, replica_groups={{0,16,32,48,64,80,96,112},{128,144,160,176,192,208,224,240},{1,17,33,49..., dimensions={0} | all-to-all | bytes 1179648 | tf_op jit(solution)/shard_map/all_to_all | solution.py:36
  193.2 2.5 %copy-done.2 = bf16[2,1152,1152]{2,1,0:T(8,128)(2,1)S(1)} copy-done((bf16[2,1152,1152]{2,1,0:T(8,128)(2,1)S(1)}, bf16[2,1152,1152]{2,1,0:T(8,128)(2,1)}, u32[]{:S(2)}) %copy-start.2) | copy-done | bytes 5308440
  195.7 0.9 shard_map.89
  196.6 1.6 shard_map.90
  198.2 19.2 %all-to-all-start.2 = ((f32[256,1,128]{2,1,0:T(1,128)}), f32[256,1,128]{2,1,0:T(1,128)S(1)}, u32[]{:S(2)}, u32[]{:S(2)}) async-start(f32[256,1,128]{2,1,0:T(1,128)} %bitcast.60), calls=%async_computation.2 | async-start | bytes 262144 | tf_op jit(solution)/shard_map/all_to_all | solution.py:286
  217.4 1.5 collective-permute-start.33
  219.0 1.2 multiply_add_fusion
  220.2 1.9 collective-permute-done.33.refs_2_
  222.1 3.9 %collective-permute-done.34.refs_3_ = bf16[64,1152]{1,0:T(8,128)(2,1)S(1)} collective-permute-done((bf16[64,1152]{1,0:T(8,128)(2,1)S(1)}, bf16[64,1152]{1,0:T(8,128)(2,1)S(1)}, u32[]{:S(2)}, u32[]{:S(2)}) %collective-permute-start.34) | collective-permute-done | bytes 147488 | tf_op jit(solution)/shard_map/ppermute | solution.py:32
  226.0 4.4 %all-to-all-done.2 = f32[256,1,128]{2,1,0:T(1,128)S(1)} async-done(((f32[256,1,128]{2,1,0:T(1,128)}), f32[256,1,128]{2,1,0:T(1,128)S(1)}, u32[]{:S(2)}, u32[]{:S(2)}) %all-to-all-start.2) | async-done | bytes 131104 | tf_op jit(solution)/shard_map/all_to_all | solution.py:286
  230.5 1.1 shard_map.91
  (96 shorter events, 4.0 us)
Async XLA Ops:
  0.6 0.7 copy-start.12
  5.3 33.7 %collective-permute-start = (bf16[144,1152]{1,0:T(8,128)(2,1)}, bf16[144,1152]{1,0:T(8,128)(2,1)}, u32[]{:S(2)}, u32[]{:S(2)}) collective-permute-start(bf16[144,1152]{1,0:T(8,128)(2,1)} %get-tuple-element.50), channel_id=1, source_target_pairs={{0,16},{16,32},{32,48},{48,64},{64,80},{80,96},{96,112},{112,0},{1... | collective-permute-start | bytes 995336 | tf_op jit(solution)/shard_map/ppermute | solution.py:28
  7.7 32.4 %collective-permute-start.1 = (bf16[144,1152]{1,0:T(8,128)(2,1)}, bf16[144,1152]{1,0:T(8,128)(2,1)}, u32[]{:S(2)}, u32[]{:S(2)}) collective-permute-start(bf16[144,1152]{1,0:T(8,128)(2,1)} %get-tuple-element.52), channel_id=1, source_target_pairs={{0,112},{16,0},{32,16},{48,32},{64,48},{80,64},{96,80},{112,96},{1... | collective-permute-start | bytes 995336 | tf_op jit(solution)/shard_map/ppermute | solution.py:28
  11.7 33.1 %collective-permute-start.2 = (bf16[144,1152]{1,0:T(8,128)(2,1)}, bf16[144,1152]{1,0:T(8,128)(2,1)}, u32[]{:S(2)}, u32[]{:S(2)}) collective-permute-start(bf16[144,1152]{1,0:T(8,128)(2,1)} %get-tuple-element.54), channel_id=1, source_target_pairs={{0,64},{16,80},{32,96},{48,112},{64,0},{80,16},{96,32},{112,48},{1... | collective-permute-start | bytes 995336 | tf_op jit(solution)/shard_map/ppermute | solution.py:28
  15.7 38.2 %collective-permute-start.3 = (bf16[144,1152]{1,0:T(8,128)(2,1)}, bf16[144,1152]{1,0:T(8,128)(2,1)}, u32[]{:S(2)}, u32[]{:S(2)}) collective-permute-start(bf16[144,1152]{1,0:T(8,128)(2,1)} %get-tuple-element.56), channel_id=1, source_target_pairs={{0,48},{16,64},{32,80},{48,96},{64,112},{80,0},{96,16},{112,32},{1... | collective-permute-start | bytes 995336 | tf_op jit(solution)/shard_map/ppermute | solution.py:28
  16.1 16.3 %copy-start.8 = (bf16[1,4608,64]{1,2,0:T(8,128)(2,1)S(1)}, bf16[1,4608,64]{1,2,0:T(8,128)(2,1)}, u32[]{:S(2)}) copy-start(bf16[1,4608,64]{1,2,0:T(8,128)(2,1)} %param.6) | copy-start | bytes 1769476
  16.1 43.1 %collective-permute-start.4 = (bf16[144,1152]{1,0:T(8,128)(2,1)}, bf16[144,1152]{1,0:T(8,128)(2,1)}, u32[]{:S(2)}, u32[]{:S(2)}) collective-permute-start(bf16[144,1152]{1,0:T(8,128)(2,1)} %get-tuple-element.58), channel_id=1, source_target_pairs={{0,80},{16,96},{32,112},{48,0},{64,16},{80,32},{96,48},{112,64},{1... | collective-permute-start | bytes 995336 | tf_op jit(solution)/shard_map/ppermute | solution.py:28
  20.2 2.4 %copy-start = (bf16[2,1152,1152]{2,1,0:T(8,128)(2,1)}, bf16[2,1152,1152]{2,1,0:T(8,128)(2,1)S(1)}, u32[]{:S(2)}) copy-start(bf16[2,1152,1152]{2,1,0:T(8,128)(2,1)S(1)} %shard_map.85) | copy-start | bytes 15925252
  29.5 1.0 copy-start.3
  37.8 2.3 %copy-start.11 = (bf16[144,1152]{1,0:T(8,128)(2,1)S(1)}, bf16[144,1152]{1,0:T(8,128)(2,1)}, u32[]{:S(2)}) copy-start(bf16[144,1152]{1,0:T(8,128)(2,1)} %get-tuple-element.62) | copy-start | bytes 995332
  39.0 24.9 %collective-permute-start.5 = (bf16[144,1152]{1,0:T(8,128)(2,1)}, bf16[144,1152]{1,0:T(8,128)(2,1)S(1)}, u32[]{:S(2)}, u32[]{:S(2)}) collective-permute-start(bf16[144,1152]{1,0:T(8,128)(2,1)} %get-tuple-element.60), channel_id=1, source_target_pairs={{0,32},{16,48},{32,64},{48,80},{64,96},{80,112},{96,0},{112,16},{1... | collective-permute-start | bytes 995336 | tf_op jit(solution)/shard_map/ppermute | solution.py:28
  40.2 30.0 %collective-permute-start.6 = (bf16[144,1152]{1,0:T(8,128)(2,1)S(1)}, bf16[144,1152]{1,0:T(8,128)(2,1)S(1)}, u32[]{:S(2)}, u32[]{:S(2)}) collective-permute-start(bf16[144,1152]{1,0:T(8,128)(2,1)S(1)} %copy-done.11), channel_id=1, source_target_pairs={{0,96},{16,112},{32,0},{48,16},{64,32},{80,48},{96,64},{112,80},{1... | collective-permute-start | bytes 995336 | tf_op jit(solution)/shard_map/ppermute | solution.py:28
  44.8 25.4 %collective-permute-start.7 = (bf16[2,64,2304]{2,1,0:T(8,128)(2,1)S(1)}, bf16[2,64,2304]{2,1,0:T(8,128)(2,1)S(1)}, u32[]{:S(2)}, u32[]{:S(2)}) collective-permute-start(bf16[2,64,2304]{2,1,0:T(8,128)(2,1)S(1)} %get-tuple-element.77), channel_id=1, source_target_pairs={{0,128},{16,144},{32,160},{48,176},{64,192},{80,208},{96,224},{112... | collective-permute-start | bytes 1769480 | tf_op jit(solution)/shard_map/ppermute | solution.py:32
  64.0 23.2 %slice-start = ((s8[5308416]{0:T(1024)(128)(4,1)}), s8[4194304]{0:T(1024)(128)(4,1)S(1)}, s32[]{:S(2)}) async-start(s8[5308416]{0:T(1024)(128)(4,1)} %bitcast.125), calls=%async_computation.3 | async-start | bytes 8388608
  70.3 4.0 %copy-start.4 = (bf16[1,1024,512]{2,1,0:T(8,128)(2,1)S(1)}, bf16[1,1024,512]{2,1,0:T(8,128)(2,1)}, u32[]{:S(2)}) copy-start(bf16[1,1024,512]{2,1,0:T(8,128)(2,1)} %copy-done.3) | copy-start | bytes 3145732
  70.4 3.9 %collective-permute-start.8 = (bf16[128,512]{1,0:T(8,128)(2,1)S(1)}, bf16[128,512]{1,0:T(8,128)(2,1)S(1)}, u32[]{:S(2)}, u32[]{:S(2)}) collective-permute-start(bf16[128,512]{1,0:T(8,128)(2,1)S(1)} %constant_dynamic-slice_fusion), channel_id=1, source_target_pairs={{0,128},{16,144},{32,160},{48,176},{64,192},{80,208},{96,224},{112... | collective-permute-start | bytes 393224 | tf_op jit(solution)/shard_map/ppermute | solution.py:32
  71.8 15.4 %slice-start.1 = ((s8[5308416]{0:T(1024)(128)(4,1)}), s8[1114112]{0:T(1024)(128)(4,1)S(1)}, s32[]{:S(2)}) async-start(s8[5308416]{0:T(1024)(128)(4,1)} %bitcast.125), calls=%async_computation.4 | async-start | bytes 2228224
  74.4 5.1 %collective-permute-start.25 = (bf16[128,512]{1,0:T(8,128)(2,1)S(1)}, bf16[128,512]{1,0:T(8,128)(2,1)S(1)}, u32[]{:S(2)}, u32[]{:S(2)}) collective-permute-start(bf16[128,512]{1,0:T(8,128)(2,1)S(1)} %get-tuple-element.64), channel_id=1, source_target_pairs={{0,16},{16,32},{32,48},{48,64},{64,80},{80,96},{96,112},{112,0},{1... | collective-permute-start | bytes 393224 | tf_op jit(solution)/shard_map/ppermute | solution.py:28
  74.8 4.9 %collective-permute-start.26 = (bf16[128,512]{1,0:T(8,128)(2,1)S(1)}, bf16[128,512]{1,0:T(8,128)(2,1)S(1)}, u32[]{:S(2)}, u32[]{:S(2)}) collective-permute-start(bf16[128,512]{1,0:T(8,128)(2,1)S(1)} %get-tuple-element.64), channel_id=1, source_target_pairs={{0,112},{16,0},{32,16},{48,32},{64,48},{80,64},{96,80},{112,96},{1... | collective-permute-start | bytes 393224 | tf_op jit(solution)/shard_map/ppermute | solution.py:28
  77.2 10.0 %collective-permute-start.9 = (bf16[144,1152]{1,0:T(8,128)(2,1)S(1)}, bf16[144,1152]{1,0:T(8,128)(2,1)S(1)}, u32[]{:S(2)}, u32[]{:S(2)}) collective-permute-start(bf16[144,1152]{1,0:T(8,128)(2,1)S(1)} %get-tuple-element.34), channel_id=1, source_target_pairs={{0,128},{16,144},{32,160},{48,176},{64,192},{80,208},{96,224},{112... | collective-permute-start | bytes 995336 | tf_op jit(solution)/shard_map/ppermute | solution.py:32
  78.6 12.2 %collective-permute-start.10 = (bf16[144,1152]{1,0:T(8,128)(2,1)S(1)}, bf16[144,1152]{1,0:T(8,128)(2,1)S(1)}, u32[]{:S(2)}, u32[]{:S(2)}) collective-permute-start(bf16[144,1152]{1,0:T(8,128)(2,1)S(1)} %get-tuple-element.35), channel_id=1, source_target_pairs={{0,128},{16,144},{32,160},{48,176},{64,192},{80,208},{96,224},{112... | collective-permute-start | bytes 995336 | tf_op jit(solution)/shard_map/ppermute | solution.py:32
  79.5 5.0 %collective-permute-start.27 = (bf16[128,512]{1,0:T(8,128)(2,1)S(1)}, bf16[128,512]{1,0:T(8,128)(2,1)S(1)}, u32[]{:S(2)}, u32[]{:S(2)}) collective-permute-start(bf16[128,512]{1,0:T(8,128)(2,1)S(1)} %collective-permute-done.25), channel_id=1, source_target_pairs={{0,16},{16,32},{32,48},{48,64},{64,80},{80,96},{96,112},{112,0},{1... | collective-permute-start | bytes 393224 | tf_op jit(solution)/shard_map/ppermute | solution.py:28
  79.7 5.2 %collective-permute-start.28 = (bf16[128,512]{1,0:T(8,128)(2,1)S(1)}, bf16[128,512]{1,0:T(8,128)(2,1)S(1)}, u32[]{:S(2)}, u32[]{:S(2)}) collective-permute-start(bf16[128,512]{1,0:T(8,128)(2,1)S(1)} %collective-permute-done.26), channel_id=1, source_target_pairs={{0,112},{16,0},{32,16},{48,32},{64,48},{80,64},{96,80},{112,96},{1... | collective-permute-start | bytes 393224 | tf_op jit(solution)/shard_map/ppermute | solution.py:28
  84.5 6.6 %collective-permute-start.29 = (bf16[128,512]{1,0:T(8,128)(2,1)S(1)}, bf16[128,512]{1,0:T(8,128)(2,1)S(1)}, u32[]{:S(2)}, u32[]{:S(2)}) collective-permute-start(bf16[128,512]{1,0:T(8,128)(2,1)S(1)} %collective-permute-done.27), channel_id=1, source_target_pairs={{0,16},{16,32},{32,48},{48,64},{64,80},{80,96},{96,112},{112,0},{1... | collective-permute-start | bytes 393224 | tf_op jit(solution)/shard_map/ppermute | solution.py:28
  84.9 7.2 %collective-permute-start.30 = (bf16[128,512]{1,0:T(8,128)(2,1)S(1)}, bf16[128,512]{1,0:T(8,128)(2,1)S(1)}, u32[]{:S(2)}, u32[]{:S(2)}) collective-permute-start(bf16[128,512]{1,0:T(8,128)(2,1)S(1)} %collective-permute-done.28), channel_id=1, source_target_pairs={{0,112},{16,0},{32,16},{48,32},{64,48},{80,64},{96,80},{112,96},{1... | collective-permute-start | bytes 393224 | tf_op jit(solution)/shard_map/ppermute | solution.py:28
  87.4 19.0 %collective-permute-start.11 = (bf16[144,1152]{1,0:T(8,128)(2,1)S(1)}, bf16[144,1152]{1,0:T(8,128)(2,1)S(1)}, u32[]{:S(2)}, u32[]{:S(2)}) collective-permute-start(bf16[144,1152]{1,0:T(8,128)(2,1)S(1)} %get-tuple-element.68), channel_id=1, source_target_pairs={{0,16},{16,32},{32,48},{48,64},{64,80},{80,96},{96,112},{112,0},{1... | collective-permute-start | bytes 995336 | tf_op jit(solution)/shard_map/ppermute | solution.py:28
  87.5 18.9 %collective-permute-start.12 = (bf16[144,1152]{1,0:T(8,128)(2,1)S(1)}, bf16[144,1152]{1,0:T(8,128)(2,1)S(1)}, u32[]{:S(2)}, u32[]{:S(2)}) collective-permute-start(bf16[144,1152]{1,0:T(8,128)(2,1)S(1)} %get-tuple-element.68), channel_id=1, source_target_pairs={{0,112},{16,0},{32,16},{48,32},{64,48},{80,64},{96,80},{112,96},{1... | collective-permute-start | bytes 995336 | tf_op jit(solution)/shard_map/ppermute | solution.py:28
  91.0 18.1 %collective-permute-start.13 = (bf16[144,1152]{1,0:T(8,128)(2,1)S(1)}, bf16[144,1152]{1,0:T(8,128)(2,1)S(1)}, u32[]{:S(2)}, u32[]{:S(2)}) collective-permute-start(bf16[144,1152]{1,0:T(8,128)(2,1)S(1)} %get-tuple-element.66), channel_id=1, source_target_pairs={{0,16},{16,32},{32,48},{48,64},{64,80},{80,96},{96,112},{112,0},{1... | collective-permute-start | bytes 995336 | tf_op jit(solution)/shard_map/ppermute | solution.py:28
  91.1 13.9 %collective-permute-start.31 = (bf16[128,512]{1,0:T(8,128)(2,1)S(1)}, bf16[128,512]{1,0:T(8,128)(2,1)S(1)}, u32[]{:S(2)}, u32[]{:S(2)}) collective-permute-start(bf16[128,512]{1,0:T(8,128)(2,1)S(1)} %collective-permute-done.29), channel_id=1, source_target_pairs={{0,16},{16,32},{32,48},{48,64},{64,80},{80,96},{96,112},{112,0},{1... | collective-permute-start | bytes 393224 | tf_op jit(solution)/shard_map/ppermute | solution.py:28
  92.1 17.1 %collective-permute-start.14 = (bf16[144,1152]{1,0:T(8,128)(2,1)S(1)}, bf16[144,1152]{1,0:T(8,128)(2,1)S(1)}, u32[]{:S(2)}, u32[]{:S(2)}) collective-permute-start(bf16[144,1152]{1,0:T(8,128)(2,1)S(1)} %get-tuple-element.66), channel_id=1, source_target_pairs={{0,112},{16,0},{32,16},{48,32},{64,48},{80,64},{96,80},{112,96},{1... | collective-permute-start | bytes 995336 | tf_op jit(solution)/shard_map/ppermute | solution.py:28
  105.0 16.1 %copy-start.5 = (bf16[1024,512]{1,0:T(8,128)(2,1)}, bf16[1024,512]{1,0:T(8,128)(2,1)S(1)}, u32[]{:S(2)}) copy-start(bf16[1024,512]{1,0:T(8,128)(2,1)S(1)} %constant_dynamic-update-slice_fusion) | copy-start | bytes 3145732
  105.0 29.7 %collective-permute-start.32 = (bf16[1024,512]{1,0:T(8,128)(2,1)S(1)}, bf16[1024,512]{1,0:T(8,128)(2,1)S(1)}, u32[]{:S(2)}, u32[]{:S(2)}) collective-permute-start(bf16[1024,512]{1,0:T(8,128)(2,1)S(1)} %constant_dynamic-update-slice_fusion), channel_id=1, source_target_pairs={{0,128},{16,144},{32,160},{48,176},{64,192},{80,208},{96,224},{112... | collective-permute-start | bytes 3145736 | tf_op jit(solution)/shard_map/ppermute | solution.py:32
  106.4 7.2 %collective-permute-start.15 = (bf16[144,1152]{1,0:T(8,128)(2,1)S(1)}, bf16[144,1152]{1,0:T(8,128)(2,1)S(1)}, u32[]{:S(2)}, u32[]{:S(2)}) collective-permute-start(bf16[144,1152]{1,0:T(8,128)(2,1)S(1)} %collective-permute-done.11), channel_id=1, source_target_pairs={{0,16},{16,32},{32,48},{48,64},{64,80},{80,96},{96,112},{112,0},{1... | collective-permute-start | bytes 995336 | tf_op jit(solution)/shard_map/ppermute | solution.py:28
  106.4 7.2 %collective-permute-start.16 = (bf16[144,1152]{1,0:T(8,128)(2,1)S(1)}, bf16[144,1152]{1,0:T(8,128)(2,1)S(1)}, u32[]{:S(2)}, u32[]{:S(2)}) collective-permute-start(bf16[144,1152]{1,0:T(8,128)(2,1)S(1)} %collective-permute-done.12), channel_id=1, source_target_pairs={{0,112},{16,0},{32,16},{48,32},{64,48},{80,64},{96,80},{112,96},{1... | collective-permute-start | bytes 995336 | tf_op jit(solution)/shard_map/ppermute | solution.py:28
  109.1 8.8 %collective-permute-start.17 = (bf16[144,1152]{1,0:T(8,128)(2,1)S(1)}, bf16[144,1152]{1,0:T(8,128)(2,1)S(1)}, u32[]{:S(2)}, u32[]{:S(2)}) collective-permute-start(bf16[144,1152]{1,0:T(8,128)(2,1)S(1)} %collective-permute-done.13), channel_id=1, source_target_pairs={{0,16},{16,32},{32,48},{48,64},{64,80},{80,96},{96,112},{112,0},{1... | collective-permute-start | bytes 995336 | tf_op jit(solution)/shard_map/ppermute | solution.py:28
  109.2 8.8 %collective-permute-start.18 = (bf16[144,1152]{1,0:T(8,128)(2,1)S(1)}, bf16[144,1152]{1,0:T(8,128)(2,1)S(1)}, u32[]{:S(2)}, u32[]{:S(2)}) collective-permute-start(bf16[144,1152]{1,0:T(8,128)(2,1)S(1)} %collective-permute-done.14), channel_id=1, source_target_pairs={{0,112},{16,0},{32,16},{48,32},{64,48},{80,64},{96,80},{112,96},{1... | collective-permute-start | bytes 995336 | tf_op jit(solution)/shard_map/ppermute | solution.py:28
  113.6 11.4 %collective-permute-start.19 = (bf16[144,1152]{1,0:T(8,128)(2,1)S(1)}, bf16[144,1152]{1,0:T(8,128)(2,1)S(1)}, u32[]{:S(2)}, u32[]{:S(2)}) collective-permute-start(bf16[144,1152]{1,0:T(8,128)(2,1)S(1)} %collective-permute-done.15), channel_id=1, source_target_pairs={{0,16},{16,32},{32,48},{48,64},{64,80},{80,96},{96,112},{112,0},{1... | collective-permute-start | bytes 995336 | tf_op jit(solution)/shard_map/ppermute | solution.py:28
  113.6 21.0 %collective-permute-start.20 = (bf16[144,1152]{1,0:T(8,128)(2,1)S(1)}, bf16[144,1152]{1,0:T(8,128)(2,1)S(1)}, u32[]{:S(2)}, u32[]{:S(2)}) collective-permute-start(bf16[144,1152]{1,0:T(8,128)(2,1)S(1)} %collective-permute-done.16), channel_id=1, source_target_pairs={{0,112},{16,0},{32,16},{48,32},{64,48},{80,64},{96,80},{112,96},{1... | collective-permute-start | bytes 995336 | tf_op jit(solution)/shard_map/ppermute | solution.py:28
  117.9 16.7 %collective-permute-start.21 = (bf16[144,1152]{1,0:T(8,128)(2,1)S(1)}, bf16[144,1152]{1,0:T(8,128)(2,1)S(1)}, u32[]{:S(2)}, u32[]{:S(2)}) collective-permute-start(bf16[144,1152]{1,0:T(8,128)(2,1)S(1)} %collective-permute-done.17), channel_id=1, source_target_pairs={{0,16},{16,32},{32,48},{48,64},{64,80},{80,96},{96,112},{112,0},{1... | collective-permute-start | bytes 995336 | tf_op jit(solution)/shard_map/ppermute | solution.py:28
  118.0 13.1 %collective-permute-start.22 = (bf16[144,1152]{1,0:T(8,128)(2,1)S(1)}, bf16[144,1152]{1,0:T(8,128)(2,1)S(1)}, u32[]{:S(2)}, u32[]{:S(2)}) collective-permute-start(bf16[144,1152]{1,0:T(8,128)(2,1)S(1)} %collective-permute-done.18), channel_id=1, source_target_pairs={{0,112},{16,0},{32,16},{48,32},{64,48},{80,64},{96,80},{112,96},{1... | collective-permute-start | bytes 995336 | tf_op jit(solution)/shard_map/ppermute | solution.py:28
  125.0 14.2 %collective-permute-start.23 = (bf16[144,1152]{1,0:T(8,128)(2,1)S(1)}, bf16[144,1152]{1,0:T(8,128)(2,1)S(1)}, u32[]{:S(2)}, u32[]{:S(2)}) collective-permute-start(bf16[144,1152]{1,0:T(8,128)(2,1)S(1)} %collective-permute-done.19), channel_id=1, source_target_pairs={{0,16},{16,32},{32,48},{48,64},{64,80},{80,96},{96,112},{112,0},{1... | collective-permute-start | bytes 995336 | tf_op jit(solution)/shard_map/ppermute | solution.py:28
  131.1 10.2 %collective-permute-start.24 = (bf16[144,1152]{1,0:T(8,128)(2,1)S(1)}, bf16[144,1152]{1,0:T(8,128)(2,1)S(1)}, u32[]{:S(2)}, u32[]{:S(2)}) collective-permute-start(bf16[144,1152]{1,0:T(8,128)(2,1)S(1)} %collective-permute-done.22), channel_id=1, source_target_pairs={{0,112},{16,0},{32,16},{48,32},{64,48},{80,64},{96,80},{112,96},{1... | collective-permute-start | bytes 995336 | tf_op jit(solution)/shard_map/ppermute | solution.py:28
  141.3 3.3 %copy-start.1 = (bf16[2,1152,1152]{2,1,0:T(8,128)(2,1)}, bf16[2,1152,1152]{2,1,0:T(8,128)(2,1)S(1)}, u32[]{:S(2)}) copy-start(bf16[2,1152,1152]{2,1,0:T(8,128)(2,1)S(1)} %bitcast_dynamic-update-slice_fusion.blocks) | copy-start | bytes 15925252
  144.7 4.8 %copy-start.6 = (bf16[1024,512]{1,0:T(8,128)(2,1)S(1)}, bf16[1024,512]{1,0:T(8,128)(2,1)}, u32[]{:S(2)}) copy-start(bf16[1024,512]{1,0:T(8,128)(2,1)} %copy-done.5) | copy-start | bytes 3145732
  144.7 27.6 %all-to-all-start = ((bf16[8,288,256]{2,1,0:T(8,128)(2,1)}), bf16[8,288,256]{2,1,0:T(8,128)(2,1)S(1)}, u32[]{:S(2)}, u32[]{:S(2)}) async-start(bf16[8,288,256]{2,1,0:T(8,128)(2,1)} %bitcast.138), calls=%async_computation | async-start | bytes 2359296 | tf_op jit(solution)/shard_map/all_to_all | solution.py:36
  172.3 1.3 copy-start.7
  193.2 2.5 %copy-start.2 = (bf16[2,1152,1152]{2,1,0:T(8,128)(2,1)S(1)}, bf16[2,1152,1152]{2,1,0:T(8,128)(2,1)}, u32[]{:S(2)}) copy-start(bf16[2,1152,1152]{2,1,0:T(8,128)(2,1)} %copy-done.1) | copy-start | bytes 15925252
  196.6 22.4 %copy-start.9 = (bf16[1,4608,64]{1,2,0:T(8,128)(2,1)S(1)}, bf16[1,4608,64]{1,2,0:T(8,128)(2,1)}, u32[]{:S(2)}) copy-start(bf16[1,4608,64]{1,2,0:T(8,128)(2,1)} %param.6) | copy-start | bytes 1769476
  196.6 22.4 %copy-start.10 = (f32[1,4608,64]{1,2,0:T(8,128)S(1)}, f32[1,4608,64]{1,2,0:T(8,128)}, u32[]{:S(2)}) copy-start(f32[1,4608,64]{1,2,0:T(8,128)} %param.7) | copy-start | bytes 3538948
  198.2 32.2 %all-to-all-start.2 = ((f32[256,1,128]{2,1,0:T(1,128)}), f32[256,1,128]{2,1,0:T(1,128)S(1)}, u32[]{:S(2)}, u32[]{:S(2)}) async-start(f32[256,1,128]{2,1,0:T(1,128)} %bitcast.60), calls=%async_computation.2 | async-start | bytes 262144 | tf_op jit(solution)/shard_map/all_to_all | solution.py:286
  217.4 4.7 %collective-permute-start.33 = (bf16[64,1152]{1,0:T(8,128)(2,1)S(1)}, bf16[64,1152]{1,0:T(8,128)(2,1)S(1)}, u32[]{:S(2)}, u32[]{:S(2)}) collective-permute-start(bf16[64,1152]{1,0:T(8,128)(2,1)S(1)} %get-tuple-element.45), channel_id=1, source_target_pairs={{0,128},{16,144},{32,160},{48,176},{64,192},{80,208},{96,224},{112... | collective-permute-start | bytes 442376 | tf_op jit(solution)/shard_map/ppermute | solution.py:32
  218.9 7.1 %collective-permute-start.34 = (bf16[64,1152]{1,0:T(8,128)(2,1)S(1)}, bf16[64,1152]{1,0:T(8,128)(2,1)S(1)}, u32[]{:S(2)}, u32[]{:S(2)}) collective-permute-start(bf16[64,1152]{1,0:T(8,128)(2,1)S(1)} %get-tuple-element.46), channel_id=1, source_target_pairs={{0,128},{16,144},{32,160},{48,176},{64,192},{80,208},{96,224},{112... | collective-permute-start | bytes 442376 | tf_op jit(solution)/shard_map/ppermute | solution.py:32
